TPU v7x, 512 devices: a whole 4x8x8 slice. The times are simulated.
512 devices in a mesh: sec: 2 (over core), ep: 64 (over z, y), tp: 4 (over x).
Axes of the slice: x: 4, y: 8, z: 8, core: 2. Of those that a mesh axis runs over, the one named last changes fastest.
Arguments:
- resid: bfloat16 [16384, 4096], P(('sec', 'ep'), 'tp'), may hold values from -6 to 6
- queries: bfloat16 [16384, 4096], P(('sec', 'ep'), 'tp'), may hold values from -48 to 48
- keys: bfloat16 [16384, 4096], P(('sec', 'ep'), 'tp'), may hold values from -6 to 6
- values: bfloat16 [16384, 4096], P(('sec', 'ep'), 'tp'), may hold values from -6 to 6
- norm_gain: float32 [4096], P('tp'), may hold values from 0.25 to 1.75
- w_router: float32 [4096, 64], P('tp'), may hold values from -0.09375 to 0.09375
- expert_ids: int32 [16384, 2], P(('sec', 'ep')), may hold values from 0 to 63, all different within a row; in each aligned block of 128 rows (0 to 127, 128 to 255, ...) at most 8 rows name the same one
- w_gate: bfloat16 [64, 4096, 1024], P('ep', 'sec', 'tp'), may hold values from -0.09375 to 0.09375
- w_up: bfloat16 [64, 4096, 1024], P('ep', 'sec', 'tp'), may hold values from -0.09375 to 0.09375
- w_down: bfloat16 [64, 1024, 4096], P('ep', 'tp', 'sec'), may hold values from -0.1875 to 0.1875
Outputs:
- mixed: bfloat16 [16384, 4096], P(('sec', 'ep'), 'tp')
Inputs may be any that keep to these rules, and one draw needn't show every extreme that they name: `expert_ids`: the two ids of a token differ. Among the 128 tokens of one device (aligned blocks of 128 rows) no expert is picked more than 8 times.
All inputs are finite; a program needn't handle non-finite values.
Results may differ from a plain program's by a relative error of at most 0.015.
Values may be sent and summed in bfloat16 or wider, within the bound.
No kernel may reach another device: no remote copies, remote signals or barrier semaphores. Data moves between devices by JAX's collectives and lax.ppermute only.
A program may use at most 64 MiB of HBM per device.

v0:
```python
import math

import jax
import jax.numpy as jnp
from jax import lax
from jax.sharding import PartitionSpec as P

D = 4096
HEAD_DIM = 128
WINDOW = 128


epsilon = 1e-06


def body(resid, queries, keys, values, norm_gain, w_router, expert_ids, w_gate, w_up, w_down):
    tok_rows, local_width = resid.shape
    head_count = local_width // HEAD_DIM
    windows = tok_rows // WINDOW
    query_blocks = queries.reshape(windows, WINDOW, head_count, HEAD_DIM)
    key_blocks = keys.reshape(windows, WINDOW, head_count, HEAD_DIM)
    value_blocks = values.reshape(windows, WINDOW, head_count, HEAD_DIM)
    scores = jnp.einsum(
        "wqhd,wkhd->whqk", query_blocks, key_blocks, preferred_element_type=jnp.float32
    ) / math.sqrt(HEAD_DIM)
    attn_weights = jax.nn.softmax(scores, axis=-1).astype(jnp.bfloat16)
    attended = jnp.einsum(
        "whqk,wkhd->wqhd", attn_weights, value_blocks, preferred_element_type=jnp.float32
    ).reshape(tok_rows, local_width)
    hidden_state = (resid.astype(jnp.float32) + attended).astype(jnp.bfloat16)
    hidden_f32 = hidden_state.astype(jnp.float32)
    square = lax.psum(jnp.sum(hidden_f32 * hidden_f32, axis=1, keepdims=True), "tp")
    inv_rms = lax.rsqrt(square / D + epsilon)
    local_logits = jnp.dot(
        hidden_f32 * inv_rms * norm_gain, w_router, precision=lax.Precision.HIGHEST
    )
    logits = lax.psum(local_logits.astype(jnp.bfloat16), "tp").astype(jnp.float32)
    normed = (hidden_f32 * inv_rms * norm_gain).astype(jnp.bfloat16)
    experts = lax.axis_size("ep")
    expert_range = jnp.arange(experts, dtype=jnp.int32)
    affinity = jax.nn.sigmoid(logits)
    picked = jnp.sum(
        jnp.where(expert_ids[:, :, None] == expert_range[None, None, :], affinity[:, None, :], 0.0),
        axis=2,
    )
    gate_share = picked / jnp.sum(picked, axis=1, keepdims=True)
    capacity = 4 * tok_rows // experts
    flat_ids = expert_ids.reshape(-1)
    onehot = (flat_ids[:, None] == expert_range[None, :]).astype(jnp.int32)
    rank_in_block = jnp.sum((jnp.cumsum(onehot, axis=0) - 1) * onehot, axis=1)
    slot_index = flat_ids * capacity + rank_in_block
    full_rows = lax.all_gather(normed, "tp", axis=1, tiled=True)
    outgoing = (
        jnp.zeros((experts * capacity, D), jnp.bfloat16)
        .at[slot_index]
        .set(jnp.repeat(full_rows, 2, axis=0))
    )
    arrived = lax.all_to_all(
        outgoing.reshape(experts, capacity, D), "ep", split_axis=0, concat_axis=0, tiled=True
    )
    routed_rows = arrived.reshape(experts * capacity, D)
    gate_proj = jnp.dot(
        routed_rows,
        lax.all_gather(w_gate, "sec", axis=1, tiled=True)[0],
        preferred_element_type=jnp.float32,
    )
    up_proj = jnp.dot(
        routed_rows,
        lax.all_gather(w_up, "sec", axis=1, tiled=True)[0],
        preferred_element_type=jnp.float32,
    )
    inner_act = (jax.nn.silu(gate_proj) * up_proj).astype(jnp.bfloat16)
    partial_out = jnp.dot(
        inner_act,
        lax.all_gather(w_down, "sec", axis=2, tiled=True)[0],
        preferred_element_type=jnp.float32,
    )
    own_share = lax.psum_scatter(
        partial_out.astype(jnp.bfloat16), "tp", scatter_dimension=1, tiled=True
    )
    returned = lax.all_to_all(
        own_share.reshape(experts, capacity, local_width),
        "ep",
        split_axis=0,
        concat_axis=0,
        tiled=True,
    )
    picked_rows = (
        returned.reshape(experts * capacity, local_width)[slot_index]
        .reshape(tok_rows, 2, local_width)
        .astype(jnp.float32)
    )
    mixed = hidden_f32 + jnp.sum(gate_share[:, :, None] * picked_rows, axis=1)
    return mixed.astype(jnp.bfloat16)


def solution(mesh):
    return jax.shard_map(
        body,
        mesh=mesh,
        in_specs=(
            P(("sec", "ep"), "tp"),
            P(("sec", "ep"), "tp"),
            P(("sec", "ep"), "tp"),
            P(("sec", "ep"), "tp"),
            P("tp"),
            P("tp", None),
            P(("sec", "ep"), None),
            P("ep", "sec", "tp"),
            P("ep", "sec", "tp"),
            P("ep", "tp", "sec"),
        ),
        out_specs=P(("sec", "ep"), "tp"),
        check_vma=False,
    )
```

profile of v0, /device:TPU:1, one launch (start us, length us, event | category | flops | bytes accessed | tf_op | source)
XLA Modules:
  0.0 332.8 jit_solution(18064860996848311413)
XLA Ops:
  7.4 0.0 copy-start
  7.4 0.0 copy-start.2
  7.4 0.0 all-gather.5.cloned.1.call-start
  7.4 0.9 copy-done
  8.3 1.2 convolution_multiply_fusion
  9.6 1.3 fusion.55
  10.9 0.0 copy-done.2
  10.9 0.0 copy-start.3
  10.9 0.2 copy.40
  11.1 0.0 copy-start.4
  11.1 0.0 copy-start.5
  11.1 0.3 fusion.36
  11.4 0.2 copy.33
  11.6 0.2 copy-done.3
  11.9 0.2 fusion.26
  12.0 9.3 %psum.14 = f32[128,1]{0,1:T(1,128)S(1)} all-reduce(f32[128,1]{0,1:T(1,128)S(1)} %bitcast.98), channel_id=1, replica_groups=mesh['sec'=2,'ep'=64,'tp'=4] {'tp'}, use_global_device_ids=true, to_apply=%region_3.0 | all-reduce | flops 128 | bytes 1024 | tf_op jit(solution)/shard_map/psum | solution.py:32
  21.3 0.0 copy-done.4
  21.3 0.8 fusion.28
  22.2 0.0 all-gather.5.cloned.1.call-update
  22.2 0.0 copy-done.5
  22.2 0.1 copy.36
  22.3 0.1 eq.45
  22.4 0.1 eq.41
  22.6 0.6 reduce-window.6
  23.2 0.2 slice_reduce_fusion
  23.4 0.1 copy.35
  23.6 0.1 mul.72
  23.7 0.1 fusion.46
  23.8 31.4 %all-gather.5.cloned.1.call-done = bf16[128,4096]{1,0:T(8,128)(2,1)} async-done(((bf16[128,1024]{1,0:T(8,128)(2,1)}), bf16[128,4096]{1,0:T(8,128)(2,1)}) %all-gather.5.cloned.1.call-update) | async-done | bytes 1048592 | tf_op jit(solution)/shard_map/all_gather | solution.py:52
  55.2 3.3 broadcast_in_dim.22
  58.5 2.2 reshape.147
  60.8 7.1 %scatter_custom_fusion = bf16[512,4096]{1,0:T(8,128)(2,1)} fusion(s32[256]{0:T(256)S(1)} %bitcast.96, bf16[256,4096]{1,0:T(8,128)(2,1)} %reshape.147, bf16[]{:T(256)} %constant.9.clone.1), kind=kCustom, calls=%fused_computation.11 | custom fusion | bytes 4194816 | tf_op jit(solution)/shard_map/scatter | solution.py:56
  67.9 13.3 %all-to-all-start = ((bf16[64,8,4096]{2,1,0:T(8,128)(2,1)}), bf16[64,8,4096]{2,1,0:T(8,128)(2,1)}, u32[]{:S(2)}, u32[]{:S(2)}) async-start(bf16[64,8,4096]{2,1,0:T(8,128)(2,1)} %bitcast.91), calls=%async_computation | async-start | bytes 8388608 | tf_op jit(solution)/shard_map/all_to_all | solution.py:58
  81.1 0.0 all-gather.7.cloned.1.call-start
  81.2 0.5 all-gather.7.cloned.1.call-update
  81.7 0.0 all-gather.11.cloned.1.call-start
  81.8 0.5 all-gather.11.cloned.1.call-update
  82.3 0.0 all-gather.9.cloned.1.call-start
  82.4 0.5 all-gather.9.cloned.1.call-update
  82.9 0.2 reduce-scatter.2.cloned.1.call-start
  83.1 21.6 %all-gather.7.cloned.1.call-done = bf16[1,4096,256]{2,1,0:T(8,128)(2,1)} async-done(((bf16[1,2048,256]{2,1,0:T(8,128)(2,1)}), bf16[1,4096,256]{2,1,0:T(8,128)(2,1)}) %all-gather.7.cloned.1.call-update) | async-done | bytes 2097168 | tf_op jit(solution)/shard_map/all_gather | solution.py:64
  104.7 86.1 %all-to-all-done = bf16[64,8,4096]{2,1,0:T(8,128)(2,1)} async-done(((bf16[64,8,4096]{2,1,0:T(8,128)(2,1)}), bf16[64,8,4096]{2,1,0:T(8,128)(2,1)}, u32[]{:S(2)}, u32[]{:S(2)}) %all-to-all-start) | async-done | bytes 4194336 | tf_op jit(solution)/shard_map/all_to_all | solution.py:58
  190.8 4.1 %fusion.3 = f32[512,256]{1,0:T(8,128)S(1)} fusion(bf16[64,8,4096]{2,1,0:T(8,128)(2,1)} %all-to-all-done, bf16[1,4096,256]{2,1,0:T(8,128)(2,1)} %all-gather.7.cloned.1.call-done), kind=kOutput, calls=%fused_computation.6 | convolution fusion | flops 1073741824 | bytes 6815744 | tf_op jit(solution)/shard_map/dot_general | solution.py:62
  194.9 0.0 all-gather.11.cloned.1.call-done
  195.0 0.0 all-gather.9.cloned.1.call-done
  195.0 9.9 %convolution_convert_fusion = bf16[512,4096]{1,0:T(8,128)(2,1)} fusion(bf16[1,256,4096]{2,1,0:T(8,128)(2,1)} %all-gather.11.cloned.1.call-done, bf16[1,4096,256]{2,1,0:T(8,128)(2,1)} %all-gather.9.cloned.1.call-done, bf16[64,8,4096]{2,1,0:T(8,128)(2,1)} %all-to-all-done, f32[512,256]{1,0:T(8,128)S(1)} %fusion.3), kind=kOutput, calls=%fused_computation.3 | convolution fusion | flops 2150367232 | bytes 13107200 | tf_op jit(solution)/shard_map/dot_general | solution.py:73
  204.9 0.0 reduce-scatter.2.cloned.1.call-update
  204.9 0.0 copy-start.1
  204.9 75.9 %reduce-scatter.2.cloned.1.call-done = bf16[512,1024]{1,0:T(8,128)(2,1)} async-done(((bf16[512,4096]{1,0:T(8,128)(2,1)}), bf16[512,1024]{1,0:T(8,128)(2,1)}) %reduce-scatter.2.cloned.1.call-update) | async-done | bytes 1048592 | tf_op jit(solution)/shard_map/reduce_scatter | solution.py:78
  280.8 13.0 %all-to-all-start.1 = ((bf16[64,8,1024]{2,1,0:T(8,128)(2,1)}), bf16[64,8,1024]{2,1,0:T(8,128)(2,1)S(1)}, u32[]{:S(2)}, u32[]{:S(2)}) async-start(bf16[64,8,1024]{2,1,0:T(8,128)(2,1)} %bitcast.92), calls=%async_computation.2 | async-start | bytes 2097152 | tf_op jit(solution)/shard_map/all_to_all | solution.py:81
  293.8 0.0 copy-done.1
  293.9 0.8 convolution_convert_fusion.1
  294.6 12.3 %psum.15 = bf16[128,64]{0,1:T(8,128)(2,1)S(1)} all-reduce(bf16[128,64]{0,1:T(8,128)(2,1)S(1)} %convolution_convert_fusion.1), channel_id=1, replica_groups=mesh['sec'=2,'ep'=64,'tp'=4] {'tp'}, use_global_device_ids=true, to_apply=%region_4.0 | all-reduce | flops 8192 | bytes 32768 | tf_op jit(solution)/shard_map/psum | solution.py:37
  307.0 0.1 copy.34
  307.1 14.2 %all-to-all-done.1 = bf16[64,8,1024]{2,1,0:T(8,128)(2,1)S(1)} async-done(((bf16[64,8,1024]{2,1,0:T(8,128)(2,1)}), bf16[64,8,1024]{2,1,0:T(8,128)(2,1)S(1)}, u32[]{:S(2)}, u32[]{:S(2)}) %all-to-all-start.1) | async-done | bytes 1048608 | tf_op jit(solution)/shard_map/all_to_all | solution.py:81
  321.3 1.2 gather_fusion
  322.5 0.7 reshape.134
  323.1 1.3 multiply_reduce_fusion
  324.5 0.8 fusion.30
  (10 shorter events, 0.1 us)
Async XLA Ops:
  7.4 1.0 copy-start
  7.4 3.5 %copy-start.2 = (bf16[128,1024]{1,0:T(8,128)(2,1)S(1)}, bf16[128,1024]{1,0:T(8,128)(2,1)}, u32[]{:S(2)}) copy-start(bf16[128,1024]{1,0:T(8,128)(2,1)} %param.13) | copy-start | bytes 786436
  7.4 47.9 %all-gather.5.cloned.1.call-start = ((), (), s32[]{:S(2)}) async-start(), calls=%async_computation.3 | async-start | bytes 1310720 | tf_op jit(solution)/shard_map/all_gather | solution.py:52
  10.9 1.0 copy-start.3
  11.1 10.2 %copy-start.4 = (f32[1024]{0:T(1024)S(1)}, f32[1024]{0:T(1024)}, u32[]{:S(2)}) copy-start(f32[1024]{0:T(1024)} %param.14) | copy-start | bytes 12292
  11.1 11.1 %copy-start.5 = (s32[128,2]{0,1:T(2,128)S(1)}, s32[128,2]{0,1:T(2,128)}, u32[]{:S(2)}) copy-start(s32[128,2]{0,1:T(2,128)} %param.16) | copy-start | bytes 3076
  67.9 122.9 %all-to-all-start = ((bf16[64,8,4096]{2,1,0:T(8,128)(2,1)}), bf16[64,8,4096]{2,1,0:T(8,128)(2,1)}, u32[]{:S(2)}, u32[]{:S(2)}) async-start(bf16[64,8,4096]{2,1,0:T(8,128)(2,1)} %bitcast.91), calls=%async_computation | async-start | bytes 8388608 | tf_op jit(solution)/shard_map/all_to_all | solution.py:58
  81.1 23.5 %all-gather.7.cloned.1.call-start = ((), (), s32[]{:S(2)}) async-start(), calls=%async_computation.4 | async-start | bytes 3145728 | tf_op jit(solution)/shard_map/all_gather | solution.py:64
  81.7 113.2 %all-gather.11.cloned.1.call-start = ((), (), s32[]{:S(2)}) async-start(), calls=%async_computation.6 | async-start | bytes 3145728 | tf_op jit(solution)/shard_map/all_gather | solution.py:75
  82.3 112.7 %all-gather.9.cloned.1.call-start = ((), (), s32[]{:S(2)}) async-start(), calls=%async_computation.5 | async-start | bytes 3145728 | tf_op jit(solution)/shard_map/all_gather | solution.py:69
  82.9 197.9 %reduce-scatter.2.cloned.1.call-start = ((), (), s32[]{:S(2)}) async-start(), calls=%async_computation.7 | async-start | bytes 5242880 | tf_op jit(solution)/shard_map/reduce_scatter | solution.py:78
  204.9 88.9 %copy-start.1 = (f32[1024,64]{0,1:T(8,128)S(1)}, f32[1024,64]{0,1:T(8,128)}, u32[]{:S(2)}) copy-start(f32[1024,64]{0,1:T(8,128)} %param.15) | copy-start | bytes 786436
  280.8 40.4 %all-to-all-start.1 = ((bf16[64,8,1024]{2,1,0:T(8,128)(2,1)}), bf16[64,8,1024]{2,1,0:T(8,128)(2,1)S(1)}, u32[]{:S(2)}, u32[]{:S(2)}) async-start(bf16[64,8,1024]{2,1,0:T(8,128)(2,1)} %bitcast.92), calls=%async_computation.2 | async-start | bytes 2097152 | tf_op jit(solution)/shard_map/all_to_all | solution.py:81
Sparse Core Ops, SparseCore 0:
  22.3 32.8 all-gather.4
  205.0 75.7 reduce-scatter.1
Sparse Core Ops, SparseCore 1:
  83.7 20.9 all-gather.6
  106.7 19.9 all-gather.10
  128.6 19.9 all-gather.8
where the time goes:
time: 335 us; the launch traced here: 333 us
  waiting for transfers between devices  231 us (69%)
  starting transfers between devices  26.6 us (8%)
  blocking collectives  21.6 us (6%)
  matrix products  17.6 us (5%)
  local copies, waits for them, and re-layouts  17 us (5%)
  between operations  15.2 us (5%)
  other arithmetic  3.97 us (1%)
    all_to_all x1, waiting for transfers between devices, body(): lax.all_to_all(outgoing.reshape(experts, capacity, D), 'ep', split_axis=0...  86.1 us
    reduce_scatter x1, waiting for transfers between devices, body(): lax.psum_scatter(partial_out.astype(jnp.bfloat16), 'tp', scatter_dimensio...  75.9 us
    all_gather x1, waiting for transfers between devices, body(): full_rows = lax.all_gather(normed, 'tp', axis=1, tiled=True)  31.4 us
    all_gather x1, waiting for transfers between devices, body(): lax.all_gather(w_gate, 'sec', axis=1, tiled=True)[0]  21.6 us
    all_to_all x1, waiting for transfers between devices, body(): lax.all_to_all(own_share.reshape(experts, capacity, local_width), 'ep', s...  14.2 us
    all_to_all x1, starting transfers between devices, body(): lax.all_to_all(outgoing.reshape(experts, capacity, D), 'ep', split_axis=0...  13.3 us
    all_to_all x1, starting transfers between devices, body(): lax.all_to_all(own_share.reshape(experts, capacity, local_width), 'ep', s...  13 us
    psum x1, blocking collectives, body(): lax.psum(local_logits.astype(jnp.bfloat16), 'tp').astype(jnp.float32)  12.3 us
  transfers between devices with their start and end apart: 7, of which 5 were waited for; matrix products, arithmetic and copies ran while one was open for 2% of the time, Pallas kernels for 0%

commit v1 on v0

v1 whole, which is shorter than its diff:
```python
import math

import jax
import jax.numpy as jnp
from jax import lax
from jax.experimental import pallas as pl
from jax.experimental.pallas import tpu as pltpu
from jax.sharding import PartitionSpec as P

D = 4096
HEAD_DIM = 128
CAP = 8
N_TP = 4
EPS = 1e-06

BF = jnp.bfloat16
F32 = jnp.float32
HIGHEST = lax.Precision.HIGHEST
VMEM_BYTES = 48 * 1024 * 1024


def call(kernel, out_shape, in_specs, scratch=(), cost=None, single=True):
    out_specs = jax.tree.map(lambda s: pl.BlockSpec(memory_space=pltpu.VMEM), out_shape)
    if not single:
        out_specs = jax.tree.map(lambda s: pl.BlockSpec(memory_space=pl.ANY), out_shape)
    return pl.pallas_call(
        kernel,
        out_shape=out_shape,
        in_specs=in_specs,
        out_specs=out_specs,
        scratch_shapes=scratch,
        cost_estimate=cost,
        compiler_params=pltpu.CompilerParams(vmem_limit_bytes=VMEM_BYTES),
    )


VM = pl.BlockSpec(memory_space=pltpu.VMEM)
ANY = pl.BlockSpec(memory_space=pl.ANY)
SM = pl.BlockSpec(memory_space=pltpu.SMEM)


def struct(shape, dtype):
    return jax.ShapeDtypeStruct(shape, dtype)


def nt(a, b, precision=None):
    return lax.dot_general(
        a, b, (((1,), (1,)), ((), ())), precision=precision, preferred_element_type=F32
    )


def pack_kernel(parity, gate, up, down, first, second, sems):
    width = gate.shape[2]
    span = down.shape[2] // 2
    copies = []
    for turn, out in enumerate((first, second)):
        block = parity[0] if turn == 0 else 1 - parity[0]
        base = block * span
        for j in range(span // width):
            rows = pl.ds(pl.multiple_of(base + j * width, width), width)
            cols = pl.ds(j * width, width)
            copies.append((gate.at[0, rows, :], out.at[pl.ds(0, width), cols]))
            copies.append((up.at[0, rows, :], out.at[pl.ds(width, width), cols]))
        cols = pl.ds(pl.multiple_of(base, span), span)
        copies.append((down.at[0, :, cols], out.at[pl.ds(2 * width, width), :]))
    started = [
        pltpu.make_async_copy(src, dst, sems.at[n]) for n, (src, dst) in enumerate(copies)
    ]
    for copy in started:
        copy.start()
    for copy in started:
        copy.wait()


def slots_of(ids_ref, experts):
    tokens = ids_ref.shape[1]
    expert = lax.broadcasted_iota(jnp.int32, (experts, tokens), 0)
    named = (ids_ref[0:1, :] == expert) | (ids_ref[1:2, :] == expert)
    before = lax.broadcasted_iota(jnp.int32, (tokens, tokens), 0) < lax.broadcasted_iota(
        jnp.int32, (tokens, tokens), 1
    )
    rank = jnp.dot(named.astype(BF), before.astype(BF), preferred_element_type=F32)
    return named, jnp.where(named, rank, -1.0)


def spread(slot, value):
    experts, tokens = slot.shape
    turn = lax.broadcasted_iota(jnp.int32, (experts, CAP, tokens), 1).astype(F32)
    hit = slot[:, None, :] == turn
    return jnp.where(hit, value[:, None, :], 0.0).reshape(experts * CAP, tokens)


def attention_kernel(experts, ids, q, k, v, resid, hidden, outgoing):
    tokens, width = q.shape
    scale = 1.0 / math.sqrt(HEAD_DIM)
    _, slot = slots_of(ids, experts)
    pick = spread(slot, jnp.ones_like(slot)).astype(BF)
    for n in range(width // HEAD_DIM):
        cols = slice(n * HEAD_DIM, (n + 1) * HEAD_DIM)
        scores = nt(q[:, cols], k[:, cols]) * scale
        top = jnp.max(scores, axis=1, keepdims=True)
        e = jnp.exp(scores - top)
        weights = (e / jnp.sum(e, axis=1, keepdims=True)).astype(BF)
        attended = jnp.dot(weights, v[:, cols], preferred_element_type=F32)
        h = (resid[:, cols].astype(F32) + attended).astype(BF)
        hidden[:, cols] = h
        outgoing[:, cols] = jnp.dot(pick, h, preferred_element_type=F32).astype(BF)


def router_kernel(hidden, gain, router, out):
    h = hidden[...].astype(F32)
    experts = router.shape[0]
    out[0:experts, :] = nt(router[...], h * gain[...], HIGHEST)
    out[experts : experts + 8, :] = nt(jnp.ones((8, h.shape[1]), F32), h * h, HIGHEST)


def pick_block(flag, mine, other, n):
    return (mine[n % 2], other[n % 2]) if n < 2 else (other[n % 2], mine[n % 2])


def up_kernel(flag, x, gain, u0, u1, v0, v1, own, own_square, s1, s2, s3, weights, sems):
    rows, depth = x.shape
    width = u0.shape[0] // 3
    order = (2, 1, 3, 0)

    def copy(n, ref):
        return pltpu.make_async_copy(ref.at[pl.ds(0, 2 * width), :], weights.at[n], sems.at[n])

    for n in order:
        yes, no = pick_block(flag, (u0, u1), (v0, v1), n)

        @pl.when(flag[0] == 1)
        def _():
            copy(n, yes).start()

        @pl.when(flag[0] != 1)
        def _():
            copy(n, no).start()

    xf = x[...].astype(F32)
    xg = (xf * gain[...]).astype(BF)
    square = xf * xf
    high = square.astype(BF)
    low = (square - high.astype(F32)).astype(BF)
    ones = jnp.ones((8, depth), BF)
    total = nt(ones, high) + nt(ones, low)
    own_square[...] = total
    t_high = total.astype(BF)
    t_low = (total - t_high.astype(F32)).astype(BF)
    sums = jnp.concatenate([t_high, t_low], axis=0)
    for n in order:
        copy(n, u0).wait()
        gate = jnp.zeros((rows, width), F32)
        up = jnp.zeros((rows, width), F32)
        for j in range(depth // width):
            cols = slice(j * width, (j + 1) * width)
            part = xg[:, cols]
            gate += jnp.dot(part, weights[n, 0:width, cols], preferred_element_type=F32)
            up += jnp.dot(part, weights[n, width : 2 * width, cols], preferred_element_type=F32)
        if n == 0:
            own[:, 0:width] = gate
            own[:, width : 2 * width] = up
        else:
            out = (s1, s2, s3)[n - 1]
            out[0:rows, 0:width] = gate.astype(BF)
            out[0:rows, width : 2 * width] = up.astype(BF)
            out[rows : rows + 16, :] = sums


def inner_kernel(own, own_square, r1, r2, r3, inner):
    rows, width2 = own.shape
    width = width2 // 2
    square = own_square[...]
    total = own[...]
    for r in (r1, r2, r3):
        sums = r[rows : rows + 16, :].astype(F32)
        square = square + sums[0:8, :] + sums[8:16, :]
        total = total + r[0:rows, :].astype(F32)
    inv = lax.rsqrt(square[0:1, :] / D + EPS)
    for j in range(rows // 128):
        part = slice(j * 128, (j + 1) * 128)
        column = jnp.transpose(jnp.broadcast_to(inv[:, part], (128, 128)), (1, 0))
        column = jnp.concatenate([column] * (width // 128), axis=1)
        gate = total[part, 0:width] * column
        up = total[part, width : 2 * width] * column
        inner[part, :] = (gate * (1.0 / (1.0 + jnp.exp(-gate))) * up).astype(BF)


def down_kernel(flag, i0, i1, i2, i3, u0, u1, v0, v1, out, weights, sems):
    width = u0.shape[0] // 3
    order = (0, 1, 2, 3)

    def copy(n, ref):
        return pltpu.make_async_copy(
            ref.at[pl.ds(2 * width, width), :], weights.at[pl.ds(n * width, width), :], sems.at[n]
        )

    for n in order:
        yes, no = pick_block(flag, (u0, u1), (v0, v1), n)

        @pl.when(flag[0] == 1)
        def _():
            copy(n, yes).start()

        @pl.when(flag[0] != 1)
        def _():
            copy(n, no).start()

    for n in order:
        copy(n, u0).wait()
    inner = jnp.concatenate([i0[...], i1[...], i2[...], i3[...]], axis=1)
    out[...] = jnp.dot(inner, weights[...], preferred_element_type=F32).astype(BF)


def mix_kernel(ids, sums, hidden, returned, out):
    experts = sums.shape[0] - 8
    named, slot = slots_of(ids, experts)
    inv = lax.rsqrt(sums[experts : experts + 1, :] / D + EPS)
    logits = sums[0:experts, :] * inv
    picked = jnp.where(named, 1.0 / (1.0 + jnp.exp(-logits)), 0.0)
    share = picked / jnp.sum(picked, axis=0, keepdims=True)
    wide = spread(slot, share)
    high = wide.astype(BF)
    low = (wide - high.astype(F32)).astype(BF)
    rows = returned[...]
    dims = (((0,), (0,)), ((), ()))
    mixed = lax.dot_general(high, rows, dims, preferred_element_type=F32)
    mixed += lax.dot_general(low, rows, dims, preferred_element_type=F32)
    out[...] = (hidden[...].astype(F32) + mixed).astype(BF)


def body(resid, queries, keys, values, norm_gain, w_router, expert_ids, w_gate, w_up, w_down):
    tokens, width = resid.shape
    experts = lax.axis_size("ep")
    slots = experts * CAP
    units = w_gate.shape[2]
    sec, tp = lax.axis_index("sec"), lax.axis_index("tp")
    parity = (tp % 2).astype(jnp.int32).reshape(1)
    flag = (sec == tp // 2).astype(jnp.int32).reshape(1)
    ids = expert_ids.T
    gain = norm_gain.reshape(1, width)

    payload = struct((3 * units, width), BF)
    first, second = call(
        pack_kernel,
        [payload, payload],
        [SM, ANY, ANY, ANY],
        [pltpu.SemaphoreType.DMA((18,))],
        single=False,
    )(parity, w_gate, w_up, w_down)
    stay, turn = [], []
    for s in range(2):
        for t in range(N_TP):
            here = s * N_TP + t
            if s == t // 2:
                stay.append((here, here))
            else:
                stay.append((here, (1 - s) * N_TP + (t + 2) % N_TP))
            if s == ((t + 1) % N_TP) // 2:
                turn.append((here, s * N_TP + (t + 1) % N_TP))
            else:
                turn.append((here, (1 - s) * N_TP + (t + 3) % N_TP))
    u0 = lax.ppermute(first, ("sec", "tp"), stay)
    u1 = lax.ppermute(second, ("sec", "tp"), turn)
    swap = [(0, 1), (1, 0)]
    v0 = lax.ppermute(u0, "sec", swap)
    v1 = lax.ppermute(u1, "sec", swap)

    hidden, outgoing = call(
        lambda *refs: attention_kernel(experts, *refs),
        [struct((tokens, width), BF), struct((slots, width), BF)],
        [VM] * 5,
        cost=pl.CostEstimate(flops=300_000_000, bytes_accessed=2_500_000, transcendentals=131072),
    )(ids, queries, keys, values, resid)
    arrived = lax.all_to_all(
        outgoing.reshape(experts, CAP, width), "ep", split_axis=0, concat_axis=0, tiled=True
    ).reshape(slots, width)

    sums = call(
        router_kernel, struct((experts + 8, tokens), F32), [VM] * 3,
        cost=pl.CostEstimate(flops=150_000_000, bytes_accessed=600_000, transcendentals=0),
    )(hidden, gain, w_router.T)
    sums = lax.psum(sums, "tp")

    message = struct((slots + 16, 2 * units), BF)
    own, own_square, *outs = call(
        up_kernel,
        [struct((slots, 2 * units), F32), struct((8, slots), F32), message, message, message],
        [SM, VM, VM, ANY, ANY, ANY, ANY],
        [pltpu.VMEM((N_TP, 2 * units, width), BF), pltpu.SemaphoreType.DMA((N_TP,))],
        cost=pl.CostEstimate(flops=2_200_000_000, bytes_accessed=8_000_000, transcendentals=0),
    )(flag, arrived, gain, u0, u1, v0, v1)
    got = [None] * N_TP
    for k in (2, 1, 3):
        got[k] = lax.ppermute(outs[k - 1], "tp", [(i, (i - k) % N_TP) for i in range(N_TP)])
    inner = call(inner_kernel, struct((slots, units), BF), [VM] * 5)(
        own, own_square, got[1], got[2], got[3]
    )
    inners = [inner] + [None] * 3
    for k in (2, 1, 3):
        inners[k] = lax.ppermute(inner, "tp", [(i, (i + k) % N_TP) for i in range(N_TP)])
    partial = call(
        down_kernel,
        struct((slots, width), BF),
        [SM, VM, VM, VM, VM, ANY, ANY, ANY, ANY],
        [pltpu.VMEM((N_TP * units, width), BF), pltpu.SemaphoreType.DMA((N_TP,))],
        cost=pl.CostEstimate(flops=1_100_000_000, bytes_accessed=4_000_000, transcendentals=0),
    )(flag, *inners, u0, u1, v0, v1)
    returned = lax.all_to_all(
        partial.reshape(experts, CAP, width), "ep", split_axis=0, concat_axis=0, tiled=True
    ).reshape(slots, width)
    return call(mix_kernel, struct((tokens, width), BF), [VM] * 4)(ids, sums, hidden, returned)


def solution(mesh):
    rows, cols = P(("sec", "ep"), "tp"), P(("sec", "ep"), None)
    return jax.shard_map(
        body,
        mesh=mesh,
        in_specs=(
            rows,
            rows,
            rows,
            rows,
            P("tp"),
            P("tp", None),
            cols,
            P("ep", "sec", "tp"),
            P("ep", "sec", "tp"),
            P("ep", "tp", "sec"),
        ),
        out_specs=rows,
        check_vma=False,
    )
```

time: 335 us -> 162 us (0.48)
  the two profiles are of different devices: /device:TPU:1 before, /device:TPU:6 now
where the time goes in v1:
time: 162 us
  waiting for transfers between devices  71.7 us (44%)
  starting transfers between devices  55.4 us (34%)
  Pallas kernels  15.2 us (9%)
  blocking collectives  14.4 us (9%)
  local copies, waits for them, and re-layouts  4.69 us (3%)
    ppermute x3, waiting for transfers between devices, body(): lax.ppermute(outs[k - 1], 'tp', [(i, (i - k) % N_TP) for i in range(N_TP)])  19 us
    all_to_all x1, waiting for transfers between devices, body(): lax.all_to_all(partial.reshape(experts, CAP, width), 'ep', split_axis=0,...  14.6 us
    psum x1, blocking collectives, body(): sums = lax.psum(sums, 'tp')  14.4 us
    all_to_all x1, waiting for transfers between devices, body(): lax.all_to_all(outgoing.reshape(experts, CAP, width), 'ep', split_axis=0,...  12.4 us
    ppermute x3, waiting for transfers between devices, body(): lax.ppermute(inner, 'tp', [(i, (i + k) % N_TP) for i in range(N_TP)])  12.3 us
    ppermute x1, waiting for transfers between devices, body(): u0 = lax.ppermute(first, ('sec', 'tp'), stay)  11.8 us
    all_to_all x1, starting transfers between devices, body(): lax.all_to_all(outgoing.reshape(experts, CAP, width), 'ep', split_axis=0,...  11.7 us
    ppermute x3, starting transfers between devices, body(): lax.ppermute(outs[k - 1], 'tp', [(i, (i - k) % N_TP) for i in range(N_TP)])  11.7 us
  transfers between devices with their start and end apart: 12, of which 10 were waited for; matrix products, arithmetic and copies ran while one was open for 0% of the time, Pallas kernels for 2%

profile of v1, /device:TPU:6, one launch (start us, length us, event | category | flops | bytes accessed | tf_op | source)
XLA Modules:
  0.0 161.7 jit_solution(10501536340614737466)
XLA Ops:
  0.0 0.0 copy-start.2
  0.0 1.2 copy-done.2
  1.2 0.0 copy-start.3
  1.2 1.2 copy-done.3
  2.5 0.0 copy-start.4
  2.5 1.2 copy-done.4
  3.7 0.0 copy-start.8
  3.7 0.0 copy-start.9
  3.7 0.0 copy-start.10
  3.7 0.0 copy-start.11
  3.7 0.0 copy-start.12
  3.7 1.8 %shard_map.102 = (bf16[768,1024]{1,0:T(8,128)(2,1)}, bf16[768,1024]{1,0:T(8,128)(2,1)}) custom-call(s32[1]{0:T(128)} %bitcast.6.parity, bf16[1,2048,256]{2,1,0:T(8,128)(2,1)S(1)} %copy-done.2, bf16[1,2048,256]{2,1,0:T(8,128)(2,1)S(1)} %copy-done.3, bf16[1,256,2048]{2,1,0:T(8,128)(2,1)S(1)} %copy-done.4), custom_call_target="tpu_custom_call" | custom-call | tf_op jit(solution)/shard_map/pallas_call | solution.py:244
  5.5 2.8 %collective-permute-start = (bf16[768,1024]{1,0:T(8,128)(2,1)}, bf16[768,1024]{1,0:T(8,128)(2,1)S(1)}, u32[]{:S(2)}, u32[]{:S(2)}) collective-permute-start(bf16[768,1024]{1,0:T(8,128)(2,1)} %get-tuple-element.16), channel_id=1, source_target_pairs={{0,0},{1,1},{2,256},{3,257},{256,2},{257,3},{258,258},{259,259},{4... | collective-permute-start | bytes 4718600 | tf_op jit(solution)/shard_map/ppermute | solution.py:263
  8.3 7.1 %collective-permute-start.1 = (bf16[768,1024]{1,0:T(8,128)(2,1)}, bf16[768,1024]{1,0:T(8,128)(2,1)S(1)}, u32[]{:S(2)}, u32[]{:S(2)}) collective-permute-start(bf16[768,1024]{1,0:T(8,128)(2,1)} %get-tuple-element.17), channel_id=1, source_target_pairs={{0,1},{1,256},{2,257},{3,0},{256,3},{257,258},{258,259},{259,2},{4... | collective-permute-start | bytes 4718600 | tf_op jit(solution)/shard_map/ppermute | solution.py:264
  15.3 0.0 copy-done.8
  15.3 0.0 copy-done.9
  15.4 0.0 copy-done.10
  15.4 0.0 copy-done.11
  15.4 0.0 copy-done.12
  15.4 0.0 copy-start.7
  15.4 2.2 %shard_map.100 = (bf16[128,1024]{1,0:T(8,128)(2,1)S(1)}, bf16[512,1024]{1,0:T(8,128)(2,1)S(1)}) custom-call(s32[2,128]{1,0:T(2,128)S(1)} %bitcast.14, bf16[128,1024]{1,0:T(8,128)(2,1)S(1)} %copy-done.9, bf16[128,1024]{1,0:T(8,128)(2,1)S(1)} %copy-done.10, bf16[128,1024]{1,0:T(8,128)(2,1)S(1)} %copy-done.11, bf16[128,1024]{1,0:T(8,128)(2,1)S(1)} %copy-done.12), custom_call_target="tpu_custom_call" | custom-call | flops 300000000 | bytes 2500000 | tf_op jit(solution)/shard_map/pallas_call | solution.py:269
  17.6 0.0 copy-start.5
  17.6 1.0 copy-done.5
  18.6 11.7 %all-to-all-start = ((bf16[64,8,1024]{2,1,0:T(8,128)(2,1)}), bf16[64,8,1024]{2,1,0:T(8,128)(2,1)}, u32[]{:S(2)}, u32[]{:S(2)}) async-start(bf16[64,8,1024]{2,1,0:T(8,128)(2,1)} %bitcast.10), calls=%async_computation | async-start | bytes 2097152 | tf_op jit(solution)/shard_map/all_to_all | solution.py:275
  30.3 11.8 %collective-permute-done.u0 = bf16[768,1024]{1,0:T(8,128)(2,1)S(1)} collective-permute-done((bf16[768,1024]{1,0:T(8,128)(2,1)}, bf16[768,1024]{1,0:T(8,128)(2,1)S(1)}, u32[]{:S(2)}, u32[]{:S(2)}) %collective-permute-start) | collective-permute-done | bytes 1572896 | tf_op jit(solution)/shard_map/ppermute | solution.py:263
  42.1 1.9 %collective-permute-start.2 = (bf16[768,1024]{1,0:T(8,128)(2,1)S(1)}, bf16[768,1024]{1,0:T(8,128)(2,1)}, u32[]{:S(2)}, u32[]{:S(2)}) collective-permute-start(bf16[768,1024]{1,0:T(8,128)(2,1)S(1)} %collective-permute-done.u0), channel_id=1, source_target_pairs={{0,256},{256,0},{1,257},{257,1},{2,258},{258,2},{3,259},{259,3},{4... | collective-permute-start | bytes 4718600 | tf_op jit(solution)/shard_map/ppermute | solution.py:266
  44.0 1.8 %collective-permute-done.1.u1 = bf16[768,1024]{1,0:T(8,128)(2,1)S(1)} collective-permute-done((bf16[768,1024]{1,0:T(8,128)(2,1)}, bf16[768,1024]{1,0:T(8,128)(2,1)S(1)}, u32[]{:S(2)}, u32[]{:S(2)}) %collective-permute-start.1) | collective-permute-done | bytes 1572896 | tf_op jit(solution)/shard_map/ppermute | solution.py:264
  45.8 0.0 copy-start
  45.8 1.9 %collective-permute-start.3 = (bf16[768,1024]{1,0:T(8,128)(2,1)S(1)}, bf16[768,1024]{1,0:T(8,128)(2,1)}, u32[]{:S(2)}, u32[]{:S(2)}) collective-permute-start(bf16[768,1024]{1,0:T(8,128)(2,1)S(1)} %collective-permute-done.1.u1), channel_id=1, source_target_pairs={{0,256},{256,0},{1,257},{257,1},{2,258},{258,2},{3,259},{259,3},{4... | collective-permute-start | bytes 4718600 | tf_op jit(solution)/shard_map/ppermute | solution.py:267
  47.8 12.4 %all-to-all-done = bf16[64,8,1024]{2,1,0:T(8,128)(2,1)} async-done(((bf16[64,8,1024]{2,1,0:T(8,128)(2,1)}), bf16[64,8,1024]{2,1,0:T(8,128)(2,1)}, u32[]{:S(2)}, u32[]{:S(2)}) %all-to-all-start) | async-done | bytes 1048608 | tf_op jit(solution)/shard_map/all_to_all | solution.py:275
  60.1 0.0 collective-permute-done.2.v0
  60.1 0.0 collective-permute-done.3.v1
  60.1 0.0 copy-done
  60.1 0.0 copy-done.7
  60.1 5.0 %shard_map.103 = (f32[512,512]{1,0:T(8,128)S(1)}, f32[8,512]{1,0:T(8,128)S(1)}, bf16[528,512]{1,0:T(8,128)(2,1)S(1)}, bf16[528,512]{1,0:T(8,128)(2,1)S(1)}, bf16[528,512]{1,0:T(8,128)(2,1)S(1)}) custom-call(s32[1]{0:T(128)} %bitcast.3.flag, bf16[512,1024]{1,0:T(8,128)(2,1)} %bitcast.5.x, f32[1,1024]{1,0:T(1,128)S(1)} %bitcast.12, ...), custom_call_target="tpu_custom_call" | custom-call | flops 2200000000 | bytes 8000000 | tf_op jit(solution)/shard_map/pallas_call | solution.py:286
  65.2 0.0 copy-start.1
  65.2 3.0 %collective-permute-start.4 = (bf16[528,512]{1,0:T(8,128)(2,1)S(1)}, bf16[528,512]{1,0:T(8,128)(2,1)S(1)}, u32[]{:S(2)}, u32[]{:S(2)}) collective-permute-start(bf16[528,512]{1,0:T(8,128)(2,1)S(1)} %get-tuple-element.20), channel_id=1, source_target_pairs={{0,3},{1,0},{2,1},{3,2},{4,7},{5,4},{6,5},{7,6},{8,11},{9,8},{10,9... | collective-permute-start | bytes 1622024 | tf_op jit(solution)/shard_map/ppermute | solution.py:295
  68.2 4.2 %collective-permute-start.5 = (bf16[528,512]{1,0:T(8,128)(2,1)S(1)}, bf16[528,512]{1,0:T(8,128)(2,1)S(1)}, u32[]{:S(2)}, u32[]{:S(2)}) collective-permute-start(bf16[528,512]{1,0:T(8,128)(2,1)S(1)} %get-tuple-element.21), channel_id=1, source_target_pairs={{0,2},{1,3},{2,0},{3,1},{4,6},{5,7},{6,4},{7,5},{8,10},{9,11},{10,... | collective-permute-start | bytes 1622024 | tf_op jit(solution)/shard_map/ppermute | solution.py:295
  72.4 4.5 %collective-permute-start.6 = (bf16[528,512]{1,0:T(8,128)(2,1)S(1)}, bf16[528,512]{1,0:T(8,128)(2,1)S(1)}, u32[]{:S(2)}, u32[]{:S(2)}) collective-permute-start(bf16[528,512]{1,0:T(8,128)(2,1)S(1)} %get-tuple-element.22), channel_id=1, source_target_pairs={{0,1},{1,2},{2,3},{3,0},{4,5},{5,6},{6,7},{7,4},{8,9},{9,10},{10,1... | collective-permute-start | bytes 1622024 | tf_op jit(solution)/shard_map/ppermute | solution.py:295
  76.9 4.9 %collective-permute-done.4.r1 = bf16[528,512]{1,0:T(8,128)(2,1)S(1)} collective-permute-done((bf16[528,512]{1,0:T(8,128)(2,1)S(1)}, bf16[528,512]{1,0:T(8,128)(2,1)S(1)}, u32[]{:S(2)}, u32[]{:S(2)}) %collective-permute-start.4) | collective-permute-done | bytes 540704 | tf_op jit(solution)/shard_map/ppermute | solution.py:295
  81.8 12.8 %collective-permute-done.5.r2 = bf16[528,512]{1,0:T(8,128)(2,1)S(1)} collective-permute-done((bf16[528,512]{1,0:T(8,128)(2,1)S(1)}, bf16[528,512]{1,0:T(8,128)(2,1)S(1)}, u32[]{:S(2)}, u32[]{:S(2)}) %collective-permute-start.5) | collective-permute-done | bytes 540704 | tf_op jit(solution)/shard_map/ppermute | solution.py:295
  94.5 1.4 collective-permute-done.6.r3
  95.9 0.4 shard_map.104.i0
  96.3 4.5 %collective-permute-start.7 = (bf16[512,256]{1,0:T(8,128)(2,1)S(1)}, bf16[512,256]{1,0:T(8,128)(2,1)S(1)}, u32[]{:S(2)}, u32[]{:S(2)}) collective-permute-start(bf16[512,256]{1,0:T(8,128)(2,1)S(1)} %shard_map.104.i0), channel_id=1, source_target_pairs={{0,1},{1,2},{2,3},{3,0},{4,5},{5,6},{6,7},{7,4},{8,9},{9,10},{10,1... | collective-permute-start | bytes 786440 | tf_op jit(solution)/shard_map/ppermute | solution.py:301
  100.8 1.9 %collective-permute-start.8 = (bf16[512,256]{1,0:T(8,128)(2,1)S(1)}, bf16[512,256]{1,0:T(8,128)(2,1)S(1)}, u32[]{:S(2)}, u32[]{:S(2)}) collective-permute-start(bf16[512,256]{1,0:T(8,128)(2,1)S(1)} %shard_map.104.i0), channel_id=1, source_target_pairs={{0,2},{1,3},{2,0},{3,1},{4,6},{5,7},{6,4},{7,5},{8,10},{9,11},{10,... | collective-permute-start | bytes 786440 | tf_op jit(solution)/shard_map/ppermute | solution.py:301
  102.8 2.8 %collective-permute-start.9 = (bf16[512,256]{1,0:T(8,128)(2,1)S(1)}, bf16[512,256]{1,0:T(8,128)(2,1)S(1)}, u32[]{:S(2)}, u32[]{:S(2)}) collective-permute-start(bf16[512,256]{1,0:T(8,128)(2,1)S(1)} %shard_map.104.i0), channel_id=1, source_target_pairs={{0,3},{1,0},{2,1},{3,2},{4,7},{5,4},{6,5},{7,6},{8,11},{9,8},{10,9... | collective-permute-start | bytes 786440 | tf_op jit(solution)/shard_map/ppermute | solution.py:301
  105.5 6.6 %collective-permute-done.7.i1 = bf16[512,256]{1,0:T(8,128)(2,1)S(1)} collective-permute-done((bf16[512,256]{1,0:T(8,128)(2,1)S(1)}, bf16[512,256]{1,0:T(8,128)(2,1)S(1)}, u32[]{:S(2)}, u32[]{:S(2)}) %collective-permute-start.7) | collective-permute-done | bytes 262176 | tf_op jit(solution)/shard_map/ppermute | solution.py:301
  112.2 1.3 collective-permute-done.8.i2
  113.5 4.3 %collective-permute-done.9.i3 = bf16[512,256]{1,0:T(8,128)(2,1)S(1)} collective-permute-done((bf16[512,256]{1,0:T(8,128)(2,1)S(1)}, bf16[512,256]{1,0:T(8,128)(2,1)S(1)}, u32[]{:S(2)}, u32[]{:S(2)}) %collective-permute-start.9) | collective-permute-done | bytes 262176 | tf_op jit(solution)/shard_map/ppermute | solution.py:301
  117.8 0.0 copy-done.1
  117.8 3.5 %shard_map.105 = bf16[512,1024]{1,0:T(8,128)(2,1)} custom-call(s32[1]{0:T(128)} %bitcast.3.flag, bf16[512,256]{1,0:T(8,128)(2,1)S(1)} %shard_map.104.i0, bf16[512,256]{1,0:T(8,128)(2,1)S(1)} %collective-permute-done.7.i1, bf16[512,256]{1,0:T(8,128)(2,1)S(1)} %collective-permute-done.8.i2, bf16[512,256]{1,0:T(8,128)(2,1)S(1)} %collective-permute-done.9.i3, ...), custom_call_target="tpu_custom_call" | custom-call | flops 1100000000 | bytes 4000000 | tf_op jit(solution)/shard_map/pallas_call | solution.py:302
  121.3 0.0 copy-start.6
  121.3 9.1 %all-to-all-start.1 = ((bf16[64,8,1024]{2,1,0:T(8,128)(2,1)}), bf16[64,8,1024]{2,1,0:T(8,128)(2,1)S(1)}, u32[]{:S(2)}, u32[]{:S(2)}) async-start(bf16[64,8,1024]{2,1,0:T(8,128)(2,1)} %bitcast.7), calls=%async_computation.1 | async-start | bytes 2097152 | tf_op jit(solution)/shard_map/all_to_all | solution.py:309
  130.4 0.0 copy-done.6
  130.4 1.0 shard_map.101
  131.4 14.4 %psum.7.sums = f32[72,128]{1,0:T(8,128)S(1)} all-reduce(f32[72,128]{1,0:T(8,128)S(1)} %shard_map.101), channel_id=1, replica_groups=mesh['sec'=2,'ep'=64,'tp'=4] {'tp'}, use_global_device_ids=true, to_apply=%region_0.1 | all-reduce | flops 9216 | bytes 73728 | tf_op jit(solution)/shard_map/psum | solution.py:283
  145.8 14.6 %all-to-all-done.1 = bf16[64,8,1024]{2,1,0:T(8,128)(2,1)S(1)} async-done(((bf16[64,8,1024]{2,1,0:T(8,128)(2,1)}), bf16[64,8,1024]{2,1,0:T(8,128)(2,1)S(1)}, u32[]{:S(2)}, u32[]{:S(2)}) %all-to-all-start.1) | async-done | bytes 1048608 | tf_op jit(solution)/shard_map/all_to_all | solution.py:309
  160.3 1.3 shard_map.106
Async XLA Ops:
  0.0 1.2 copy-start.2
  1.2 1.2 copy-start.3
  2.5 1.2 copy-start.4
  3.7 11.7 %copy-start.8 = (s32[128,2]{0,1:T(2,128)S(1)}, s32[128,2]{0,1:T(2,128)}, u32[]{:S(2)}) copy-start(s32[128,2]{0,1:T(2,128)} %param.16) | copy-start | bytes 3076
  3.7 11.7 %copy-start.9 = (bf16[128,1024]{1,0:T(8,128)(2,1)S(1)}, bf16[128,1024]{1,0:T(8,128)(2,1)}, u32[]{:S(2)}) copy-start(bf16[128,1024]{1,0:T(8,128)(2,1)} %refs_1_.1) | copy-start | bytes 786436
  3.7 11.7 %copy-start.10 = (bf16[128,1024]{1,0:T(8,128)(2,1)S(1)}, bf16[128,1024]{1,0:T(8,128)(2,1)}, u32[]{:S(2)}) copy-start(bf16[128,1024]{1,0:T(8,128)(2,1)} %refs_2_.1) | copy-start | bytes 786436
  3.7 11.7 %copy-start.11 = (bf16[128,1024]{1,0:T(8,128)(2,1)S(1)}, bf16[128,1024]{1,0:T(8,128)(2,1)}, u32[]{:S(2)}) copy-start(bf16[128,1024]{1,0:T(8,128)(2,1)} %refs_3_.1) | copy-start | bytes 786436
  3.7 11.7 %copy-start.12 = (bf16[128,1024]{1,0:T(8,128)(2,1)S(1)}, bf16[128,1024]{1,0:T(8,128)(2,1)}, u32[]{:S(2)}) copy-start(bf16[128,1024]{1,0:T(8,128)(2,1)} %refs_4_.1) | copy-start | bytes 786436
  5.5 36.6 %collective-permute-start = (bf16[768,1024]{1,0:T(8,128)(2,1)}, bf16[768,1024]{1,0:T(8,128)(2,1)S(1)}, u32[]{:S(2)}, u32[]{:S(2)}) collective-permute-start(bf16[768,1024]{1,0:T(8,128)(2,1)} %get-tuple-element.16), channel_id=1, source_target_pairs={{0,0},{1,1},{2,256},{3,257},{256,2},{257,3},{258,258},{259,259},{4... | collective-permute-start | bytes 4718600 | tf_op jit(solution)/shard_map/ppermute | solution.py:263
  8.3 37.5 %collective-permute-start.1 = (bf16[768,1024]{1,0:T(8,128)(2,1)}, bf16[768,1024]{1,0:T(8,128)(2,1)S(1)}, u32[]{:S(2)}, u32[]{:S(2)}) collective-permute-start(bf16[768,1024]{1,0:T(8,128)(2,1)} %get-tuple-element.17), channel_id=1, source_target_pairs={{0,1},{1,256},{2,257},{3,0},{256,3},{257,258},{258,259},{259,2},{4... | collective-permute-start | bytes 4718600 | tf_op jit(solution)/shard_map/ppermute | solution.py:264
  15.4 44.7 %copy-start.7 = (f32[1024]{0:T(1024)S(1)}, f32[1024]{0:T(1024)}, u32[]{:S(2)}) copy-start(f32[1024]{0:T(1024)} %param.14) | copy-start | bytes 12292
  17.6 1.0 copy-start.5
  18.6 41.5 %all-to-all-start = ((bf16[64,8,1024]{2,1,0:T(8,128)(2,1)}), bf16[64,8,1024]{2,1,0:T(8,128)(2,1)}, u32[]{:S(2)}, u32[]{:S(2)}) async-start(bf16[64,8,1024]{2,1,0:T(8,128)(2,1)} %bitcast.10), calls=%async_computation | async-start | bytes 2097152 | tf_op jit(solution)/shard_map/all_to_all | solution.py:275
  42.1 18.0 %collective-permute-start.2 = (bf16[768,1024]{1,0:T(8,128)(2,1)S(1)}, bf16[768,1024]{1,0:T(8,128)(2,1)}, u32[]{:S(2)}, u32[]{:S(2)}) collective-permute-start(bf16[768,1024]{1,0:T(8,128)(2,1)S(1)} %collective-permute-done.u0), channel_id=1, source_target_pairs={{0,256},{256,0},{1,257},{257,1},{2,258},{258,2},{3,259},{259,3},{4... | collective-permute-start | bytes 4718600 | tf_op jit(solution)/shard_map/ppermute | solution.py:266
  45.8 14.3 %copy-start = (bf16[768,1024]{1,0:T(8,128)(2,1)}, bf16[768,1024]{1,0:T(8,128)(2,1)S(1)}, u32[]{:S(2)}) copy-start(bf16[768,1024]{1,0:T(8,128)(2,1)S(1)} %collective-permute-done.1.u1) | copy-start | bytes 4718596
  45.8 14.3 %collective-permute-start.3 = (bf16[768,1024]{1,0:T(8,128)(2,1)S(1)}, bf16[768,1024]{1,0:T(8,128)(2,1)}, u32[]{:S(2)}, u32[]{:S(2)}) collective-permute-start(bf16[768,1024]{1,0:T(8,128)(2,1)S(1)} %collective-permute-done.1.u1), channel_id=1, source_target_pairs={{0,256},{256,0},{1,257},{257,1},{2,258},{258,2},{3,259},{259,3},{4... | collective-permute-start | bytes 4718600 | tf_op jit(solution)/shard_map/ppermute | solution.py:267
  65.2 52.6 %copy-start.1 = (bf16[768,1024]{1,0:T(8,128)(2,1)S(1)}, bf16[768,1024]{1,0:T(8,128)(2,1)}, u32[]{:S(2)}) copy-start(bf16[768,1024]{1,0:T(8,128)(2,1)} %copy-done) | copy-start | bytes 4718596
  65.2 16.6 %collective-permute-start.4 = (bf16[528,512]{1,0:T(8,128)(2,1)S(1)}, bf16[528,512]{1,0:T(8,128)(2,1)S(1)}, u32[]{:S(2)}, u32[]{:S(2)}) collective-permute-start(bf16[528,512]{1,0:T(8,128)(2,1)S(1)} %get-tuple-element.20), channel_id=1, source_target_pairs={{0,3},{1,0},{2,1},{3,2},{4,7},{5,4},{6,5},{7,6},{8,11},{9,8},{10,9... | collective-permute-start | bytes 1622024 | tf_op jit(solution)/shard_map/ppermute | solution.py:295
  68.2 26.4 %collective-permute-start.5 = (bf16[528,512]{1,0:T(8,128)(2,1)S(1)}, bf16[528,512]{1,0:T(8,128)(2,1)S(1)}, u32[]{:S(2)}, u32[]{:S(2)}) collective-permute-start(bf16[528,512]{1,0:T(8,128)(2,1)S(1)} %get-tuple-element.21), channel_id=1, source_target_pairs={{0,2},{1,3},{2,0},{3,1},{4,6},{5,7},{6,4},{7,5},{8,10},{9,11},{10,... | collective-permute-start | bytes 1622024 | tf_op jit(solution)/shard_map/ppermute | solution.py:295
  72.4 23.5 %collective-permute-start.6 = (bf16[528,512]{1,0:T(8,128)(2,1)S(1)}, bf16[528,512]{1,0:T(8,128)(2,1)S(1)}, u32[]{:S(2)}, u32[]{:S(2)}) collective-permute-start(bf16[528,512]{1,0:T(8,128)(2,1)S(1)} %get-tuple-element.22), channel_id=1, source_target_pairs={{0,1},{1,2},{2,3},{3,0},{4,5},{5,6},{6,7},{7,4},{8,9},{9,10},{10,1... | collective-permute-start | bytes 1622024 | tf_op jit(solution)/shard_map/ppermute | solution.py:295
  96.3 15.9 %collective-permute-start.7 = (bf16[512,256]{1,0:T(8,128)(2,1)S(1)}, bf16[512,256]{1,0:T(8,128)(2,1)S(1)}, u32[]{:S(2)}, u32[]{:S(2)}) collective-permute-start(bf16[512,256]{1,0:T(8,128)(2,1)S(1)} %shard_map.104.i0), channel_id=1, source_target_pairs={{0,1},{1,2},{2,3},{3,0},{4,5},{5,6},{6,7},{7,4},{8,9},{9,10},{10,1... | collective-permute-start | bytes 786440 | tf_op jit(solution)/shard_map/ppermute | solution.py:301
  100.8 12.7 %collective-permute-start.8 = (bf16[512,256]{1,0:T(8,128)(2,1)S(1)}, bf16[512,256]{1,0:T(8,128)(2,1)S(1)}, u32[]{:S(2)}, u32[]{:S(2)}) collective-permute-start(bf16[512,256]{1,0:T(8,128)(2,1)S(1)} %shard_map.104.i0), channel_id=1, source_target_pairs={{0,2},{1,3},{2,0},{3,1},{4,6},{5,7},{6,4},{7,5},{8,10},{9,11},{10,... | collective-permute-start | bytes 786440 | tf_op jit(solution)/shard_map/ppermute | solution.py:301
  102.8 15.0 %collective-permute-start.9 = (bf16[512,256]{1,0:T(8,128)(2,1)S(1)}, bf16[512,256]{1,0:T(8,128)(2,1)S(1)}, u32[]{:S(2)}, u32[]{:S(2)}) collective-permute-start(bf16[512,256]{1,0:T(8,128)(2,1)S(1)} %shard_map.104.i0), channel_id=1, source_target_pairs={{0,3},{1,0},{2,1},{3,2},{4,7},{5,4},{6,5},{7,6},{8,11},{9,8},{10,9... | collective-permute-start | bytes 786440 | tf_op jit(solution)/shard_map/ppermute | solution.py:301
  121.3 9.1 %copy-start.6 = (f32[1024,64]{0,1:T(8,128)S(1)}, f32[1024,64]{0,1:T(8,128)}, u32[]{:S(2)}) copy-start(f32[1024,64]{0,1:T(8,128)} %param.15) | copy-start | bytes 786436
  121.3 39.1 %all-to-all-start.1 = ((bf16[64,8,1024]{2,1,0:T(8,128)(2,1)}), bf16[64,8,1024]{2,1,0:T(8,128)(2,1)S(1)}, u32[]{:S(2)}, u32[]{:S(2)}) async-start(bf16[64,8,1024]{2,1,0:T(8,128)(2,1)} %bitcast.7), calls=%async_computation.1 | async-start | bytes 2097152 | tf_op jit(solution)/shard_map/all_to_all | solution.py:309

commit v2 on v1

v2 whole, which is shorter than its diff:
```python
import math

import jax
import jax.numpy as jnp
from jax import lax
from jax.experimental import pallas as pl
from jax.experimental.pallas import tpu as pltpu
from jax.sharding import PartitionSpec as P

D = 4096
HEAD_DIM = 128
CAP = 8
N_TP = 4
EPS = 1e-06

BF = jnp.bfloat16
F32 = jnp.float32
HIGHEST = lax.Precision.HIGHEST
VMEM_BYTES = 48 * 1024 * 1024
WHOLE_VMEM = 63 * 1024 * 1024


def call(kernel, out_shape, in_specs, out_specs, scratch=(), cost=(0, 0), vmem=VMEM_BYTES):
    return pl.pallas_call(
        kernel,
        out_shape=out_shape,
        in_specs=in_specs,
        out_specs=out_specs,
        scratch_shapes=scratch,
        cost_estimate=pl.CostEstimate(flops=cost[0], bytes_accessed=cost[1], transcendentals=0),
        compiler_params=pltpu.CompilerParams(vmem_limit_bytes=vmem),
    )


VM = pl.BlockSpec(memory_space=pltpu.VMEM)
ANY = pl.BlockSpec(memory_space=pl.ANY)
SM = pl.BlockSpec(memory_space=pltpu.SMEM)


def struct(shape, dtype):
    return jax.ShapeDtypeStruct(shape, dtype)


def nt(a, b, precision=None):
    return lax.dot_general(
        a, b, (((1,), (1,)), ((), ())), precision=precision, preferred_element_type=F32
    )


def pack_kernel(block, gate, up, down, *rest):
    out, sems = rest[-2:]
    width = gate.shape[2]
    span = down.shape[2] // 2
    base = pl.multiple_of(block[0] * span, span)
    rows = pl.ds(base, span)
    copies = [
        (gate.at[0, rows, :], out.at[pl.ds(0, span), pl.ds(0, width)]),
        (up.at[0, rows, :], out.at[pl.ds(0, span), pl.ds(width, width)]),
    ]
    for j in range(2):
        cols = pl.ds(pl.multiple_of(base + j * 2 * width, 2 * width), 2 * width)
        copies.append((down.at[0, :, cols], out.at[pl.ds(span + j * width, width), :]))
    started = [
        pltpu.make_async_copy(src, dst, sems.at[n]) for n, (src, dst) in enumerate(copies)
    ]
    for copy in started:
        copy.start()
    for copy in started:
        copy.wait()


def slots_of(ids_ref, experts):
    tokens = ids_ref.shape[1]
    expert = lax.broadcasted_iota(jnp.int32, (experts, tokens), 0)
    named = (ids_ref[0:1, :] == expert) | (ids_ref[1:2, :] == expert)
    before = lax.broadcasted_iota(jnp.int32, (tokens, tokens), 0) < lax.broadcasted_iota(
        jnp.int32, (tokens, tokens), 1
    )
    rank = jnp.dot(named.astype(BF), before.astype(BF), preferred_element_type=F32)
    return named, jnp.where(named, rank, -1.0)


def spread(slot, value):
    experts, tokens = slot.shape
    turn = lax.broadcasted_iota(jnp.int32, (experts, CAP, tokens), 1).astype(F32)
    hit = slot[:, None, :] == turn
    return jnp.where(hit, value[:, None, :], 0.0).reshape(experts * CAP, tokens)


def attention_kernel(experts, ids, q, k, v, resid, hidden, outgoing, rows, sems):
    tokens, width = q.shape
    scale = 1.0 / math.sqrt(HEAD_DIM)
    _, slot = slots_of(ids, experts)
    pick = spread(slot, jnp.ones_like(slot)).astype(BF)
    copies = []
    for n in range(width // HEAD_DIM):
        cols = slice(n * HEAD_DIM, (n + 1) * HEAD_DIM)
        scores = nt(q[:, cols], k[:, cols]) * scale
        top = jnp.max(scores, axis=1, keepdims=True)
        e = jnp.exp(scores - top)
        weights = (e / jnp.sum(e, axis=1, keepdims=True)).astype(BF)
        attended = jnp.dot(weights, v[:, cols], preferred_element_type=F32)
        h = (resid[:, cols].astype(F32) + attended).astype(BF)
        hidden[:, cols] = h
        rows[:, cols] = jnp.dot(pick, h, preferred_element_type=F32).astype(BF)
        if n % 2 == 1:
            pair = pl.ds((n - 1) * HEAD_DIM, 2 * HEAD_DIM)
            copies.append(
                pltpu.make_async_copy(rows.at[:, pair], outgoing.at[:, pair], sems.at[n // 2])
            )
            copies[-1].start()
    for copy in copies:
        copy.wait()


def router_kernel(hidden, gain, router, out):
    h = hidden[...].astype(F32)
    experts = router.shape[0]
    out[0:experts, :] = nt(router[...], h * gain[...], HIGHEST)
    out[experts : experts + 8, :] = nt(jnp.ones((8, h.shape[1]), F32), h * h, HIGHEST)


def fetch(flag, mine, other, copies_of, nblocks):
    for n in range(nblocks):
        refs = (mine[n % 2], other[n % 2])

        @pl.when(flag[0] == (1 if n < 2 else 0))
        def _():
            for copy in copies_of(n, refs[0]):
                copy.start()

        @pl.when(flag[0] != (1 if n < 2 else 0))
        def _():
            for copy in copies_of(n, refs[1]):
                copy.start()


def split(value):
    high = value.astype(BF)
    return high, (value - high.astype(F32)).astype(BF)


def up_kernel(place, x, gain, sums, u0, u1, v0, v1, out, weights, made, sems, out_sems):
    rows, depth = x.shape
    order = (2, 1, 3, 0)

    def copies_of(n, ref):
        return [pltpu.make_async_copy(ref.at[pl.ds(0, depth), :], weights.at[n], sems.at[n])]

    fetch(place, (u0, u1), (v0, v1), copies_of, N_TP)
    xf = x[...].astype(F32)
    xg = (xf * gain[...]).astype(BF)
    high, low = split(xf * xf)
    ones = jnp.ones((8, depth), BF)
    total = nt(ones, high) + nt(ones, low)
    experts = sums.shape[0] - 8
    tokens = jnp.concatenate([sums[experts : experts + 8, :]] * 4, axis=1)
    tile = lax.broadcasted_iota(jnp.int32, total.shape, 0)
    squares = jnp.concatenate(split(jnp.where(tile < 4, total, tokens)), axis=0)
    half = experts // 2
    parts = split(sums[0:experts, :])
    logits = jnp.concatenate([part[i * half : (i + 1) * half, :] for part in parts for i in range(2)], axis=1)
    done = []
    for n in order:
        copies_of(n, u0)[0].wait()
        made[n, 0:rows, :] = jnp.dot(xg, weights[n], preferred_element_type=F32).astype(BF)
        made[n, rows : rows + 16, :] = squares
        made[n, rows + 16 : rows + 16 + half, :] = logits
        done.append(pltpu.make_async_copy(made.at[n], out.at[place[1 + n]], out_sems.at[n]))
        done[-1].start()
    for copy in done:
        copy.wait()


def inner_kernel(got, inner, sums):
    rows, width = inner.shape
    half = sums.shape[0] // 2 - 4
    total = got[0, 0:rows, :].astype(F32)
    tail = got[0, rows:, :].astype(F32)
    for n in range(1, N_TP):
        total = total + got[n, 0:rows, :].astype(F32)
        tail = tail + got[n, rows:, :].astype(F32)
    square = tail[0:8, :] + tail[8:16, :]
    logits = tail[16 : 16 + half, :]
    logits = logits[:, 0:256] + logits[:, 256:512]
    sums[0:half, :] = logits[:, 0:128]
    sums[half : 2 * half, :] = logits[:, 128:256]
    sums[2 * half : 2 * half + 8, :] = jnp.broadcast_to(square[4:5, 0:128], (8, 128))
    inv = lax.rsqrt(square[0:1, :] / D + EPS)
    for j in range(rows // 128):
        part = slice(j * 128, (j + 1) * 128)
        column = jnp.transpose(jnp.broadcast_to(inv[:, part], (128, 128)), (1, 0))
        column = jnp.concatenate([column] * (width // 128), axis=1)
        gate = total[part, 0:width] * column
        up = total[part, width : 2 * width] * column
        inner[part, :] = (gate * (1.0 / (1.0 + jnp.exp(-gate))) * up).astype(BF)


def down_kernel(flag, i0, i1, i2, i3, u0, u1, v0, v1, out, weights, made, sems, out_sems):
    width = i0.shape[1]
    span = out.shape[1]

    def copies_of(n, ref):
        return [
            pltpu.make_async_copy(
                ref.at[pl.ds(span + j * width, width), :],
                weights.at[pl.ds(n * width, width), pl.ds(j * 2 * width, 2 * width)],
                sems.at[n, j],
            )
            for j in range(2)
        ]

    fetch(flag, (u0, u1), (v0, v1), copies_of, N_TP)
    inner = jnp.concatenate([i0[...], i1[...], i2[...], i3[...]], axis=1)
    for n in range(N_TP):
        for copy in copies_of(n, u0):
            copy.wait()
    done = []
    for j in range(4):
        cols = pl.ds(j * width, width)
        made[:, cols] = jnp.dot(inner, weights[:, cols], preferred_element_type=F32).astype(BF)
        done.append(pltpu.make_async_copy(made.at[:, cols], out.at[:, cols], out_sems.at[j]))
        done[-1].start()
    for copy in done:
        copy.wait()


def mix_kernel(ids, sums, hidden, returned, out):
    experts = sums.shape[0] - 8
    named, slot = slots_of(ids, experts)
    inv = lax.rsqrt(sums[experts : experts + 1, :] / D + EPS)
    logits = sums[0:experts, :] * inv
    picked = jnp.where(named, 1.0 / (1.0 + jnp.exp(-logits)), 0.0)
    share = picked / jnp.sum(picked, axis=0, keepdims=True)
    wide = spread(slot, share)
    high = wide.astype(BF)
    low = (wide - high.astype(F32)).astype(BF)
    rows = returned[...]
    dims = (((0,), (0,)), ((), ()))
    mixed = lax.dot_general(high, rows, dims, preferred_element_type=F32)
    mixed += lax.dot_general(low, rows, dims, preferred_element_type=F32)
    out[...] = (hidden[...].astype(F32) + mixed).astype(BF)


def body(resid, queries, keys, values, norm_gain, w_router, expert_ids, w_gate, w_up, w_down):
    tokens, width = resid.shape
    experts = lax.axis_size("ep")
    slots = experts * CAP
    units = w_gate.shape[2]
    sec, tp = lax.axis_index("sec"), lax.axis_index("tp")
    parity = (tp % 2).astype(jnp.int32).reshape(1)
    flag = (sec == tp // 2).astype(jnp.int32).reshape(1)
    ids = expert_ids.T
    gain = norm_gain.reshape(1, width)

    payload = struct((width + 2 * units, 2 * units), BF)
    dma = pltpu.SemaphoreType.DMA

    def pack(block, *after):
        return call(
            pack_kernel, payload, [SM] + [ANY] * (3 + len(after)), ANY, [dma((4,))],
            (0, 3_000_000), WHOLE_VMEM,
        )(block, w_gate, w_up, w_down, *after)

    stay, turn = [], []
    for s in range(2):
        for t in range(N_TP):
            here = s * N_TP + t
            if s == t // 2:
                stay.append((here, here))
            else:
                stay.append((here, (1 - s) * N_TP + (t + 2) % N_TP))
            if s == ((t + 1) % N_TP) // 2:
                turn.append((here, s * N_TP + (t + 1) % N_TP))
            else:
                turn.append((here, (1 - s) * N_TP + (t + 3) % N_TP))
    swap = [(0, 1), (1, 0)]
    u0 = lax.ppermute(pack(parity), ("sec", "tp"), stay)
    v0 = lax.ppermute(u0, "sec", swap)

    hidden, outgoing = call(
        lambda *refs: attention_kernel(experts, *refs),
        [struct((tokens, width), BF), struct((slots, width), BF)],
        [VM] * 5,
        [VM, ANY],
        [pltpu.VMEM((slots, width), BF), dma((4,))],
        (300_000_000, 2_500_000),
    )(ids, queries, keys, values, resid)
    arrived = lax.all_to_all(
        outgoing.reshape(experts, CAP, width), "ep", split_axis=0, concat_axis=0, tiled=True
    ).reshape(slots, width)

    u1 = lax.ppermute(pack(1 - parity, outgoing), ("sec", "tp"), turn)
    v1 = lax.ppermute(u1, "sec", swap)
    sums = call(
        router_kernel, struct((experts + 8, tokens), F32), [VM] * 3, VM, (), (150_000_000, 600_000)
    )(hidden, gain, w_router.T)

    lines = slots + 16 + experts // 2
    message = struct((N_TP, lines, 2 * units), BF)
    place = jnp.concatenate([flag] + [((tp - k) % N_TP).reshape(1) for k in range(N_TP)])
    partial = call(
        up_kernel,
        message,
        [SM, VM, VM, VM, ANY, ANY, ANY, ANY],
        ANY,
        [
            pltpu.VMEM((N_TP, width, 2 * units), BF),
            pltpu.VMEM((N_TP, lines, 2 * units), BF),
            dma((N_TP,)),
            dma((N_TP,)),
        ],
        (2_200_000_000, 8_000_000),
    )(place, arrived, gain, sums, u0, u1, v0, v1)
    got = lax.all_to_all(partial, "tp", split_axis=0, concat_axis=0, tiled=True)
    inner, sums = call(
        inner_kernel,
        [struct((slots, units), BF), struct((experts + 8, tokens), F32)],
        [VM],
        [VM, VM],
        (),
        (1_000_000, 2_500_000),
    )(got)
    inners = [inner] + [None] * 3
    for k in (2, 1, 3):
        inners[k] = lax.ppermute(inner, "tp", [(i, (i + k) % N_TP) for i in range(N_TP)])
    expert_out = call(
        down_kernel,
        struct((slots, width), BF),
        [SM, VM, VM, VM, VM, ANY, ANY, ANY, ANY],
        ANY,
        [
            pltpu.VMEM((N_TP * units, width), BF),
            pltpu.VMEM((slots, width), BF),
            dma((N_TP, 2)),
            dma((4,)),
        ],
        (1_100_000_000, 4_000_000),
    )(flag, *inners, u0, u1, v0, v1)
    returned = lax.all_to_all(
        expert_out.reshape(experts, CAP, width), "ep", split_axis=0, concat_axis=0, tiled=True
    ).reshape(slots, width)
    return call(mix_kernel, struct((tokens, width), BF), [VM] * 4, VM)(ids, sums, hidden, returned)


def solution(mesh):
    rows, cols = P(("sec", "ep"), "tp"), P(("sec", "ep"), None)
    return jax.shard_map(
        body,
        mesh=mesh,
        in_specs=(
            rows,
            rows,
            rows,
            rows,
            P("tp"),
            P("tp", None),
            cols,
            P("ep", "sec", "tp"),
            P("ep", "sec", "tp"),
            P("ep", "tp", "sec"),
        ),
        out_specs=rows,
        check_vma=False,
    )
```

time: 162 us -> 270 us (1.67)
  the two profiles are of different devices: /device:TPU:6 before, /device:TPU:1 now
where the time goes in v2:
time: 270 us; the launch traced here: 267 us
  Pallas kernels  114 us (42%)
  blocking collectives  80.5 us (30%)
  starting transfers between devices  54.8 us (20%)
  waiting for transfers between devices  13.1 us (5%)
  local copies, waits for them, and re-layouts  3.94 us (1%)
    pallas_call x2, Pallas kernels, pack(): call(pack_kernel, payload, [SM] + [ANY] * (3 + len(after)), ANY, [dma((4,...  97.6 us
    all_to_all x1, blocking collectives, body(): got = lax.all_to_all(partial, 'tp', split_axis=0, concat_axis=0, tiled=True)  43.8 us
    all_to_all x1, blocking collectives, body(): lax.all_to_all(expert_out.reshape(experts, CAP, width), 'ep', split_axis=...  36.7 us
    all_to_all x1, starting transfers between devices, body(): lax.all_to_all(outgoing.reshape(experts, CAP, width), 'ep', split_axis=0,...  16.6 us
    ppermute x3, waiting for transfers between devices, body(): lax.ppermute(inner, 'tp', [(i, (i + k) % N_TP) for i in range(N_TP)])  12.1 us
    ppermute x1, starting transfers between devices, body(): v0 = lax.ppermute(u0, 'sec', swap)  11.8 us
    ppermute x3, starting transfers between devices, body(): lax.ppermute(inner, 'tp', [(i, (i + k) % N_TP) for i in range(N_TP)])  9.06 us
    ppermute x1, starting transfers between devices, body(): v1 = lax.ppermute(u1, 'sec', swap)  8.78 us
  transfers between devices with their start and end apart: 8, of which 4 were waited for; matrix products, arithmetic and copies ran while one was open for 0% of the time, Pallas kernels for 20%

profile of v2, /device:TPU:1, one launch (start us, length us, event | category | flops | bytes accessed | tf_op | source)
XLA Modules:
  0.0 266.8 jit_solution(4347560144079208320)
XLA Ops:
  0.0 0.0 copy-start.4
  0.0 0.0 copy-start.5
  0.0 0.0 copy-start.6
  0.0 48.8 %shard_map.102 = bf16[1536,512]{1,0:T(8,128)(2,1)} custom-call(s32[1]{0:T(128)} %bitcast.10.block, bf16[1,2048,256]{2,1,0:T(8,128)(2,1)} %gate.3, bf16[1,2048,256]{2,1,0:T(8,128)(2,1)} %up.3, bf16[1,256,2048]{2,1,0:T(8,128)(2,1)} %down.3), custom_call_target="tpu_custom_call" | custom-call | bytes 3000000 | tf_op jit(solution)/shard_map/pallas_call | solution.py:260
  48.8 6.0 %collective-permute-start = (bf16[1536,512]{1,0:T(8,128)(2,1)}, bf16[1536,512]{1,0:T(8,128)(2,1)}, u32[]{:S(2)}, u32[]{:S(2)}) collective-permute-start(bf16[1536,512]{1,0:T(8,128)(2,1)} %shard_map.102), channel_id=1, source_target_pairs={{0,0},{1,1},{2,256},{3,257},{256,2},{257,3},{258,258},{259,259},{4... | collective-permute-start | bytes 4718600 | tf_op jit(solution)/shard_map/ppermute | solution.py:278
  54.9 0.0 copy-done.4
  54.9 0.0 copy-done.5
  54.9 0.0 copy-done.6
  54.9 0.0 copy-start.7
  54.9 0.9 copy-done.7
  55.8 0.0 copy-start.8
  55.8 0.9 copy-done.8
  56.8 2.9 %shard_map.100 = (bf16[128,1024]{1,0:T(8,128)(2,1)S(1)}, bf16[512,1024]{1,0:T(8,128)(2,1)S(1)}) custom-call(s32[2,128]{1,0:T(2,128)S(1)} %bitcast.19, bf16[128,1024]{1,0:T(8,128)(2,1)S(1)} %copy-done.5, bf16[128,1024]{1,0:T(8,128)(2,1)S(1)} %copy-done.6, bf16[128,1024]{1,0:T(8,128)(2,1)S(1)} %copy-done.7, bf16[128,1024]{1,0:T(8,128)(2,1)S(1)} %copy-done.8), custom_call_target="tpu_custom_call" | custom-call | flops 300000000 | bytes 2500000 | tf_op jit(solution)/shard_map/pallas_call | solution.py:281
  59.7 0.0 copy-start.1
  59.7 1.0 copy-done.1
  60.7 48.8 %shard_map.103 = bf16[1536,512]{1,0:T(8,128)(2,1)} custom-call(s32[1]{0:T(128)S(6)} %sub.20.block, bf16[1,2048,256]{2,1,0:T(8,128)(2,1)} %gate.3, bf16[1,2048,256]{2,1,0:T(8,128)(2,1)} %up.3, bf16[1,256,2048]{2,1,0:T(8,128)(2,1)} %down.3, bf16[512,1024]{1,0:T(8,128)(2,1)} %copy-done.1), custom_call_target="tpu_custom_call" | custom-call | bytes 3000000 | tf_op jit(solution)/shard_map/pallas_call | solution.py:260
  109.5 0.0 copy-start.3
  109.5 2.5 collective-permute-start.1
  112.0 16.6 %all-to-all-start = ((bf16[64,8,1024]{2,1,0:T(8,128)(2,1)}), bf16[64,8,1024]{2,1,0:T(8,128)(2,1)}, u32[]{:S(2)}, u32[]{:S(2)}) async-start(bf16[64,8,1024]{2,1,0:T(8,128)(2,1)} %bitcast.15), calls=%async_computation | async-start | bytes 2097152 | tf_op jit(solution)/shard_map/all_to_all | solution.py:289
  128.6 0.0 collective-permute-done.u0
  128.6 11.8 %collective-permute-start.2 = (bf16[1536,512]{1,0:T(8,128)(2,1)}, bf16[1536,512]{1,0:T(8,128)(2,1)S(1)}, u32[]{:S(2)}, u32[]{:S(2)}) collective-permute-start(bf16[1536,512]{1,0:T(8,128)(2,1)} %collective-permute-done.u0), channel_id=1, source_target_pairs={{0,256},{256,0},{1,257},{257,1},{2,258},{258,2},{3,259},{259,3},{4... | collective-permute-start | bytes 4718600 | tf_op jit(solution)/shard_map/ppermute | solution.py:279
  140.4 0.0 collective-permute-done.1.u1
  140.5 8.8 %collective-permute-start.3 = (bf16[1536,512]{1,0:T(8,128)(2,1)S(1)}, bf16[1536,512]{1,0:T(8,128)(2,1)}, u32[]{:S(2)}, u32[]{:S(2)}) collective-permute-start(bf16[1536,512]{1,0:T(8,128)(2,1)S(1)} %collective-permute-done.1.u1), channel_id=1, source_target_pairs={{0,256},{256,0},{1,257},{257,1},{2,258},{258,2},{3,259},{259,3},{4... | collective-permute-start | bytes 4718600 | tf_op jit(solution)/shard_map/ppermute | solution.py:294
  149.3 0.1 concatenate.3.place
  149.4 0.0 copy-done.3
  149.4 0.0 copy-start.2
  149.4 0.9 copy-done.2
  150.4 1.0 shard_map.101.sums
  151.3 0.0 all-to-all-done
  151.4 0.0 collective-permute-done.2.v0
  151.4 0.0 copy-start
  151.4 1.0 collective-permute-done.3.v1
  152.4 6.6 %shard_map.104 = bf16[4,560,512]{2,1,0:T(8,128)(2,1)} custom-call(s32[5]{0:T(128)S(1)} %concatenate.3.place, bf16[512,1024]{1,0:T(8,128)(2,1)} %bitcast.7.x, f32[1,1024]{1,0:T(1,128)S(1)} %bitcast.18, f32[72,128]{1,0:T(8,128)S(1)} %shard_map.101.sums, bf16[1536,512]{1,0:T(8,128)(2,1)} %collective-permute-done.u0, ...), custom_call_target="tpu_custom_call" | custom-call | flops 2200000000 | bytes 8000000 | tf_op jit(solution)/shard_map/pallas_call | solution.py:302
  159.0 0.0 copy-done
  159.0 43.8 %all_to_all.15.got = bf16[4,560,512]{2,1,0:T(8,128)(2,1)S(1)} all-to-all(bf16[4,560,512]{2,1,0:T(8,128)(2,1)} %shard_map.104), channel_id=1, replica_groups=mesh['sec'=2,'ep'=64,'tp'=4] {'tp'}, dimensions={0} | all-to-all | bytes 4587520 | tf_op jit(solution)/shard_map/all_to_all | solution.py:315
  202.8 0.4 shard_map.105
  203.3 4.7 %collective-permute-start.6 = (bf16[512,256]{1,0:T(8,128)(2,1)S(1)}, bf16[512,256]{1,0:T(8,128)(2,1)S(1)}, u32[]{:S(2)}, u32[]{:S(2)}) collective-permute-start(bf16[512,256]{1,0:T(8,128)(2,1)S(1)} %get-tuple-element.12.i0), channel_id=1, source_target_pairs={{0,3},{1,0},{2,1},{3,2},{4,7},{5,4},{6,5},{7,6},{8,11},{9,8},{10,9... | collective-permute-start | bytes 786440 | tf_op jit(solution)/shard_map/ppermute | solution.py:326
  207.9 1.9 collective-permute-start.5
  209.9 2.5 collective-permute-start.4
  212.3 0.1 collective-permute-done.6.i3
  212.5 4.6 %collective-permute-done.5.i2 = bf16[512,256]{1,0:T(8,128)(2,1)S(1)} collective-permute-done((bf16[512,256]{1,0:T(8,128)(2,1)S(1)}, bf16[512,256]{1,0:T(8,128)(2,1)S(1)}, u32[]{:S(2)}, u32[]{:S(2)}) %collective-permute-start.5) | collective-permute-done | bytes 262176 | tf_op jit(solution)/shard_map/ppermute | solution.py:326
  217.1 7.3 %collective-permute-done.4.i1 = bf16[512,256]{1,0:T(8,128)(2,1)S(1)} collective-permute-done((bf16[512,256]{1,0:T(8,128)(2,1)S(1)}, bf16[512,256]{1,0:T(8,128)(2,1)S(1)}, u32[]{:S(2)}, u32[]{:S(2)}) %collective-permute-start.4) | collective-permute-done | bytes 262176 | tf_op jit(solution)/shard_map/ppermute | solution.py:326
  224.4 4.4 %shard_map.106 = bf16[512,1024]{1,0:T(8,128)(2,1)S(1)} custom-call(s32[1]{0:T(128)} %bitcast.1.flag, bf16[512,256]{1,0:T(8,128)(2,1)S(1)} %get-tuple-element.12.i0, bf16[512,256]{1,0:T(8,128)(2,1)S(1)} %collective-permute-done.4.i1, bf16[512,256]{1,0:T(8,128)(2,1)S(1)} %collective-permute-done.5.i2, bf16[512,256]{1,0:T(8,128)(2,1)S(1)} %collective-permute-done.6.i3, ...), custom_call_target="tpu_custom_call" | custom-call | flops 1100000000 | bytes 4000000 | tf_op jit(solution)/shard_map/pallas_call | solution.py:327
  228.8 36.7 %all_to_all.16 = bf16[64,8,1024]{2,1,0:T(8,128)(2,1)S(1)} all-to-all(bf16[64,8,1024]{2,1,0:T(8,128)(2,1)S(1)} %bitcast.13), channel_id=1, replica_groups=mesh['sec'=2,'ep'=64,'tp'=4] {'ep'}, dimensions={0} | all-to-all | bytes 2097152 | tf_op jit(solution)/shard_map/all_to_all | solution.py:340
  265.5 1.3 shard_map.107
Async XLA Ops:
  0.0 54.9 %copy-start.4 = (s32[128,2]{0,1:T(2,128)S(1)}, s32[128,2]{0,1:T(2,128)}, u32[]{:S(2)}) copy-start(s32[128,2]{0,1:T(2,128)} %param.16) | copy-start | bytes 3076
  0.0 54.9 %copy-start.5 = (bf16[128,1024]{1,0:T(8,128)(2,1)S(1)}, bf16[128,1024]{1,0:T(8,128)(2,1)}, u32[]{:S(2)}) copy-start(bf16[128,1024]{1,0:T(8,128)(2,1)} %refs_1_.1) | copy-start | bytes 786436
  0.0 54.9 %copy-start.6 = (bf16[128,1024]{1,0:T(8,128)(2,1)S(1)}, bf16[128,1024]{1,0:T(8,128)(2,1)}, u32[]{:S(2)}) copy-start(bf16[128,1024]{1,0:T(8,128)(2,1)} %refs_2_.1) | copy-start | bytes 786436
  48.8 79.8 %collective-permute-start = (bf16[1536,512]{1,0:T(8,128)(2,1)}, bf16[1536,512]{1,0:T(8,128)(2,1)}, u32[]{:S(2)}, u32[]{:S(2)}) collective-permute-start(bf16[1536,512]{1,0:T(8,128)(2,1)} %shard_map.102), channel_id=1, source_target_pairs={{0,0},{1,1},{2,256},{3,257},{256,2},{257,3},{258,258},{259,259},{4... | collective-permute-start | bytes 4718600 | tf_op jit(solution)/shard_map/ppermute | solution.py:278
  54.9 1.0 copy-start.7
  55.8 0.9 copy-start.8
  59.7 1.0 copy-start.1
  109.5 39.9 %copy-start.3 = (f32[1024]{0:T(1024)S(1)}, f32[1024]{0:T(1024)}, u32[]{:S(2)}) copy-start(f32[1024]{0:T(1024)} %param.14) | copy-start | bytes 12292
  109.5 30.9 %collective-permute-start.1 = (bf16[1536,512]{1,0:T(8,128)(2,1)}, bf16[1536,512]{1,0:T(8,128)(2,1)S(1)}, u32[]{:S(2)}, u32[]{:S(2)}) collective-permute-start(bf16[1536,512]{1,0:T(8,128)(2,1)} %shard_map.103), channel_id=1, source_target_pairs={{0,1},{1,256},{2,257},{3,0},{256,3},{257,258},{258,259},{259,2},{4... | collective-permute-start | bytes 4718600 | tf_op jit(solution)/shard_map/ppermute | solution.py:293
  112.0 39.4 %all-to-all-start = ((bf16[64,8,1024]{2,1,0:T(8,128)(2,1)}), bf16[64,8,1024]{2,1,0:T(8,128)(2,1)}, u32[]{:S(2)}, u32[]{:S(2)}) async-start(bf16[64,8,1024]{2,1,0:T(8,128)(2,1)} %bitcast.15), calls=%async_computation | async-start | bytes 2097152 | tf_op jit(solution)/shard_map/all_to_all | solution.py:289
  128.6 22.8 %collective-permute-start.2 = (bf16[1536,512]{1,0:T(8,128)(2,1)}, bf16[1536,512]{1,0:T(8,128)(2,1)S(1)}, u32[]{:S(2)}, u32[]{:S(2)}) collective-permute-start(bf16[1536,512]{1,0:T(8,128)(2,1)} %collective-permute-done.u0), channel_id=1, source_target_pairs={{0,256},{256,0},{1,257},{257,1},{2,258},{258,2},{3,259},{259,3},{4... | collective-permute-start | bytes 4718600 | tf_op jit(solution)/shard_map/ppermute | solution.py:279
  140.5 11.9 %collective-permute-start.3 = (bf16[1536,512]{1,0:T(8,128)(2,1)S(1)}, bf16[1536,512]{1,0:T(8,128)(2,1)}, u32[]{:S(2)}, u32[]{:S(2)}) collective-permute-start(bf16[1536,512]{1,0:T(8,128)(2,1)S(1)} %collective-permute-done.1.u1), channel_id=1, source_target_pairs={{0,256},{256,0},{1,257},{257,1},{2,258},{258,2},{3,259},{259,3},{4... | collective-permute-start | bytes 4718600 | tf_op jit(solution)/shard_map/ppermute | solution.py:294
  149.4 1.0 copy-start.2
  151.4 7.6 %copy-start = (bf16[1536,512]{1,0:T(8,128)(2,1)}, bf16[1536,512]{1,0:T(8,128)(2,1)S(1)}, u32[]{:S(2)}) copy-start(bf16[1536,512]{1,0:T(8,128)(2,1)S(1)} %collective-permute-done.2.v0) | copy-start | bytes 4718596
  203.3 9.2 %collective-permute-start.6 = (bf16[512,256]{1,0:T(8,128)(2,1)S(1)}, bf16[512,256]{1,0:T(8,128)(2,1)S(1)}, u32[]{:S(2)}, u32[]{:S(2)}) collective-permute-start(bf16[512,256]{1,0:T(8,128)(2,1)S(1)} %get-tuple-element.12.i0), channel_id=1, source_target_pairs={{0,3},{1,0},{2,1},{3,2},{4,7},{5,4},{6,5},{7,6},{8,11},{9,8},{10,9... | collective-permute-start | bytes 786440 | tf_op jit(solution)/shard_map/ppermute | solution.py:326
  207.9 9.2 %collective-permute-start.5 = (bf16[512,256]{1,0:T(8,128)(2,1)S(1)}, bf16[512,256]{1,0:T(8,128)(2,1)S(1)}, u32[]{:S(2)}, u32[]{:S(2)}) collective-permute-start(bf16[512,256]{1,0:T(8,128)(2,1)S(1)} %get-tuple-element.12.i0), channel_id=1, source_target_pairs={{0,2},{1,3},{2,0},{3,1},{4,6},{5,7},{6,4},{7,5},{8,10},{9,11},{10,... | collective-permute-start | bytes 786440 | tf_op jit(solution)/shard_map/ppermute | solution.py:326
  209.9 14.6 %collective-permute-start.4 = (bf16[512,256]{1,0:T(8,128)(2,1)S(1)}, bf16[512,256]{1,0:T(8,128)(2,1)S(1)}, u32[]{:S(2)}, u32[]{:S(2)}) collective-permute-start(bf16[512,256]{1,0:T(8,128)(2,1)S(1)} %get-tuple-element.12.i0), channel_id=1, source_target_pairs={{0,1},{1,2},{2,3},{3,0},{4,5},{5,6},{6,7},{7,4},{8,9},{9,10},{10,1... | collective-permute-start | bytes 786440 | tf_op jit(solution)/shard_map/ppermute | solution.py:326

commit v3 on v2

v3 whole, which is shorter than its diff:
```python
import math

import jax
import jax.numpy as jnp
from jax import lax
from jax.experimental import pallas as pl
from jax.experimental.pallas import tpu as pltpu
from jax.sharding import PartitionSpec as P

D = 4096
HEAD_DIM = 128
CAP = 8
N_TP = 4
EPS = 1e-06

BF = jnp.bfloat16
F32 = jnp.float32
HIGHEST = lax.Precision.HIGHEST
VMEM_BYTES = 28 * 1024 * 1024
WHOLE_VMEM = 63 * 1024 * 1024


def call(kernel, out_shape, in_specs, out_specs, scratch=(), cost=(0, 0), vmem=VMEM_BYTES):
    return pl.pallas_call(
        kernel,
        out_shape=out_shape,
        in_specs=in_specs,
        out_specs=out_specs,
        scratch_shapes=scratch,
        cost_estimate=pl.CostEstimate(flops=cost[0], bytes_accessed=cost[1], transcendentals=0),
        compiler_params=pltpu.CompilerParams(vmem_limit_bytes=vmem),
    )


VM = pl.BlockSpec(memory_space=pltpu.VMEM)
ANY = pl.BlockSpec(memory_space=pl.ANY)
SM = pl.BlockSpec(memory_space=pltpu.SMEM)


def struct(shape, dtype):
    return jax.ShapeDtypeStruct(shape, dtype)


def nt(a, b, precision=None):
    return lax.dot_general(
        a, b, (((1,), (1,)), ((), ())), precision=precision, preferred_element_type=F32
    )


def pack_copies(base, gate, up, down, out, sems):
    width, span = gate.shape[2], down.shape[2] // 2
    rows = pl.ds(base, span)
    pairs = [
        (gate.at[0, rows, :], out.at[pl.ds(0, span), pl.ds(0, width)]),
        (up.at[0, rows, :], out.at[pl.ds(0, span), pl.ds(width, width)]),
    ]
    for j in range(2):
        cols = pl.ds(pl.multiple_of(base + j * 2 * width, 2 * width), 2 * width)
        pairs.append((down.at[0, :, cols], out.at[pl.ds(span + j * width, width), :]))
    return [pltpu.make_async_copy(src, dst, sems.at[n]) for n, (src, dst) in enumerate(pairs)]


def slots_of(ids_ref, experts):
    tokens = ids_ref.shape[1]
    expert = lax.broadcasted_iota(jnp.int32, (experts, tokens), 0)
    named = (ids_ref[0:1, :] == expert) | (ids_ref[1:2, :] == expert)
    before = lax.broadcasted_iota(jnp.int32, (tokens, tokens), 0) < lax.broadcasted_iota(
        jnp.int32, (tokens, tokens), 1
    )
    rank = jnp.dot(named.astype(BF), before.astype(BF), preferred_element_type=F32)
    return named, jnp.where(named, rank, -1.0)


def spread(slot, value):
    experts, tokens = slot.shape
    turn = lax.broadcasted_iota(jnp.int32, (experts, CAP, tokens), 1).astype(F32)
    hit = slot[:, None, :] == turn
    return jnp.where(hit, value[:, None, :], 0.0).reshape(experts * CAP, tokens)


def front_kernel(experts, parity, ids, q_, k_, v_, resid_, gate, up, down,
                 hidden_, outgoing, first, second,
                 q, k, v, resid, hidden, rows, pack, sems, pack_sems, out_sems):
    tokens, width = q.shape
    loads = [
        pltpu.make_async_copy(src, dst, sems.at[n])
        for n, (src, dst) in enumerate(((q_, q), (k_, k), (v_, v), (resid_, resid)))
    ]
    loads_pack = []
    for turn in range(2):
        block = parity[0] if turn == 0 else 1 - parity[0]
        base = pl.multiple_of(block * (down.shape[2] // 2), down.shape[2] // 2)
        loads_pack.append(pack_copies(base, gate, up, down, pack.at[turn], pack_sems.at[turn]))
    for copy in loads + loads_pack[0] + loads_pack[1]:
        copy.start()
    scale = 1.0 / math.sqrt(HEAD_DIM)
    _, slot = slots_of(ids, experts)
    pick = spread(slot, jnp.ones_like(slot)).astype(BF)
    for copy in loads:
        copy.wait()
    stores = []

    def store(src, dst):
        stores.append(pltpu.make_async_copy(src, dst, out_sems.at[len(stores)]))
        stores[-1].start()

    for n in range(width // HEAD_DIM):
        cols = slice(n * HEAD_DIM, (n + 1) * HEAD_DIM)
        scores = nt(q[:, cols], k[:, cols]) * scale
        top = jnp.max(scores, axis=1, keepdims=True)
        e = jnp.exp(scores - top)
        weights = (e / jnp.sum(e, axis=1, keepdims=True)).astype(BF)
        attended = jnp.dot(weights, v[:, cols], preferred_element_type=F32)
        h = (resid[:, cols].astype(F32) + attended).astype(BF)
        hidden[:, cols] = h
        rows[:, cols] = jnp.dot(pick, h, preferred_element_type=F32).astype(BF)
        if n % 2 == 1:
            pair = pl.ds((n - 1) * HEAD_DIM, 2 * HEAD_DIM)
            store(rows.at[:, pair], outgoing.at[:, pair])
        if n in (2, 5):
            turn = n // 3
            for copy in loads_pack[turn]:
                copy.wait()
            store(pack.at[turn], (first, second)[turn])
    store(hidden, hidden_)
    for copy in stores:
        copy.wait()


def router_kernel(hidden, gain, router, out):
    h = hidden[...].astype(F32)
    experts = router.shape[0]
    out[0:experts, :] = nt(router[...], h * gain[...], HIGHEST)
    out[experts : experts + 8, :] = nt(jnp.ones((8, h.shape[1]), F32), h * h, HIGHEST)


def split(value):
    high = value.astype(BF)
    return high, (value - high.astype(F32)).astype(BF)


def up_kernel(place, x, gain, sums, u0, u1, v0, v1, after, out, weights, sems):
    rows, depth = x.shape
    loads = [
        pltpu.make_async_copy(ref.at[pl.ds(0, depth), :], weights.at[n], sems.at[n])
        for n, ref in enumerate((u0, u1, v0, v1))
    ]
    for copy in loads:
        copy.start()
    xf = x[...].astype(F32)
    xg = (xf * gain[...]).astype(BF)
    high, low = split(xf * xf)
    ones = jnp.ones((8, depth), BF)
    total = nt(ones, high) + nt(ones, low)
    experts = sums.shape[0] - 8
    tokens = jnp.concatenate([sums[experts : experts + 8, :]] * 4, axis=1)
    tile = lax.broadcasted_iota(jnp.int32, total.shape, 0)
    squares = jnp.concatenate(split(jnp.where(tile < 4, total, tokens)), axis=0)
    half = experts // 2
    parts = split(sums[0:experts, :])
    logits = jnp.concatenate(
        [part[i * half : (i + 1) * half, :] for part in parts for i in range(2)], axis=1
    )
    for n in range(N_TP):
        target = place[n]
        loads[n].wait()
        out[target, 0:rows, :] = jnp.dot(xg, weights[n], preferred_element_type=F32).astype(BF)
        out[target, rows : rows + 16, :] = squares
        out[target, rows + 16 : rows + 16 + half, :] = logits


def inner_kernel(got, inner, sums):
    rows, width = inner.shape[1:]
    half = sums.shape[0] // 2 - 4
    total = got[0, 0:rows, :].astype(F32)
    tail = got[0, rows:, :].astype(F32)
    for n in range(1, N_TP):
        total = total + got[n, 0:rows, :].astype(F32)
        tail = tail + got[n, rows:, :].astype(F32)
    square = tail[0:8, :] + tail[8:16, :]
    logits = tail[16 : 16 + half, :]
    logits = logits[:, 0:256] + logits[:, 256:512]
    sums[0:half, :] = logits[:, 0:128]
    sums[half : 2 * half, :] = logits[:, 128:256]
    sums[2 * half : 2 * half + 8, :] = jnp.broadcast_to(square[4:5, 0:128], (8, 128))
    inv = lax.rsqrt(square[0:1, :] / D + EPS)
    for j in range(rows // 128):
        part = slice(j * 128, (j + 1) * 128)
        column = jnp.transpose(jnp.broadcast_to(inv[:, part], (128, 128)), (1, 0))
        column = jnp.concatenate([column] * (width // 128), axis=1)
        gate = total[part, 0:width] * column
        up = total[part, width : 2 * width] * column
        act = (gate * (1.0 / (1.0 + jnp.exp(-gate))) * up).astype(BF)
        for n in range(N_TP):
            inner[n, part, :] = act


def down_kernel(place, inners, u0, u1, v0, v1, out, weights, sems):
    width, span = inners.shape[2], out.shape[1]
    loads = [
        pltpu.make_async_copy(ref.at[pl.ds(span, 2 * width), :], weights.at[n], sems.at[n])
        for n, ref in enumerate((u0, u1, v0, v1))
    ]
    for copy in loads:
        copy.start()
    parts = [inners[place[n]] for n in range(N_TP)]
    for copy in loads:
        copy.wait()
    for j in range(2):
        total = jnp.zeros((out.shape[0], 2 * width), F32)
        for n, part in enumerate(parts):
            rows = weights[n, j * width : (j + 1) * width, :]
            total += jnp.dot(part, rows, preferred_element_type=F32)
        out[:, j * 2 * width : (j + 1) * 2 * width] = total.astype(BF)


def mix_kernel(ids, sums, hidden, returned, out):
    experts = sums.shape[0] - 8
    named, slot = slots_of(ids, experts)
    inv = lax.rsqrt(sums[experts : experts + 1, :] / D + EPS)
    logits = sums[0:experts, :] * inv
    picked = jnp.where(named, 1.0 / (1.0 + jnp.exp(-logits)), 0.0)
    share = picked / jnp.sum(picked, axis=0, keepdims=True)
    wide = spread(slot, share)
    high = wide.astype(BF)
    low = (wide - high.astype(F32)).astype(BF)
    rows = returned[...]
    dims = (((0,), (0,)), ((), ()))
    mixed = lax.dot_general(high, rows, dims, preferred_element_type=F32)
    mixed += lax.dot_general(low, rows, dims, preferred_element_type=F32)
    out[...] = (hidden[...].astype(F32) + mixed).astype(BF)


def body(resid, queries, keys, values, norm_gain, w_router, expert_ids, w_gate, w_up, w_down):
    tokens, width = resid.shape
    experts = lax.axis_size("ep")
    slots = experts * CAP
    units = w_gate.shape[2]
    sec, tp = lax.axis_index("sec"), lax.axis_index("tp")
    parity = (tp % 2).astype(jnp.int32).reshape(1)
    ids = expert_ids.T
    gain = norm_gain.reshape(1, width)

    dma = pltpu.SemaphoreType.DMA
    payload = struct((width + 2 * units, 2 * units), BF)
    hidden, outgoing, first, second = call(
        lambda *refs: front_kernel(experts, *refs),
        [struct((tokens, width), BF), struct((slots, width), BF), payload, payload],
        [SM, VM] + [ANY] * 7,
        [ANY] * 4,
        [pltpu.VMEM((tokens, width), BF)] * 5
        + [pltpu.VMEM((slots, width), BF), pltpu.VMEM((2,) + payload.shape, BF)]
        + [dma((4,)), dma((2, 4)), dma((7,))],
        (300_000_000, 8_500_000),
        WHOLE_VMEM,
    )(parity, ids, queries, keys, values, resid, w_gate, w_up, w_down)

    stay, turn = [], []
    for s in range(2):
        for t in range(N_TP):
            here = s * N_TP + t
            if s == t // 2:
                stay.append((here, here))
            else:
                stay.append((here, (1 - s) * N_TP + (t + 2) % N_TP))
            if s == ((t + 1) % N_TP) // 2:
                turn.append((here, s * N_TP + (t + 1) % N_TP))
            else:
                turn.append((here, (1 - s) * N_TP + (t + 3) % N_TP))
    swap = [(0, 1), (1, 0)]
    u0 = lax.ppermute(first, ("sec", "tp"), stay)
    u1 = lax.ppermute(second, ("sec", "tp"), turn)
    weights = [u0, u1, lax.ppermute(u0, "sec", swap), lax.ppermute(u1, "sec", swap)]
    base = jnp.where(sec == tp // 2, tp, tp + 2)
    place = jnp.stack([(base - n) % N_TP for n in range(N_TP)]).astype(jnp.int32)

    arrived = lax.all_to_all(
        outgoing.reshape(experts, CAP, width), "ep", split_axis=0, concat_axis=0, tiled=True
    ).reshape(slots, width)

    sums = call(
        router_kernel, struct((experts + 8, tokens), F32), [VM] * 3, VM, (), (150_000_000, 600_000)
    )(hidden, gain, w_router.T)

    pairs = [(experts + i, experts + i // 8 * 8 + (i + 1) % 8) for i in range(experts)]
    after = lax.ppermute(arrived, ("sec", "ep"), pairs)
    message = struct((N_TP, slots + 16 + experts // 2, 2 * units), BF)
    partial = call(
        up_kernel,
        message,
        [SM] + [VM] * 3 + [ANY] * 5,
        VM,
        [pltpu.VMEM((N_TP, width, 2 * units), BF), dma((N_TP,))],
        (2_200_000_000, 8_000_000),
    )(place, arrived, gain, sums, *weights, after)
    got = lax.all_to_all(partial, "tp", split_axis=0, concat_axis=0, tiled=True)
    inner, sums = call(
        inner_kernel,
        [struct((N_TP, slots, units), BF), struct((experts + 8, tokens), F32)],
        [VM],
        [VM, VM],
        (),
        (1_000_000, 2_500_000),
    )(got)
    inners = lax.all_to_all(inner, "tp", split_axis=0, concat_axis=0, tiled=True)
    expert_out = call(
        down_kernel,
        struct((slots, width), BF),
        [SM, VM] + [ANY] * 4,
        VM,
        [pltpu.VMEM((N_TP, 2 * units, 2 * units), BF), dma((N_TP,))],
        (1_100_000_000, 4_000_000),
    )(place, inners, *weights)
    returned = lax.all_to_all(
        expert_out.reshape(experts, CAP, width), "ep", split_axis=0, concat_axis=0, tiled=True
    ).reshape(slots, width)
    return call(mix_kernel, struct((tokens, width), BF), [VM] * 4, VM)(ids, sums, hidden, returned)


def solution(mesh):
    rows, cols = P(("sec", "ep"), "tp"), P(("sec", "ep"), None)
    return jax.shard_map(
        body,
        mesh=mesh,
        in_specs=(
            rows,
            rows,
            rows,
            rows,
            P("tp"),
            P("tp", None),
            cols,
            P("ep", "sec", "tp"),
            P("ep", "sec", "tp"),
            P("ep", "tp", "sec"),
        ),
        out_specs=rows,
        check_vma=False,
    )
```

time: 270 us -> 152 us (0.56); the launches traced: 267 us -> 152 us
  Pallas kernels: 114 us -> 17.7 us
  waiting for transfers between devices: 13.1 us -> 34.2 us
  starting transfers between devices: 54.8 us -> 35 us
  blocking collectives: 80.5 us -> 63.6 us
  local copies, waits for them, and re-layouts: 3.94 us -> 0.96 us
    pallas_call x6 -> x4, Pallas kernels: 112 us -> 15.3 us  [the longest x1 6.7 us: body(): call(lambda *refs: front_kernel(experts, *refs), [struct((tokens, width),...]
    all_to_all x1, blocking collectives: 43.8 us -> 23.3 us  [body(): got = lax.all_to_all(partial, 'tp', split_axis=0, concat_axis=0, tiled=True)]
    ppermute x7 -> x5, starting transfers between devices: 38.2 us -> 18.4 us  [the longest x1 6.17 us: body(): u0 = lax.ppermute(first, ('sec', 'tp'), stay)]
    ppermute x7 -> x5, waiting for transfers between devices: 13.1 us -> 26.7 us  [the longest x1 14.3 us: body(): u0 = lax.ppermute(first, ('sec', 'tp'), stay)]
    all_to_all x0 -> x1, blocking collectives: none -> 12.2 us  [body(): lax.all_to_all(inner, 'tp', split_axis=0, concat_axis=0, tiled=True)]
    all_to_all x1, blocking collectives: 36.7 us -> 28.1 us  [body(): lax.all_to_all(expert_out.reshape(experts, CAP, width), 'ep', split_axis=...]
    all_to_all x1, waiting for transfers between devices: 0.02 us -> 7.45 us  [body(): lax.all_to_all(outgoing.reshape(experts, CAP, width), 'ep', split_axis=0,...]
    unnamed x18 -> x8, local copies, waits for them, and re-layouts: 3.85 us -> 0.96 us
  transfers between devices with their start and end apart: 8 -> 6, of which waited for: 4 -> 4; matrix products, arithmetic and copies ran while one was open for 0% -> 0% of each run, Pallas kernels for 20% -> 1%
where the time goes in v3:
time: 152 us
  blocking collectives  63.6 us (42%)
  starting transfers between devices  35 us (23%)
  waiting for transfers between devices  34.2 us (23%)
  Pallas kernels  17.7 us (12%)
    all_to_all x1, blocking collectives, body(): lax.all_to_all(expert_out.reshape(experts, CAP, width), 'ep', split_axis=...  28.1 us
    all_to_all x1, blocking collectives, body(): got = lax.all_to_all(partial, 'tp', split_axis=0, concat_axis=0, tiled=True)  23.3 us
    all_to_all x1, starting transfers between devices, body(): lax.all_to_all(outgoing.reshape(experts, CAP, width), 'ep', split_axis=0,...  16.6 us
    ppermute x1, waiting for transfers between devices, body(): u0 = lax.ppermute(first, ('sec', 'tp'), stay)  14.3 us
    ppermute x1, waiting for transfers between devices, body(): after = lax.ppermute(arrived, ('sec', 'ep'), pairs)  12.2 us
    all_to_all x1, blocking collectives, body(): lax.all_to_all(inner, 'tp', split_axis=0, concat_axis=0, tiled=True)  12.2 us
    all_to_all x1, waiting for transfers between devices, body(): lax.all_to_all(outgoing.reshape(experts, CAP, width), 'ep', split_axis=0,...  7.45 us
    pallas_call x1, Pallas kernels, body(): call(lambda *refs: front_kernel(experts, *refs), [struct((tokens, width),...  6.7 us
  transfers between devices with their start and end apart: 6, of which 4 were waited for; matrix products, arithmetic and copies ran while one was open for 0% of the time, Pallas kernels for 1%

profile of v3, /device:TPU:1, one launch (start us, length us, event | category | flops | bytes accessed | tf_op | source)
XLA Modules:
  0.0 151.7 jit_solution(13423497733847306995)
XLA Ops:
  0.0 6.7 %shard_map.100 = (bf16[128,1024]{1,0:T(8,128)(2,1)}, bf16[512,1024]{1,0:T(8,128)(2,1)}, bf16[1536,512]{1,0:T(8,128)(2,1)}, bf16[1536,512]{1,0:T(8,128)(2,1)}) custom-call(s32[1]{0:T(128)} %bitcast.5.refs_0_, s32[2,128]{1,0:T(2,128)} %bitcast.17, bf16[128,1024]{1,0:T(8,128)(2,1)} %refs_2_.1, bf16[128,1024]{1,0:T(8,128)(2,1)} %refs_3_.1, ...), custom_call_target="tpu_custom_call" | custom-call | flops 300000000 | bytes 8500000 | tf_op jit(solution)/shard_map/pallas_call | solution.py:246
  6.7 0.0 copy-start
  6.7 0.0 copy-start.2
  6.7 6.2 %collective-permute-start = (bf16[1536,512]{1,0:T(8,128)(2,1)}, bf16[1536,512]{1,0:T(8,128)(2,1)S(1)}, u32[]{:S(2)}, u32[]{:S(2)}) collective-permute-start(bf16[1536,512]{1,0:T(8,128)(2,1)} %get-tuple-element.13), channel_id=1, source_target_pairs={{0,0},{1,1},{2,256},{3,257},{256,2},{257,3},{258,258},{259,259},{4... | collective-permute-start | bytes 4718600 | tf_op jit(solution)/shard_map/ppermute | solution.py:271
  12.9 2.5 %collective-permute-start.1 = (bf16[1536,512]{1,0:T(8,128)(2,1)}, bf16[1536,512]{1,0:T(8,128)(2,1)S(1)}, u32[]{:S(2)}, u32[]{:S(2)}) collective-permute-start(bf16[1536,512]{1,0:T(8,128)(2,1)} %get-tuple-element.14), channel_id=1, source_target_pairs={{0,1},{1,256},{2,257},{3,0},{256,3},{257,258},{258,259},{259,2},{4... | collective-permute-start | bytes 4718600 | tf_op jit(solution)/shard_map/ppermute | solution.py:272
  15.4 16.6 %all-to-all-start = ((bf16[64,8,1024]{2,1,0:T(8,128)(2,1)}), bf16[64,8,1024]{2,1,0:T(8,128)(2,1)}, u32[]{:S(2)}, u32[]{:S(2)}) async-start(bf16[64,8,1024]{2,1,0:T(8,128)(2,1)} %bitcast.19), calls=%async_computation | async-start | bytes 2097152 | tf_op jit(solution)/shard_map/all_to_all | solution.py:277
  32.0 14.3 %collective-permute-done.u0 = bf16[1536,512]{1,0:T(8,128)(2,1)S(1)} collective-permute-done((bf16[1536,512]{1,0:T(8,128)(2,1)}, bf16[1536,512]{1,0:T(8,128)(2,1)S(1)}, u32[]{:S(2)}, u32[]{:S(2)}) %collective-permute-start) | collective-permute-done | bytes 1572896 | tf_op jit(solution)/shard_map/ppermute | solution.py:271
  46.3 1.9 %collective-permute-start.2 = (bf16[1536,512]{1,0:T(8,128)(2,1)S(1)}, bf16[1536,512]{1,0:T(8,128)(2,1)}, u32[]{:S(2)}, u32[]{:S(2)}) collective-permute-start(bf16[1536,512]{1,0:T(8,128)(2,1)S(1)} %collective-permute-done.u0), channel_id=1, source_target_pairs={{0,256},{256,0},{1,257},{257,1},{2,258},{258,2},{3,259},{259,3},{4... | collective-permute-start | bytes 4718600 | tf_op jit(solution)/shard_map/ppermute | solution.py:273
  48.2 0.3 collective-permute-done.1.u1
  48.5 4.9 %collective-permute-start.3 = (bf16[1536,512]{1,0:T(8,128)(2,1)S(1)}, bf16[1536,512]{1,0:T(8,128)(2,1)}, u32[]{:S(2)}, u32[]{:S(2)}) collective-permute-start(bf16[1536,512]{1,0:T(8,128)(2,1)S(1)} %collective-permute-done.1.u1), channel_id=1, source_target_pairs={{0,256},{256,0},{1,257},{257,1},{2,258},{258,2},{3,259},{259,3},{4... | collective-permute-start | bytes 4718600 | tf_op jit(solution)/shard_map/ppermute | solution.py:273
  53.4 7.4 %all-to-all-done = bf16[64,8,1024]{2,1,0:T(8,128)(2,1)} async-done(((bf16[64,8,1024]{2,1,0:T(8,128)(2,1)}), bf16[64,8,1024]{2,1,0:T(8,128)(2,1)}, u32[]{:S(2)}, u32[]{:S(2)}) %all-to-all-start) | async-done | bytes 1048608 | tf_op jit(solution)/shard_map/all_to_all | solution.py:277
  60.8 2.9 %collective-permute-start.4 = (bf16[512,1024]{1,0:T(8,128)(2,1)}, bf16[512,1024]{1,0:T(8,128)(2,1)}, u32[]{:S(2)}, u32[]{:S(2)}) collective-permute-start(bf16[512,1024]{1,0:T(8,128)(2,1)} %bitcast.7.x), channel_id=1, source_target_pairs={{256,260},{260,264},{264,268},{268,272},{272,276},{276,280},{280,2... | collective-permute-start | bytes 3145736 | tf_op jit(solution)/shard_map/ppermute | solution.py:286
  63.8 0.0 copy-done
  63.9 0.0 copy-done.2
  63.9 0.0 copy-start.1
  63.9 0.9 copy-done.1
  64.8 1.0 shard_map.101.sums
  65.8 0.1 pad_add_fusion.place
  65.9 12.2 %collective-permute-done.4.after = bf16[512,1024]{1,0:T(8,128)(2,1)} collective-permute-done((bf16[512,1024]{1,0:T(8,128)(2,1)}, bf16[512,1024]{1,0:T(8,128)(2,1)}, u32[]{:S(2)}, u32[]{:S(2)}) %collective-permute-start.4) | collective-permute-done | bytes 1048608 | tf_op jit(solution)/shard_map/ppermute | solution.py:286
  78.1 0.0 collective-permute-done.2.v0
  78.1 0.0 collective-permute-done.3.v1
  78.1 5.1 %shard_map.102 = bf16[4,560,512]{2,1,0:T(8,128)(2,1)S(1)} custom-call(s32[4]{0:T(128)S(1)} %pad_add_fusion.place, bf16[512,1024]{1,0:T(8,128)(2,1)} %bitcast.7.x, f32[1,1024]{1,0:T(1,128)S(1)} %bitcast.16, f32[72,128]{1,0:T(8,128)S(1)} %shard_map.101.sums, bf16[1536,512]{1,0:T(8,128)(2,1)S(1)} %collective-permute-done.u0, ...), custom_call_target="tpu_custom_call" | custom-call | flops 2200000000 | bytes 8000000 | tf_op jit(solution)/shard_map/pallas_call | solution.py:288
  83.2 23.3 %all_to_all.20.got = bf16[4,560,512]{2,1,0:T(8,128)(2,1)S(1)} all-to-all(bf16[4,560,512]{2,1,0:T(8,128)(2,1)S(1)} %shard_map.102), channel_id=1, replica_groups=mesh['sec'=2,'ep'=64,'tp'=4] {'tp'}, dimensions={0} | all-to-all | bytes 4587520 | tf_op jit(solution)/shard_map/all_to_all | solution.py:296
  106.5 0.4 shard_map.103
  106.9 12.2 %all_to_all.21.inners = bf16[4,512,256]{2,1,0:T(8,128)(2,1)S(1)} all-to-all(bf16[4,512,256]{2,1,0:T(8,128)(2,1)S(1)} %get-tuple-element.16), channel_id=1, replica_groups=mesh['sec'=2,'ep'=64,'tp'=4] {'tp'}, dimensions={0} | all-to-all | bytes 2097152 | tf_op jit(solution)/shard_map/all_to_all | solution.py:305
  119.1 3.1 %shard_map.104 = bf16[512,1024]{1,0:T(8,128)(2,1)S(1)} custom-call(s32[4]{0:T(128)S(1)} %pad_add_fusion.place, bf16[4,512,256]{2,1,0:T(8,128)(2,1)S(1)} %all_to_all.21.inners, bf16[1536,512]{1,0:T(8,128)(2,1)S(1)} %collective-permute-done.u0, bf16[1536,512]{1,0:T(8,128)(2,1)S(1)} %collective-permute-done.1.u1, bf16[1536,512]{1,0:T(8,128)(2,1)} %collective-permute-done.2.v0, ...), custom_call_target="tpu_custom_call" | custom-call | flops 1100000000 | bytes 4000000 | tf_op jit(solution)/shard_map/pallas_call | solution.py:306
  122.2 0.0 copy-start.3
  122.2 28.1 %all_to_all.22 = bf16[64,8,1024]{2,1,0:T(8,128)(2,1)S(1)} all-to-all(bf16[64,8,1024]{2,1,0:T(8,128)(2,1)S(1)} %bitcast.12), channel_id=1, replica_groups=mesh['sec'=2,'ep'=64,'tp'=4] {'ep'}, dimensions={0} | all-to-all | bytes 2097152 | tf_op jit(solution)/shard_map/all_to_all | solution.py:314
  150.3 0.0 copy-done.3
  150.3 1.3 shard_map.105
Async XLA Ops:
  6.7 57.1 %copy-start = (bf16[128,1024]{1,0:T(8,128)(2,1)S(1)}, bf16[128,1024]{1,0:T(8,128)(2,1)}, u32[]{:S(2)}) copy-start(bf16[128,1024]{1,0:T(8,128)(2,1)} %get-tuple-element.12.hidden) | copy-start | bytes 786436
  6.7 57.1 %copy-start.2 = (f32[1024]{0:T(1024)S(1)}, f32[1024]{0:T(1024)}, u32[]{:S(2)}) copy-start(f32[1024]{0:T(1024)} %param.14) | copy-start | bytes 12292
  6.7 39.6 %collective-permute-start = (bf16[1536,512]{1,0:T(8,128)(2,1)}, bf16[1536,512]{1,0:T(8,128)(2,1)S(1)}, u32[]{:S(2)}, u32[]{:S(2)}) collective-permute-start(bf16[1536,512]{1,0:T(8,128)(2,1)} %get-tuple-element.13), channel_id=1, source_target_pairs={{0,0},{1,1},{2,256},{3,257},{256,2},{257,3},{258,258},{259,259},{4... | collective-permute-start | bytes 4718600 | tf_op jit(solution)/shard_map/ppermute | solution.py:271
  12.9 35.6 %collective-permute-start.1 = (bf16[1536,512]{1,0:T(8,128)(2,1)}, bf16[1536,512]{1,0:T(8,128)(2,1)S(1)}, u32[]{:S(2)}, u32[]{:S(2)}) collective-permute-start(bf16[1536,512]{1,0:T(8,128)(2,1)} %get-tuple-element.14), channel_id=1, source_target_pairs={{0,1},{1,256},{2,257},{3,0},{256,3},{257,258},{258,259},{259,2},{4... | collective-permute-start | bytes 4718600 | tf_op jit(solution)/shard_map/ppermute | solution.py:272
  15.4 45.4 %all-to-all-start = ((bf16[64,8,1024]{2,1,0:T(8,128)(2,1)}), bf16[64,8,1024]{2,1,0:T(8,128)(2,1)}, u32[]{:S(2)}, u32[]{:S(2)}) async-start(bf16[64,8,1024]{2,1,0:T(8,128)(2,1)} %bitcast.19), calls=%async_computation | async-start | bytes 2097152 | tf_op jit(solution)/shard_map/all_to_all | solution.py:277
  46.3 31.8 %collective-permute-start.2 = (bf16[1536,512]{1,0:T(8,128)(2,1)S(1)}, bf16[1536,512]{1,0:T(8,128)(2,1)}, u32[]{:S(2)}, u32[]{:S(2)}) collective-permute-start(bf16[1536,512]{1,0:T(8,128)(2,1)S(1)} %collective-permute-done.u0), channel_id=1, source_target_pairs={{0,256},{256,0},{1,257},{257,1},{2,258},{258,2},{3,259},{259,3},{4... | collective-permute-start | bytes 4718600 | tf_op jit(solution)/shard_map/ppermute | solution.py:273
  48.5 29.6 %collective-permute-start.3 = (bf16[1536,512]{1,0:T(8,128)(2,1)S(1)}, bf16[1536,512]{1,0:T(8,128)(2,1)}, u32[]{:S(2)}, u32[]{:S(2)}) collective-permute-start(bf16[1536,512]{1,0:T(8,128)(2,1)S(1)} %collective-permute-done.1.u1), channel_id=1, source_target_pairs={{0,256},{256,0},{1,257},{257,1},{2,258},{258,2},{3,259},{259,3},{4... | collective-permute-start | bytes 4718600 | tf_op jit(solution)/shard_map/ppermute | solution.py:273
  60.8 17.2 %collective-permute-start.4 = (bf16[512,1024]{1,0:T(8,128)(2,1)}, bf16[512,1024]{1,0:T(8,128)(2,1)}, u32[]{:S(2)}, u32[]{:S(2)}) collective-permute-start(bf16[512,1024]{1,0:T(8,128)(2,1)} %bitcast.7.x), channel_id=1, source_target_pairs={{256,260},{260,264},{264,268},{268,272},{272,276},{276,280},{280,2... | collective-permute-start | bytes 3145736 | tf_op jit(solution)/shard_map/ppermute | solution.py:286
  63.9 1.0 copy-start.1
  122.2 28.1 %copy-start.3 = (s32[128,2]{0,1:T(2,128)S(1)}, s32[128,2]{0,1:T(2,128)}, u32[]{:S(2)}) copy-start(s32[128,2]{0,1:T(2,128)} %param.16) | copy-start | bytes 3076

commit v4 on v3

--- a/solution.py
+++ b/solution.py
@@ -20,13 +20,16 @@
 WHOLE_VMEM = 63 * 1024 * 1024
 
 
-def call(kernel, out_shape, in_specs, out_specs, scratch=(), cost=(0, 0), vmem=VMEM_BYTES):
+def call(
+    kernel, out_shape, in_specs, out_specs, scratch=(), cost=(0, 0), vmem=VMEM_BYTES, aliases=None
+):
     return pl.pallas_call(
         kernel,
         out_shape=out_shape,
         in_specs=in_specs,
         out_specs=out_specs,
         scratch_shapes=scratch,
+        input_output_aliases=aliases or {},
         cost_estimate=pl.CostEstimate(flops=cost[0], bytes_accessed=cost[1], transcendentals=0),
         compiler_params=pltpu.CompilerParams(vmem_limit_bytes=vmem),
     )
@@ -78,20 +81,33 @@
     return jnp.where(hit, value[:, None, :], 0.0).reshape(experts * CAP, tokens)
 
 
-def front_kernel(experts, parity, ids, q_, k_, v_, resid_, gate, up, down,
-                 hidden_, outgoing, first, second,
-                 q, k, v, resid, hidden, rows, pack, sems, pack_sems, out_sems):
+def pack_kernel(parity, gate, up, down, first, second, pack, sems, out_sems):
+    span = down.shape[2] // 2
+    loads = []
+    for turn in range(2):
+        block = parity[0] if turn == 0 else 1 - parity[0]
+        base = pl.multiple_of(block * span, span)
+        loads.append(pack_copies(base, gate, up, down, pack.at[turn], sems.at[turn]))
+    for copy in loads[0] + loads[1]:
+        copy.start()
+    stores = []
+    for turn, out in enumerate((first, second)):
+        for copy in loads[turn]:
+            copy.wait()
+        stores.append(pltpu.make_async_copy(pack.at[turn], out, out_sems.at[turn]))
+        stores[-1].start()
+    for copy in stores:
+        copy.wait()
+
+
+def front_kernel(experts, ids, q_, k_, v_, resid_, hidden_, outgoing,
+                 q, k, v, resid, hidden, rows, sems, out_sems):
     tokens, width = q.shape
     loads = [
         pltpu.make_async_copy(src, dst, sems.at[n])
         for n, (src, dst) in enumerate(((q_, q), (k_, k), (v_, v), (resid_, resid)))
     ]
-    loads_pack = []
-    for turn in range(2):
-        block = parity[0] if turn == 0 else 1 - parity[0]
-        base = pl.multiple_of(block * (down.shape[2] // 2), down.shape[2] // 2)
-        loads_pack.append(pack_copies(base, gate, up, down, pack.at[turn], pack_sems.at[turn]))
-    for copy in loads + loads_pack[0] + loads_pack[1]:
+    for copy in loads:
         copy.start()
     scale = 1.0 / math.sqrt(HEAD_DIM)
     _, slot = slots_of(ids, experts)
@@ -99,12 +115,8 @@
     for copy in loads:
         copy.wait()
     stores = []
-
-    def store(src, dst):
-        stores.append(pltpu.make_async_copy(src, dst, out_sems.at[len(stores)]))
-        stores[-1].start()
-
-    for n in range(width // HEAD_DIM):
+    heads = width // HEAD_DIM
+    for n in range(heads):
         cols = slice(n * HEAD_DIM, (n + 1) * HEAD_DIM)
         scores = nt(q[:, cols], k[:, cols]) * scale
         top = jnp.max(scores, axis=1, keepdims=True)
@@ -114,15 +126,15 @@
         h = (resid[:, cols].astype(F32) + attended).astype(BF)
         hidden[:, cols] = h
         rows[:, cols] = jnp.dot(pick, h, preferred_element_type=F32).astype(BF)
-        if n % 2 == 1:
-            pair = pl.ds((n - 1) * HEAD_DIM, 2 * HEAD_DIM)
-            store(rows.at[:, pair], outgoing.at[:, pair])
-        if n in (2, 5):
-            turn = n // 3
-            for copy in loads_pack[turn]:
-                copy.wait()
-            store(pack.at[turn], (first, second)[turn])
-    store(hidden, hidden_)
+        if (n + 1) % (heads // 2) == 0:
+            part = pl.ds((n + 1) * HEAD_DIM - width // 2, width // 2)
+            for src, dst in ((rows, outgoing), (hidden, hidden_)):
+                stores.append(
+                    pltpu.make_async_copy(
+                        src.at[:, part], dst.at[:, part], out_sems.at[len(stores)]
+                    )
+                )
+                stores[-1].start()
     for copy in stores:
         copy.wait()
 
@@ -139,18 +151,48 @@
     return high, (value - high.astype(F32)).astype(BF)
 
 
-def up_kernel(place, x, gain, sums, u0, u1, v0, v1, after, out, weights, sems):
+def start_either(place, yes, no):
+    @pl.when(place[N_TP] == 1)
+    def _():
+        for copy in yes:
+            copy.start()
+
+    @pl.when(place[N_TP] != 1)
+    def _():
+        for copy in no:
+            copy.start()
+
+
+def up_kernel(place, x, gain, sums, u0, u1, first, v0, v1, out, columns,
+              xg, weights, sems, column_sems):
     rows, depth = x.shape
-    loads = [
-        pltpu.make_async_copy(ref.at[pl.ds(0, depth), :], weights.at[n], sems.at[n])
-        for n, ref in enumerate((u0, u1, v0, v1))
-    ]
-    for copy in loads:
-        copy.start()
+    units = weights.shape[2] // 2
+
+    def load(n, ref):
+        return pltpu.make_async_copy(ref.at[pl.ds(0, depth), :], weights.at[n], sems.at[n])
+
+    def load_columns(n, j, ref):
+        return pltpu.make_async_copy(
+            ref.at[pl.ds(depth + j * units, units), :],
+            columns.at[pl.ds(n * units, units), pl.ds(2 * j * units, 2 * units)],
+            column_sems.at[n, j],
+        )
+
+    for n, ref in ((0, u0), (1, u1), (3, v1)):
+        load(n, ref).start()
+    start_either(place, [load(2, first)], [load(2, v0)])
+    for j in range(2):
+        for n, ref in ((0, u0), (1, u1), (3, v1)):
+            load_columns(n, j, ref).start()
+        start_either(place, [load_columns(2, j, first)], [load_columns(2, j, v0)])
     xf = x[...].astype(F32)
-    xg = (xf * gain[...]).astype(BF)
-    high, low = split(xf * xf)
-    ones = jnp.ones((8, depth), BF)
+    xg[...] = (xf * gain[...]).astype(BF)
+    partial = jnp.zeros((rows, 128), F32)
+    for j in range(depth // 128):
+        part = xf[:, j * 128 : (j + 1) * 128]
+        partial += part * part
+    high, low = split(partial)
+    ones = jnp.ones((8, 128), BF)
     total = nt(ones, high) + nt(ones, low)
     experts = sums.shape[0] - 8
     tokens = jnp.concatenate([sums[experts : experts + 8, :]] * 4, axis=1)
@@ -162,11 +204,19 @@
         [part[i * half : (i + 1) * half, :] for part in parts for i in range(2)], axis=1
     )
     for n in range(N_TP):
-        target = place[n]
-        loads[n].wait()
-        out[target, 0:rows, :] = jnp.dot(xg, weights[n], preferred_element_type=F32).astype(BF)
-        out[target, rows : rows + 16, :] = squares
-        out[target, rows + 16 : rows + 16 + half, :] = logits
+        out[n, rows : rows + 16, :] = squares
+        out[n, rows + 16 : rows + 16 + half, :] = logits
+    for n in (0, 1, 3, 2):
+        load(n, v1).wait()
+        product = jnp.dot(xg[...], weights[n], preferred_element_type=F32)
+        out[place[n], 0:rows, :] = product.astype(BF)
+    for j in range(2):
+        for n in range(N_TP):
+            load_columns(n, j, v1).wait()
+
+
+def after_kernel(message, after, out):
+    pass
 
 
 def inner_kernel(got, inner, sums):
@@ -195,23 +245,11 @@
             inner[n, part, :] = act
 
 
-def down_kernel(place, inners, u0, u1, v0, v1, out, weights, sems):
-    width, span = inners.shape[2], out.shape[1]
-    loads = [
-        pltpu.make_async_copy(ref.at[pl.ds(span, 2 * width), :], weights.at[n], sems.at[n])
-        for n, ref in enumerate((u0, u1, v0, v1))
-    ]
-    for copy in loads:
-        copy.start()
-    parts = [inners[place[n]] for n in range(N_TP)]
-    for copy in loads:
-        copy.wait()
-    for j in range(2):
-        total = jnp.zeros((out.shape[0], 2 * width), F32)
-        for n, part in enumerate(parts):
-            rows = weights[n, j * width : (j + 1) * width, :]
-            total += jnp.dot(part, rows, preferred_element_type=F32)
-        out[:, j * 2 * width : (j + 1) * 2 * width] = total.astype(BF)
+def down_kernel(place, inners, columns, out, inner):
+    width = inners.shape[2]
+    for n in range(N_TP):
+        inner[:, n * width : (n + 1) * width] = inners[place[n]]
+    out[...] = jnp.dot(inner[...], columns[...], preferred_element_type=F32).astype(BF)
 
 
 def mix_kernel(ids, sums, hidden, returned, out):
@@ -243,56 +281,73 @@
 
     dma = pltpu.SemaphoreType.DMA
     payload = struct((width + 2 * units, 2 * units), BF)
-    hidden, outgoing, first, second = call(
+    first, second = call(
+        pack_kernel,
+        [payload, payload],
+        [SM] + [ANY] * 3,
+        [ANY] * 2,
+        [pltpu.VMEM((2,) + payload.shape, BF), dma((2, 4)), dma((2,))],
+        (0, 6_000_000),
+        WHOLE_VMEM,
+    )(parity, w_gate, w_up, w_down)
+    hidden, outgoing = call(
         lambda *refs: front_kernel(experts, *refs),
-        [struct((tokens, width), BF), struct((slots, width), BF), payload, payload],
-        [SM, VM] + [ANY] * 7,
-        [ANY] * 4,
+        [struct((tokens, width), BF), struct((slots, width), BF)],
+        [VM] + [ANY] * 4,
+        [ANY] * 2,
         [pltpu.VMEM((tokens, width), BF)] * 5
-        + [pltpu.VMEM((slots, width), BF), pltpu.VMEM((2,) + payload.shape, BF)]
-        + [dma((4,)), dma((2, 4)), dma((7,))],
-        (300_000_000, 8_500_000),
+        + [pltpu.VMEM((slots, width), BF), dma((4,)), dma((4,))],
+        (300_000_000, 3_000_000),
         WHOLE_VMEM,
-    )(parity, ids, queries, keys, values, resid, w_gate, w_up, w_down)
-
-    stay, turn = [], []
+    )(ids, queries, keys, values, resid)
+    sums = call(
+        router_kernel, struct((experts + 8, tokens), F32), [VM] * 3, VM, (), (150_000_000, 600_000)
+    )(hidden, gain, w_router.T)
+
+    near = [(t // 2, t) for t in range(N_TP)]
+
+    def index(s, t):
+        return s * N_TP + t % N_TP
+
+    stay, turn, over = [], [], []
     for s in range(2):
         for t in range(N_TP):
-            here = s * N_TP + t
-            if s == t // 2:
-                stay.append((here, here))
-            else:
-                stay.append((here, (1 - s) * N_TP + (t + 2) % N_TP))
-            if s == ((t + 1) % N_TP) // 2:
-                turn.append((here, s * N_TP + (t + 1) % N_TP))
-            else:
-                turn.append((here, (1 - s) * N_TP + (t + 3) % N_TP))
-    swap = [(0, 1), (1, 0)]
-    u0 = lax.ppermute(first, ("sec", "tp"), stay)
-    u1 = lax.ppermute(second, ("sec", "tp"), turn)
-    weights = [u0, u1, lax.ppermute(u0, "sec", swap), lax.ppermute(u1, "sec", swap)]
-    base = jnp.where(sec == tp // 2, tp, tp + 2)
-    place = jnp.stack([(base - n) % N_TP for n in range(N_TP)]).astype(jnp.int32)
+            here = index(s, t)
+            stay.append((here, index(1 - s, t) if (s, t) in near else index(s, t + 2)))
+            odd = s == ((t + 1) % N_TP) // 2
+            turn.append((here, index(s, t + 1) if odd else index(1 - s, t + 3)))
+            if (s, t) in near:
+                over.append((here, index(1 - s, t)))
+    both = ("sec", "tp")
+    u0, u1 = lax.ppermute(first, both, stay), lax.ppermute(second, both, turn)
+    u1 = call(after_kernel, payload, [ANY, ANY], ANY, aliases={0: 0})(u1, sums)
+    v0, v1 = lax.ppermute(u0, both, over), lax.ppermute(u1, "sec", [(0, 1), (1, 0)])
+    weights = [u0, u1, first, v0, v1]
+    is_near = sec == tp // 2
+    back = jnp.where(is_near, jnp.array([2, 1, 0, 3]), jnp.array([0, 3, 2, 1]))
+    place = jnp.append((tp - back) % N_TP, is_near).astype(jnp.int32)
 
     arrived = lax.all_to_all(
         outgoing.reshape(experts, CAP, width), "ep", split_axis=0, concat_axis=0, tiled=True
     ).reshape(slots, width)
 
-    sums = call(
-        router_kernel, struct((experts + 8, tokens), F32), [VM] * 3, VM, (), (150_000_000, 600_000)
-    )(hidden, gain, w_router.T)
-
     pairs = [(experts + i, experts + i // 8 * 8 + (i + 1) % 8) for i in range(experts)]
     after = lax.ppermute(arrived, ("sec", "ep"), pairs)
     message = struct((N_TP, slots + 16 + experts // 2, 2 * units), BF)
-    partial = call(
+    partial, columns = call(
         up_kernel,
-        message,
+        [message, struct((N_TP * units, width), BF)],
         [SM] + [VM] * 3 + [ANY] * 5,
-        VM,
-        [pltpu.VMEM((N_TP, width, 2 * units), BF), dma((N_TP,))],
-        (2_200_000_000, 8_000_000),
-    )(place, arrived, gain, sums, *weights, after)
+        [VM, VM],
+        [
+            pltpu.VMEM((slots, width), BF),
+            pltpu.VMEM((N_TP, width, 2 * units), BF),
+            dma((N_TP,)),
+            dma((N_TP, 2)),
+        ],
+        (2_200_000_000, 9_000_000),
+    )(place, arrived, gain, sums, *weights)
+    partial = call(after_kernel, message, [VM, ANY], VM, aliases={0: 0})(partial, after)
     got = lax.all_to_all(partial, "tp", split_axis=0, concat_axis=0, tiled=True)
     inner, sums = call(
         inner_kernel,
@@ -306,11 +361,11 @@
     expert_out = call(
         down_kernel,
         struct((slots, width), BF),
-        [SM, VM] + [ANY] * 4,
+        [SM, VM, VM],
         VM,
-        [pltpu.VMEM((N_TP, 2 * units, 2 * units), BF), dma((N_TP,))],
+        [pltpu.VMEM((slots, N_TP * units), BF)],
         (1_100_000_000, 4_000_000),
-    )(place, inners, *weights)
+    )(place, inners, columns)
     returned = lax.all_to_all(
         expert_out.reshape(experts, CAP, width), "ep", split_axis=0, concat_axis=0, tiled=True
     ).reshape(slots, width)

time: 152 us -> 149 us (0.980)
  waiting for transfers between devices: 34.2 us -> 25.8 us
  starting transfers between devices: 35 us -> 38.5 us
  blocking collectives: 63.6 us -> 66.7 us
    ppermute x4, waiting for transfers between devices: 14.6 us -> 9.37 us  [the longest x2 9.37 us: body(): u0, u1 = (lax.ppermute(first, both, stay), lax.ppermute(second, both, turn))]
    ppermute x1, waiting for transfers between devices: 12.2 us -> 8.81 us  [body(): after = lax.ppermute(arrived, ('sec', 'ep'), pairs)]
    all_to_all x1, blocking collectives: 28.1 us -> 31.5 us  [body(): lax.all_to_all(expert_out.reshape(experts, CAP, width), 'ep', split_axis=...]
    ppermute x4, starting transfers between devices: 15.5 us -> 18.7 us  [the longest x1 9.14 us: body(): lax.ppermute(u1, 'sec', [(0, 1), (1, 0)])]
    pallas_call x1, Pallas kernels: 6.7 us -> 5.07 us  [body(): call(lambda *refs: front_kernel(experts, *refs), [struct((tokens, width),...]
    pallas_call x2 -> x5, Pallas kernels: 8.18 us -> 9.6 us  [the longest x1 4.72 us: body(): call(up_kernel, [message, struct((N_TP * units, width), BF)], [SM] + [VM]...]
  transfers between devices with their start and end apart: 6 -> 6, of which waited for: 4 -> 3; matrix products, arithmetic and copies ran while one was open for 0% -> 0% of each run, Pallas kernels for 1% -> 7%
where the time goes in v4:
time: 149 us
  blocking collectives  66.7 us (45%)
  starting transfers between devices  38.5 us (26%)
  waiting for transfers between devices  25.8 us (17%)
  Pallas kernels  17.4 us (12%)
    all_to_all x1, blocking collectives, body(): lax.all_to_all(expert_out.reshape(experts, CAP, width), 'ep', split_axis=...  31.5 us
    all_to_all x1, blocking collectives, body(): got = lax.all_to_all(partial, 'tp', split_axis=0, concat_axis=0, tiled=True)  23.1 us
    all_to_all x1, starting transfers between devices, body(): lax.all_to_all(outgoing.reshape(experts, CAP, width), 'ep', split_axis=0,...  16.4 us
    all_to_all x1, blocking collectives, body(): lax.all_to_all(inner, 'tp', split_axis=0, concat_axis=0, tiled=True)  12.2 us
    ppermute x2, waiting for transfers between devices, body(): u0, u1 = (lax.ppermute(first, both, stay), lax.ppermute(second, both, turn))  9.37 us
    ppermute x1, starting transfers between devices, body(): lax.ppermute(u1, 'sec', [(0, 1), (1, 0)])  9.14 us
    ppermute x1, waiting for transfers between devices, body(): after = lax.ppermute(arrived, ('sec', 'ep'), pairs)  8.81 us
    ppermute x2, starting transfers between devices, body(): u0, u1 = (lax.ppermute(first, both, stay), lax.ppermute(second, both, turn))  8.31 us
  transfers between devices with their start and end apart: 6, of which 3 were waited for; matrix products, arithmetic and copies ran while one was open for 0% of the time, Pallas kernels for 7%

profile of v4, /device:TPU:1, one launch (start us, length us, event | category | flops | bytes accessed | tf_op | source)
XLA Modules:
  0.0 148.9 jit_solution(11993867674456701536)
XLA Ops:
  0.0 3.1 %shard_map.120 = (bf16[1536,512]{1,0:T(8,128)(2,1)}, bf16[1536,512]{1,0:T(8,128)(2,1)}) custom-call(s32[1]{0:T(128)} %bitcast.6.parity, bf16[1,2048,256]{2,1,0:T(8,128)(2,1)} %gate.1, bf16[1,2048,256]{2,1,0:T(8,128)(2,1)} %up.1, bf16[1,256,2048]{2,1,0:T(8,128)(2,1)} %down.1), custom_call_target="tpu_custom_call" | custom-call | bytes 6000000 | tf_op jit(solution)/shard_map/pallas_call | solution.py:284
  3.1 5.8 %collective-permute-start.1 = (bf16[1536,512]{1,0:T(8,128)(2,1)}, bf16[1536,512]{1,0:T(8,128)(2,1)}, u32[]{:S(2)}, u32[]{:S(2)}) collective-permute-start(bf16[1536,512]{1,0:T(8,128)(2,1)} %get-tuple-element.16), channel_id=1, source_target_pairs={{0,1},{1,256},{2,257},{3,0},{256,3},{257,258},{258,259},{259,2},{4... | collective-permute-start | bytes 4718600 | tf_op jit(solution)/shard_map/ppermute | solution.py:322
  8.9 2.5 %collective-permute-start = (bf16[1536,512]{1,0:T(8,128)(2,1)}, bf16[1536,512]{1,0:T(8,128)(2,1)}, u32[]{:S(2)}, u32[]{:S(2)}) collective-permute-start(bf16[1536,512]{1,0:T(8,128)(2,1)} %get-tuple-element.15.first), channel_id=1, source_target_pairs={{0,256},{1,257},{2,0},{3,1},{256,258},{257,259},{258,2},{259,3},{4... | collective-permute-start | bytes 4718600 | tf_op jit(solution)/shard_map/ppermute | solution.py:322
  11.4 0.0 copy-start.2
  11.4 0.0 copy-start.3
  11.4 5.1 %shard_map.118 = (bf16[128,1024]{1,0:T(8,128)(2,1)}, bf16[512,1024]{1,0:T(8,128)(2,1)}) custom-call(s32[2,128]{1,0:T(2,128)} %bitcast.16, bf16[128,1024]{1,0:T(8,128)(2,1)} %refs_1_.1, bf16[128,1024]{1,0:T(8,128)(2,1)} %refs_2_.1, bf16[128,1024]{1,0:T(8,128)(2,1)} %refs_3_.1, bf16[128,1024]{1,0:T(8,128)(2,1)} %refs_4_.1), custom_call_target="tpu_custom_call" | custom-call | flops 300000000 | bytes 3000000 | tf_op jit(solution)/shard_map/pallas_call | solution.py:293
  16.5 0.0 copy-start.1
  16.5 16.4 %all-to-all-start = ((bf16[64,8,1024]{2,1,0:T(8,128)(2,1)}), bf16[64,8,1024]{2,1,0:T(8,128)(2,1)S(1)}, u32[]{:S(2)}, u32[]{:S(2)}) async-start(bf16[64,8,1024]{2,1,0:T(8,128)(2,1)} %bitcast.18), calls=%async_computation | async-start | bytes 2097152 | tf_op jit(solution)/shard_map/all_to_all | solution.py:330
  33.0 0.0 copy-done.2
  33.0 0.0 copy-done.3
  33.0 0.0 copy-done.1
  33.0 1.0 shard_map.119.after.sums
  34.0 0.0 copy-start.5
  34.0 0.0 copy-start.6
  34.0 0.0 copy-start
  34.1 9.4 %collective-permute-done.1.message = bf16[1536,512]{1,0:T(8,128)(2,1)} collective-permute-done((bf16[1536,512]{1,0:T(8,128)(2,1)}, bf16[1536,512]{1,0:T(8,128)(2,1)}, u32[]{:S(2)}, u32[]{:S(2)}) %collective-permute-start.1) | collective-permute-done | bytes 1572896 | tf_op jit(solution)/shard_map/ppermute | solution.py:322
  43.4 9.1 %collective-permute-start.3 = (bf16[1536,512]{1,0:T(8,128)(2,1)}, bf16[1536,512]{1,0:T(8,128)(2,1)}, u32[]{:S(2)}, u32[]{:S(2)}) collective-permute-start(bf16[1536,512]{1,0:T(8,128)(2,1)} %shard_map.121.u1), channel_id=1, source_target_pairs={{0,256},{256,0},{1,257},{257,1},{2,258},{258,2},{3,259},{259,3},{4... | collective-permute-start | bytes 4718600 | tf_op jit(solution)/shard_map/ppermute | solution.py:324
  52.6 0.0 collective-permute-done.u0
  52.6 1.3 collective-permute-start.2
  53.9 7.6 %all-to-all-done = bf16[64,8,1024]{2,1,0:T(8,128)(2,1)S(1)} async-done(((bf16[64,8,1024]{2,1,0:T(8,128)(2,1)}), bf16[64,8,1024]{2,1,0:T(8,128)(2,1)S(1)}, u32[]{:S(2)}, u32[]{:S(2)}) %all-to-all-start) | async-done | bytes 1048608 | tf_op jit(solution)/shard_map/all_to_all | solution.py:330
  61.5 3.3 %collective-permute-start.4 = (bf16[512,1024]{1,0:T(8,128)(2,1)S(1)}, bf16[512,1024]{1,0:T(8,128)(2,1)}, u32[]{:S(2)}, u32[]{:S(2)}) collective-permute-start(bf16[512,1024]{1,0:T(8,128)(2,1)S(1)} %bitcast.11), channel_id=1, source_target_pairs={{256,260},{260,264},{264,268},{268,272},{272,276},{276,280},{280,2... | collective-permute-start | bytes 3145736 | tf_op jit(solution)/shard_map/ppermute | solution.py:335
  64.9 0.0 copy-done.5
  64.9 0.0 copy-done.6
  64.9 0.1 pad_add_fusion.place
  65.0 0.0 collective-permute-done.3.v1
  65.0 0.0 collective-permute-done.2.v0
  65.0 0.0 copy-done
  65.0 4.7 %shard_map.122 = (bf16[4,560,512]{2,1,0:T(8,128)(2,1)S(1)}, bf16[1024,1024]{1,0:T(8,128)(2,1)S(1)}) custom-call(s32[5]{0:T(128)S(1)} %pad_add_fusion.place, bf16[512,1024]{1,0:T(8,128)(2,1)S(1)} %bitcast.12, f32[1,1024]{1,0:T(1,128)S(1)} %bitcast.15, f32[72,128]{1,0:T(8,128)S(1)} %shard_map.119.after.sums, bf16[1536,512]{1,0:T(8,128)(2,1)} %collective-permute-done.u0, ...), custom_call_target="tpu_custom_call" | custom-call | flops 2200000000 | bytes 9000000 | tf_op jit(solution)/shard_map/pallas_call | solution.py:337
  69.7 8.8 %collective-permute-done.4.after = bf16[512,1024]{1,0:T(8,128)(2,1)} collective-permute-done((bf16[512,1024]{1,0:T(8,128)(2,1)S(1)}, bf16[512,1024]{1,0:T(8,128)(2,1)}, u32[]{:S(2)}, u32[]{:S(2)}) %collective-permute-start.4) | collective-permute-done | bytes 1048608 | tf_op jit(solution)/shard_map/ppermute | solution.py:335
  78.6 23.1 %all_to_all.20.got = bf16[4,560,512]{2,1,0:T(8,128)(2,1)S(1)} all-to-all(bf16[4,560,512]{2,1,0:T(8,128)(2,1)S(1)} %shard_map.123), channel_id=1, replica_groups=mesh['sec'=2,'ep'=64,'tp'=4] {'tp'}, dimensions={0} | all-to-all | bytes 4587520 | tf_op jit(solution)/shard_map/all_to_all | solution.py:351
  101.7 0.4 shard_map.124
  102.1 12.2 %all_to_all.21.inners = bf16[4,512,256]{2,1,0:T(8,128)(2,1)S(1)} all-to-all(bf16[4,512,256]{2,1,0:T(8,128)(2,1)S(1)} %get-tuple-element.19), channel_id=1, replica_groups=mesh['sec'=2,'ep'=64,'tp'=4] {'tp'}, dimensions={0} | all-to-all | bytes 2097152 | tf_op jit(solution)/shard_map/all_to_all | solution.py:360
  114.3 1.8 %shard_map.125 = bf16[512,1024]{1,0:T(8,128)(2,1)S(1)} custom-call(s32[5]{0:T(128)S(1)} %pad_add_fusion.place, bf16[4,512,256]{2,1,0:T(8,128)(2,1)S(1)} %all_to_all.21.inners, bf16[1024,1024]{1,0:T(8,128)(2,1)S(1)} %get-tuple-element.20.columns), custom_call_target="tpu_custom_call" | custom-call | flops 1100000000 | bytes 4000000 | tf_op jit(solution)/shard_map/pallas_call | solution.py:361
  116.1 0.0 copy-start.4
  116.1 31.5 %all_to_all.22 = bf16[64,8,1024]{2,1,0:T(8,128)(2,1)S(1)} all-to-all(bf16[64,8,1024]{2,1,0:T(8,128)(2,1)S(1)} %bitcast.9), channel_id=1, replica_groups=mesh['sec'=2,'ep'=64,'tp'=4] {'ep'}, dimensions={0} | all-to-all | bytes 2097152 | tf_op jit(solution)/shard_map/all_to_all | solution.py:369
  147.5 0.0 copy-done.4
  147.5 1.3 shard_map.126
  (3 shorter events, 0.0 us)
Async XLA Ops:
  3.1 40.3 %collective-permute-start.1 = (bf16[1536,512]{1,0:T(8,128)(2,1)}, bf16[1536,512]{1,0:T(8,128)(2,1)}, u32[]{:S(2)}, u32[]{:S(2)}) collective-permute-start(bf16[1536,512]{1,0:T(8,128)(2,1)} %get-tuple-element.16), channel_id=1, source_target_pairs={{0,1},{1,256},{2,257},{3,0},{256,3},{257,258},{258,259},{259,2},{4... | collective-permute-start | bytes 4718600 | tf_op jit(solution)/shard_map/ppermute | solution.py:322
  8.9 43.7 %collective-permute-start = (bf16[1536,512]{1,0:T(8,128)(2,1)}, bf16[1536,512]{1,0:T(8,128)(2,1)}, u32[]{:S(2)}, u32[]{:S(2)}) collective-permute-start(bf16[1536,512]{1,0:T(8,128)(2,1)} %get-tuple-element.15.first), channel_id=1, source_target_pairs={{0,256},{1,257},{2,0},{3,1},{256,258},{257,259},{258,2},{259,3},{4... | collective-permute-start | bytes 4718600 | tf_op jit(solution)/shard_map/ppermute | solution.py:322
  11.4 21.6 %copy-start.2 = (f32[1024,64]{0,1:T(8,128)S(1)}, f32[1024,64]{0,1:T(8,128)}, u32[]{:S(2)}) copy-start(f32[1024,64]{0,1:T(8,128)} %param.17) | copy-start | bytes 786436
  11.4 21.6 %copy-start.3 = (f32[1024]{0:T(1024)S(1)}, f32[1024]{0:T(1024)}, u32[]{:S(2)}) copy-start(f32[1024]{0:T(1024)} %param.16) | copy-start | bytes 12292
  16.5 16.5 %copy-start.1 = (bf16[128,1024]{1,0:T(8,128)(2,1)S(1)}, bf16[128,1024]{1,0:T(8,128)(2,1)}, u32[]{:S(2)}) copy-start(bf16[128,1024]{1,0:T(8,128)(2,1)} %get-tuple-element.14.hidden) | copy-start | bytes 786436
  16.5 45.0 %all-to-all-start = ((bf16[64,8,1024]{2,1,0:T(8,128)(2,1)}), bf16[64,8,1024]{2,1,0:T(8,128)(2,1)S(1)}, u32[]{:S(2)}, u32[]{:S(2)}) async-start(bf16[64,8,1024]{2,1,0:T(8,128)(2,1)} %bitcast.18), calls=%async_computation | async-start | bytes 2097152 | tf_op jit(solution)/shard_map/all_to_all | solution.py:330
  34.0 30.9 %copy-start.5 = (s32[4]{0:T(128)S(1)}, s32[4]{0:T(128)}, u32[]{:S(2)}) copy-start(s32[4]{0:T(128)} %constant.52.clone) | copy-start | bytes 52
  34.0 30.9 %copy-start.6 = (s32[4]{0:T(128)S(1)}, s32[4]{0:T(128)}, u32[]{:S(2)}) copy-start(s32[4]{0:T(128)} %constant.53.clone) | copy-start | bytes 52
  34.0 31.0 %copy-start = (bf16[1536,512]{1,0:T(8,128)(2,1)S(1)}, bf16[1536,512]{1,0:T(8,128)(2,1)}, u32[]{:S(2)}) copy-start(bf16[1536,512]{1,0:T(8,128)(2,1)} %get-tuple-element.15.first) | copy-start | bytes 4718596
  43.4 21.6 %collective-permute-start.3 = (bf16[1536,512]{1,0:T(8,128)(2,1)}, bf16[1536,512]{1,0:T(8,128)(2,1)}, u32[]{:S(2)}, u32[]{:S(2)}) collective-permute-start(bf16[1536,512]{1,0:T(8,128)(2,1)} %shard_map.121.u1), channel_id=1, source_target_pairs={{0,256},{256,0},{1,257},{257,1},{2,258},{258,2},{3,259},{259,3},{4... | collective-permute-start | bytes 4718600 | tf_op jit(solution)/shard_map/ppermute | solution.py:324
  52.6 12.4 %collective-permute-start.2 = (bf16[1536,512]{1,0:T(8,128)(2,1)}, bf16[1536,512]{1,0:T(8,128)(2,1)}, u32[]{:S(2)}, u32[]{:S(2)}) collective-permute-start(bf16[1536,512]{1,0:T(8,128)(2,1)} %collective-permute-done.u0), channel_id=1, source_target_pairs={{0,256},{1,257},{258,2},{259,3},{4,260},{5,261},{262,6},{263,7},{8... | collective-permute-start | bytes 4718600 | tf_op jit(solution)/shard_map/ppermute | solution.py:324
  61.5 17.0 %collective-permute-start.4 = (bf16[512,1024]{1,0:T(8,128)(2,1)S(1)}, bf16[512,1024]{1,0:T(8,128)(2,1)}, u32[]{:S(2)}, u32[]{:S(2)}) collective-permute-start(bf16[512,1024]{1,0:T(8,128)(2,1)S(1)} %bitcast.11), channel_id=1, source_target_pairs={{256,260},{260,264},{264,268},{268,272},{272,276},{276,280},{280,2... | collective-permute-start | bytes 3145736 | tf_op jit(solution)/shard_map/ppermute | solution.py:335
  116.1 31.5 %copy-start.4 = (s32[128,2]{0,1:T(2,128)S(1)}, s32[128,2]{0,1:T(2,128)}, u32[]{:S(2)}) copy-start(s32[128,2]{0,1:T(2,128)} %param.18) | copy-start | bytes 3076

commit v5 on v4

--- a/solution.py
+++ b/solution.py
@@ -163,7 +163,7 @@
             copy.start()
 
 
-def up_kernel(place, x, gain, sums, u0, u1, first, v0, v1, out, columns,
+def up_kernel(place, x, gain, sums, u0, u1, first, v0, v1, out, columns, head,
               xg, weights, sems, column_sems):
     rows, depth = x.shape
     units = weights.shape[2] // 2
@@ -187,6 +187,7 @@
         start_either(place, [load_columns(2, j, first)], [load_columns(2, j, v0)])
     xf = x[...].astype(F32)
     xg[...] = (xf * gain[...]).astype(BF)
+    head[...] = x[0 : head.shape[0], :]
     partial = jnp.zeros((rows, 128), F32)
     for j in range(depth // 128):
         part = xf[:, j * 128 : (j + 1) * 128]
@@ -198,14 +199,13 @@
     tokens = jnp.concatenate([sums[experts : experts + 8, :]] * 4, axis=1)
     tile = lax.broadcasted_iota(jnp.int32, total.shape, 0)
     squares = jnp.concatenate(split(jnp.where(tile < 4, total, tokens)), axis=0)
-    half = experts // 2
-    parts = split(sums[0:experts, :])
+    quarter = experts // 4
     logits = jnp.concatenate(
-        [part[i * half : (i + 1) * half, :] for part in parts for i in range(2)], axis=1
+        [sums[i * quarter : (i + 1) * quarter, :].astype(BF) for i in range(4)], axis=1
     )
     for n in range(N_TP):
         out[n, rows : rows + 16, :] = squares
-        out[n, rows + 16 : rows + 16 + half, :] = logits
+        out[n, rows + 16 : rows + 16 + quarter, :] = logits
     for n in (0, 1, 3, 2):
         load(n, v1).wait()
         product = jnp.dot(xg[...], weights[n], preferred_element_type=F32)
@@ -221,18 +221,17 @@
 
 def inner_kernel(got, inner, sums):
     rows, width = inner.shape[1:]
-    half = sums.shape[0] // 2 - 4
+    quarter = sums.shape[0] // 4 - 2
     total = got[0, 0:rows, :].astype(F32)
     tail = got[0, rows:, :].astype(F32)
     for n in range(1, N_TP):
         total = total + got[n, 0:rows, :].astype(F32)
         tail = tail + got[n, rows:, :].astype(F32)
     square = tail[0:8, :] + tail[8:16, :]
-    logits = tail[16 : 16 + half, :]
-    logits = logits[:, 0:256] + logits[:, 256:512]
-    sums[0:half, :] = logits[:, 0:128]
-    sums[half : 2 * half, :] = logits[:, 128:256]
-    sums[2 * half : 2 * half + 8, :] = jnp.broadcast_to(square[4:5, 0:128], (8, 128))
+    for i in range(4):
+        lanes = slice(i * 128, (i + 1) * 128)
+        sums[i * quarter : (i + 1) * quarter, :] = tail[16 : 16 + quarter, lanes]
+    sums[4 * quarter : 4 * quarter + 8, :] = jnp.broadcast_to(square[4:5, 0:128], (8, 128))
     inv = lax.rsqrt(square[0:1, :] / D + EPS)
     for j in range(rows // 128):
         part = slice(j * 128, (j + 1) * 128)
@@ -267,6 +266,10 @@
     mixed = lax.dot_general(high, rows, dims, preferred_element_type=F32)
     mixed += lax.dot_general(low, rows, dims, preferred_element_type=F32)
     out[...] = (hidden[...].astype(F32) + mixed).astype(BF)
+
+
+def second_only(experts, step):
+    return [(experts + i, experts + i // 8 * 8 + (i + step) % 8) for i in range(experts)]
 
 
 def body(resid, queries, keys, values, norm_gain, w_router, expert_ids, w_gate, w_up, w_down):
@@ -327,18 +330,20 @@
     back = jnp.where(is_near, jnp.array([2, 1, 0, 3]), jnp.array([0, 3, 2, 1]))
     place = jnp.append((tp - back) % N_TP, is_near).astype(jnp.int32)
 
+    after = lax.ppermute(hidden, ("sec", "ep"), second_only(experts, 1))
+    outgoing = call(
+        after_kernel, struct((slots, width), BF), [ANY, ANY], ANY, vmem=WHOLE_VMEM, aliases={0: 0}
+    )(outgoing, after)
     arrived = lax.all_to_all(
         outgoing.reshape(experts, CAP, width), "ep", split_axis=0, concat_axis=0, tiled=True
     ).reshape(slots, width)
 
-    pairs = [(experts + i, experts + i // 8 * 8 + (i + 1) % 8) for i in range(experts)]
-    after = lax.ppermute(arrived, ("sec", "ep"), pairs)
-    message = struct((N_TP, slots + 16 + experts // 2, 2 * units), BF)
-    partial, columns = call(
+    message = struct((N_TP, slots + 16 + experts // 4, 2 * units), BF)
+    partial, columns, head = call(
         up_kernel,
-        [message, struct((N_TP * units, width), BF)],
+        [message, struct((N_TP * units, width), BF), struct((tokens, width), BF)],
         [SM] + [VM] * 3 + [ANY] * 5,
-        [VM, VM],
+        [VM, VM, VM],
         [
             pltpu.VMEM((slots, width), BF),
             pltpu.VMEM((N_TP, width, 2 * units), BF),
@@ -347,6 +352,7 @@
         ],
         (2_200_000_000, 9_000_000),
     )(place, arrived, gain, sums, *weights)
+    after = lax.ppermute(head, ("sec", "ep"), second_only(experts, 1))
     partial = call(after_kernel, message, [VM, ANY], VM, aliases={0: 0})(partial, after)
     got = lax.all_to_all(partial, "tp", split_axis=0, concat_axis=0, tiled=True)
     inner, sums = call(

time: 149 us -> 147 us (0.987)
  waiting for transfers between devices: 25.8 us -> 22.3 us
  starting transfers between devices: 38.5 us -> 41.1 us
  blocking collectives: 66.7 us -> 65 us
    ppermute x2, waiting for transfers between devices: 9.37 us -> 0.01 us  [body(): u0, u1 = (lax.ppermute(first, both, stay), lax.ppermute(second, both, turn))]
    ppermute x1 -> x2, starting transfers between devices: 3.34 us -> 6.62 us  [the longest x1 3.41 us: body(): after = lax.ppermute(head, ('sec', 'ep'), second_only(experts, 1))]
    all_to_all x1, waiting for transfers between devices: 7.63 us -> 10.9 us  [body(): lax.all_to_all(outgoing.reshape(experts, CAP, width), 'ep', split_axis=0,...]
    ppermute x1 -> x2, waiting for transfers between devices: 8.81 us -> 11.4 us  [the longest x1 6.25 us: body(): after = lax.ppermute(hidden, ('sec', 'ep'), second_only(experts, 1))]
    all_to_all x1, blocking collectives: 31.5 us -> 28.9 us  [body(): lax.all_to_all(expert_out.reshape(experts, CAP, width), 'ep', split_axis=...]
    pallas_call x1 -> x2, Pallas kernels: 4.72 us -> 4.72 us  [the longest x1 4.72 us: body(): call(up_kernel, [message, struct((N_TP * units, width), BF), struct((toke...]
  transfers between devices with their start and end apart: 6 -> 7, of which waited for: 3 -> 3; matrix products, arithmetic and copies ran while one was open for 0% -> 0% of each run, Pallas kernels for 7% -> 4%
where the time goes in v5:
time: 147 us
  blocking collectives  65 us (44%)
  starting transfers between devices  41.1 us (28%)
  waiting for transfers between devices  22.3 us (15%)
  Pallas kernels  17.4 us (12%)
    all_to_all x1, blocking collectives, body(): lax.all_to_all(expert_out.reshape(experts, CAP, width), 'ep', split_axis=...  28.9 us
    all_to_all x1, blocking collectives, body(): got = lax.all_to_all(partial, 'tp', split_axis=0, concat_axis=0, tiled=True)  24 us
    all_to_all x1, starting transfers between devices, body(): lax.all_to_all(outgoing.reshape(experts, CAP, width), 'ep', split_axis=0,...  15.9 us
    all_to_all x1, blocking collectives, body(): lax.all_to_all(inner, 'tp', split_axis=0, concat_axis=0, tiled=True)  12.2 us
    all_to_all x1, waiting for transfers between devices, body(): lax.all_to_all(outgoing.reshape(experts, CAP, width), 'ep', split_axis=0,...  10.9 us
    ppermute x1, starting transfers between devices, body(): lax.ppermute(u1, 'sec', [(0, 1), (1, 0)])  8.93 us
    ppermute x2, starting transfers between devices, body(): u0, u1 = (lax.ppermute(first, both, stay), lax.ppermute(second, both, turn))  8.31 us
    ppermute x1, waiting for transfers between devices, body(): after = lax.ppermute(hidden, ('sec', 'ep'), second_only(experts, 1))  6.25 us
  transfers between devices with their start and end apart: 7, of which 3 were waited for; matrix products, arithmetic and copies ran while one was open for 0% of the time, Pallas kernels for 4%

profile of v5, /device:TPU:1, one launch (start us, length us, event | category | flops | bytes accessed | tf_op | source)
XLA Modules:
  0.0 146.8 jit_solution(14644246951606652757)
XLA Ops:
  0.0 3.1 %shard_map.121 = (bf16[1536,512]{1,0:T(8,128)(2,1)}, bf16[1536,512]{1,0:T(8,128)(2,1)}) custom-call(s32[1]{0:T(128)} %bitcast.6.parity, bf16[1,2048,256]{2,1,0:T(8,128)(2,1)} %gate.1, bf16[1,2048,256]{2,1,0:T(8,128)(2,1)} %up.1, bf16[1,256,2048]{2,1,0:T(8,128)(2,1)} %down.1), custom_call_target="tpu_custom_call" | custom-call | bytes 6000000 | tf_op jit(solution)/shard_map/pallas_call | solution.py:287
  3.1 5.8 %collective-permute-start.2 = (bf16[1536,512]{1,0:T(8,128)(2,1)}, bf16[1536,512]{1,0:T(8,128)(2,1)}, u32[]{:S(2)}, u32[]{:S(2)}) collective-permute-start(bf16[1536,512]{1,0:T(8,128)(2,1)} %get-tuple-element.17), channel_id=1, source_target_pairs={{0,1},{1,256},{2,257},{3,0},{256,3},{257,258},{258,259},{259,2},{4... | collective-permute-start | bytes 4718600 | tf_op jit(solution)/shard_map/ppermute | solution.py:325
  8.9 2.5 %collective-permute-start.1 = (bf16[1536,512]{1,0:T(8,128)(2,1)}, bf16[1536,512]{1,0:T(8,128)(2,1)}, u32[]{:S(2)}, u32[]{:S(2)}) collective-permute-start(bf16[1536,512]{1,0:T(8,128)(2,1)} %get-tuple-element.16.first), channel_id=1, source_target_pairs={{0,256},{1,257},{2,0},{3,1},{256,258},{257,259},{258,2},{259,3},{4... | collective-permute-start | bytes 4718600 | tf_op jit(solution)/shard_map/ppermute | solution.py:325
  11.4 5.0 %shard_map.118 = (bf16[128,1024]{1,0:T(8,128)(2,1)}, bf16[512,1024]{1,0:T(8,128)(2,1)}) custom-call(s32[2,128]{1,0:T(2,128)} %bitcast.15, bf16[128,1024]{1,0:T(8,128)(2,1)} %refs_1_.1, bf16[128,1024]{1,0:T(8,128)(2,1)} %refs_2_.1, bf16[128,1024]{1,0:T(8,128)(2,1)} %refs_3_.1, bf16[128,1024]{1,0:T(8,128)(2,1)} %refs_4_.1), custom_call_target="tpu_custom_call" | custom-call | flops 300000000 | bytes 3000000 | tf_op jit(solution)/shard_map/pallas_call | solution.py:296
  16.5 3.2 %collective-permute-start = (bf16[128,1024]{1,0:T(8,128)(2,1)}, bf16[128,1024]{1,0:T(8,128)(2,1)S(1)}, u32[]{:S(2)}, u32[]{:S(2)}) collective-permute-start(bf16[128,1024]{1,0:T(8,128)(2,1)} %get-tuple-element.15.hidden), channel_id=1, source_target_pairs={{256,260},{260,264},{264,268},{268,272},{272,276},{276,280},{280,2... | collective-permute-start | bytes 786440 | tf_op jit(solution)/shard_map/ppermute | solution.py:333
  19.7 6.2 %collective-permute-done.after = bf16[128,1024]{1,0:T(8,128)(2,1)S(1)} collective-permute-done((bf16[128,1024]{1,0:T(8,128)(2,1)}, bf16[128,1024]{1,0:T(8,128)(2,1)S(1)}, u32[]{:S(2)}, u32[]{:S(2)}) %collective-permute-start) | collective-permute-done | bytes 262176 | tf_op jit(solution)/shard_map/ppermute | solution.py:333
  25.9 0.0 copy-start.5
  25.9 0.7 copy-done.5
  26.6 0.0 copy-start.1
  26.6 0.0 copy-start.2
  26.6 0.0 copy-start.3
  26.6 15.9 %all-to-all-start = ((bf16[64,8,1024]{2,1,0:T(8,128)(2,1)}), bf16[64,8,1024]{2,1,0:T(8,128)(2,1)S(1)}, u32[]{:S(2)}, u32[]{:S(2)}) async-start(bf16[64,8,1024]{2,1,0:T(8,128)(2,1)} %bitcast.17), calls=%async_computation | async-start | bytes 2097152 | tf_op jit(solution)/shard_map/all_to_all | solution.py:337
  42.6 0.0 copy-done.1
  42.6 0.0 copy-done.2
  42.6 0.0 copy-done.3
  42.6 1.0 shard_map.120.after.sums
  43.6 0.0 copy-start.6
  43.6 0.0 copy-start.7
  43.6 0.0 copy-start
  43.6 0.0 collective-permute-done.2.message
  43.6 8.9 %collective-permute-start.4 = (bf16[1536,512]{1,0:T(8,128)(2,1)}, bf16[1536,512]{1,0:T(8,128)(2,1)}, u32[]{:S(2)}, u32[]{:S(2)}) collective-permute-start(bf16[1536,512]{1,0:T(8,128)(2,1)} %shard_map.122.u1), channel_id=1, source_target_pairs={{0,256},{256,0},{1,257},{257,1},{2,258},{258,2},{3,259},{259,3},{4... | collective-permute-start | bytes 4718600 | tf_op jit(solution)/shard_map/ppermute | solution.py:327
  52.6 0.0 collective-permute-done.1.u0
  52.6 1.3 collective-permute-start.3
  53.9 0.0 copy-done.6
  53.9 0.0 copy-done.7
  53.9 0.1 pad_add_fusion.place
  54.0 10.9 %all-to-all-done = bf16[64,8,1024]{2,1,0:T(8,128)(2,1)S(1)} async-done(((bf16[64,8,1024]{2,1,0:T(8,128)(2,1)}), bf16[64,8,1024]{2,1,0:T(8,128)(2,1)S(1)}, u32[]{:S(2)}, u32[]{:S(2)}) %all-to-all-start) | async-done | bytes 1048608 | tf_op jit(solution)/shard_map/all_to_all | solution.py:337
  64.9 0.0 collective-permute-done.4.v1
  64.9 0.0 collective-permute-done.3.v0
  64.9 0.0 copy-done
  64.9 4.7 %shard_map.123 = (bf16[4,544,512]{2,1,0:T(8,128)(2,1)S(1)}, bf16[1024,1024]{1,0:T(8,128)(2,1)S(1)}, bf16[128,1024]{1,0:T(8,128)(2,1)S(1)}) custom-call(s32[5]{0:T(128)S(1)} %pad_add_fusion.place, bf16[512,1024]{1,0:T(8,128)(2,1)S(1)} %bitcast.11, f32[1,1024]{1,0:T(1,128)S(1)} %bitcast.14, f32[72,128]{1,0:T(8,128)S(1)} %shard_map.120.after.sums, ...), custom_call_target="tpu_custom_call" | custom-call | flops 2200000000 | bytes 9000000 | tf_op jit(solution)/shard_map/pallas_call | solution.py:342
  69.6 3.4 %collective-permute-start.5 = (bf16[128,1024]{1,0:T(8,128)(2,1)S(1)}, bf16[128,1024]{1,0:T(8,128)(2,1)S(1)}, u32[]{:S(2)}, u32[]{:S(2)}) collective-permute-start(bf16[128,1024]{1,0:T(8,128)(2,1)S(1)} %get-tuple-element.19), channel_id=1, source_target_pairs={{256,260},{260,264},{264,268},{268,272},{272,276},{276,280},{280,2... | collective-permute-start | bytes 786440 | tf_op jit(solution)/shard_map/ppermute | solution.py:355
  73.0 5.2 %collective-permute-done.5.after = bf16[128,1024]{1,0:T(8,128)(2,1)S(1)} collective-permute-done((bf16[128,1024]{1,0:T(8,128)(2,1)S(1)}, bf16[128,1024]{1,0:T(8,128)(2,1)S(1)}, u32[]{:S(2)}, u32[]{:S(2)}) %collective-permute-start.5) | collective-permute-done | bytes 262176 | tf_op jit(solution)/shard_map/ppermute | solution.py:355
  78.2 24.0 %all_to_all.20.got = bf16[4,544,512]{2,1,0:T(8,128)(2,1)S(1)} all-to-all(bf16[4,544,512]{2,1,0:T(8,128)(2,1)S(1)} %shard_map.124), channel_id=1, replica_groups=mesh['sec'=2,'ep'=64,'tp'=4] {'tp'}, dimensions={0} | all-to-all | bytes 4456448 | tf_op jit(solution)/shard_map/all_to_all | solution.py:357
  102.2 0.4 shard_map.125
  102.6 12.2 %all_to_all.21.inners = bf16[4,512,256]{2,1,0:T(8,128)(2,1)S(1)} all-to-all(bf16[4,512,256]{2,1,0:T(8,128)(2,1)S(1)} %get-tuple-element.21), channel_id=1, replica_groups=mesh['sec'=2,'ep'=64,'tp'=4] {'tp'}, dimensions={0} | all-to-all | bytes 2097152 | tf_op jit(solution)/shard_map/all_to_all | solution.py:366
  114.8 1.8 %shard_map.126 = bf16[512,1024]{1,0:T(8,128)(2,1)S(1)} custom-call(s32[5]{0:T(128)S(1)} %pad_add_fusion.place, bf16[4,512,256]{2,1,0:T(8,128)(2,1)S(1)} %all_to_all.21.inners, bf16[1024,1024]{1,0:T(8,128)(2,1)S(1)} %get-tuple-element.22.columns), custom_call_target="tpu_custom_call" | custom-call | flops 1100000000 | bytes 4000000 | tf_op jit(solution)/shard_map/pallas_call | solution.py:367
  116.6 0.0 copy-start.4
  116.6 28.9 %all_to_all.22 = bf16[64,8,1024]{2,1,0:T(8,128)(2,1)S(1)} all-to-all(bf16[64,8,1024]{2,1,0:T(8,128)(2,1)S(1)} %bitcast.9), channel_id=1, replica_groups=mesh['sec'=2,'ep'=64,'tp'=4] {'ep'}, dimensions={0} | all-to-all | bytes 2097152 | tf_op jit(solution)/shard_map/all_to_all | solution.py:375
  145.5 0.0 copy-done.4
  145.5 1.3 shard_map.127
  (4 shorter events, 0.0 us)
Async XLA Ops:
  3.1 40.5 %collective-permute-start.2 = (bf16[1536,512]{1,0:T(8,128)(2,1)}, bf16[1536,512]{1,0:T(8,128)(2,1)}, u32[]{:S(2)}, u32[]{:S(2)}) collective-permute-start(bf16[1536,512]{1,0:T(8,128)(2,1)} %get-tuple-element.17), channel_id=1, source_target_pairs={{0,1},{1,256},{2,257},{3,0},{256,3},{257,258},{258,259},{259,2},{4... | collective-permute-start | bytes 4718600 | tf_op jit(solution)/shard_map/ppermute | solution.py:325
  8.9 43.7 %collective-permute-start.1 = (bf16[1536,512]{1,0:T(8,128)(2,1)}, bf16[1536,512]{1,0:T(8,128)(2,1)}, u32[]{:S(2)}, u32[]{:S(2)}) collective-permute-start(bf16[1536,512]{1,0:T(8,128)(2,1)} %get-tuple-element.16.first), channel_id=1, source_target_pairs={{0,256},{1,257},{2,0},{3,1},{256,258},{257,259},{258,2},{259,3},{4... | collective-permute-start | bytes 4718600 | tf_op jit(solution)/shard_map/ppermute | solution.py:325
  16.5 9.5 %collective-permute-start = (bf16[128,1024]{1,0:T(8,128)(2,1)}, bf16[128,1024]{1,0:T(8,128)(2,1)S(1)}, u32[]{:S(2)}, u32[]{:S(2)}) collective-permute-start(bf16[128,1024]{1,0:T(8,128)(2,1)} %get-tuple-element.15.hidden), channel_id=1, source_target_pairs={{256,260},{260,264},{264,268},{268,272},{272,276},{276,280},{280,2... | collective-permute-start | bytes 786440 | tf_op jit(solution)/shard_map/ppermute | solution.py:333
  25.9 0.7 copy-start.5
  26.6 15.9 %copy-start.1 = (bf16[128,1024]{1,0:T(8,128)(2,1)S(1)}, bf16[128,1024]{1,0:T(8,128)(2,1)}, u32[]{:S(2)}) copy-start(bf16[128,1024]{1,0:T(8,128)(2,1)} %get-tuple-element.15.hidden) | copy-start | bytes 786436
  26.6 15.9 %copy-start.2 = (f32[1024,64]{0,1:T(8,128)S(1)}, f32[1024,64]{0,1:T(8,128)}, u32[]{:S(2)}) copy-start(f32[1024,64]{0,1:T(8,128)} %param.17) | copy-start | bytes 786436
  26.6 15.9 %copy-start.3 = (f32[1024]{0:T(1024)S(1)}, f32[1024]{0:T(1024)}, u32[]{:S(2)}) copy-start(f32[1024]{0:T(1024)} %param.16) | copy-start | bytes 12292
  26.6 38.2 %all-to-all-start = ((bf16[64,8,1024]{2,1,0:T(8,128)(2,1)}), bf16[64,8,1024]{2,1,0:T(8,128)(2,1)S(1)}, u32[]{:S(2)}, u32[]{:S(2)}) async-start(bf16[64,8,1024]{2,1,0:T(8,128)(2,1)} %bitcast.17), calls=%async_computation | async-start | bytes 2097152 | tf_op jit(solution)/shard_map/all_to_all | solution.py:337
  43.6 10.3 %copy-start.6 = (s32[4]{0:T(128)S(1)}, s32[4]{0:T(128)}, u32[]{:S(2)}) copy-start(s32[4]{0:T(128)} %constant.53.clone) | copy-start | bytes 52
  43.6 10.3 %copy-start.7 = (s32[4]{0:T(128)S(1)}, s32[4]{0:T(128)}, u32[]{:S(2)}) copy-start(s32[4]{0:T(128)} %constant.52.clone) | copy-start | bytes 52
  43.6 21.3 %copy-start = (bf16[1536,512]{1,0:T(8,128)(2,1)S(1)}, bf16[1536,512]{1,0:T(8,128)(2,1)}, u32[]{:S(2)}) copy-start(bf16[1536,512]{1,0:T(8,128)(2,1)} %get-tuple-element.16.first) | copy-start | bytes 4718596
  43.6 21.2 %collective-permute-start.4 = (bf16[1536,512]{1,0:T(8,128)(2,1)}, bf16[1536,512]{1,0:T(8,128)(2,1)}, u32[]{:S(2)}, u32[]{:S(2)}) collective-permute-start(bf16[1536,512]{1,0:T(8,128)(2,1)} %shard_map.122.u1), channel_id=1, source_target_pairs={{0,256},{256,0},{1,257},{257,1},{2,258},{258,2},{3,259},{259,3},{4... | collective-permute-start | bytes 4718600 | tf_op jit(solution)/shard_map/ppermute | solution.py:327
  52.6 12.3 %collective-permute-start.3 = (bf16[1536,512]{1,0:T(8,128)(2,1)}, bf16[1536,512]{1,0:T(8,128)(2,1)}, u32[]{:S(2)}, u32[]{:S(2)}) collective-permute-start(bf16[1536,512]{1,0:T(8,128)(2,1)} %collective-permute-done.1.u0), channel_id=1, source_target_pairs={{0,256},{1,257},{258,2},{259,3},{4,260},{5,261},{262,6},{263,7},{8... | collective-permute-start | bytes 4718600 | tf_op jit(solution)/shard_map/ppermute | solution.py:327
  69.6 8.6 %collective-permute-start.5 = (bf16[128,1024]{1,0:T(8,128)(2,1)S(1)}, bf16[128,1024]{1,0:T(8,128)(2,1)S(1)}, u32[]{:S(2)}, u32[]{:S(2)}) collective-permute-start(bf16[128,1024]{1,0:T(8,128)(2,1)S(1)} %get-tuple-element.19), channel_id=1, source_target_pairs={{256,260},{260,264},{264,268},{268,272},{272,276},{276,280},{280,2... | collective-permute-start | bytes 786440 | tf_op jit(solution)/shard_map/ppermute | solution.py:355
  116.6 28.9 %copy-start.4 = (s32[128,2]{0,1:T(2,128)S(1)}, s32[128,2]{0,1:T(2,128)}, u32[]{:S(2)}) copy-start(s32[128,2]{0,1:T(2,128)} %param.18) | copy-start | bytes 3076

commit v6 on v5

--- a/solution.py
+++ b/solution.py
@@ -256,7 +256,9 @@
     named, slot = slots_of(ids, experts)
     inv = lax.rsqrt(sums[experts : experts + 1, :] / D + EPS)
     logits = sums[0:experts, :] * inv
-    picked = jnp.where(named, 1.0 / (1.0 + jnp.exp(-logits)), 0.0)
+    negative = jnp.where(named, jnp.minimum(logits, 0.0), -1e30)
+    negative = negative - jnp.max(negative, axis=0, keepdims=True)
+    picked = jnp.where(named, jnp.exp(negative) / (1.0 + jnp.exp(-jnp.abs(logits))), 0.0)
     share = picked / jnp.sum(picked, axis=0, keepdims=True)
     wide = spread(slot, share)
     high = wide.astype(BF)

time: 147 us -> 147 us (level)
  no operation moved by 1% of the time
where the time goes in v6:
time: 147 us
  blocking collectives  65 us (44%)
  starting transfers between devices  41.1 us (28%)
  waiting for transfers between devices  22.3 us (15%)
  Pallas kernels  17.4 us (12%)
    all_to_all x1, blocking collectives, body(): lax.all_to_all(expert_out.reshape(experts, CAP, width), 'ep', split_axis=...  28.9 us
    all_to_all x1, blocking collectives, body(): got = lax.all_to_all(partial, 'tp', split_axis=0, concat_axis=0, tiled=True)  24 us
    all_to_all x1, starting transfers between devices, body(): lax.all_to_all(outgoing.reshape(experts, CAP, width), 'ep', split_axis=0,...  15.9 us
    all_to_all x1, blocking collectives, body(): lax.all_to_all(inner, 'tp', split_axis=0, concat_axis=0, tiled=True)  12.2 us
    all_to_all x1, waiting for transfers between devices, body(): lax.all_to_all(outgoing.reshape(experts, CAP, width), 'ep', split_axis=0,...  10.9 us
    ppermute x1, starting transfers between devices, body(): lax.ppermute(u1, 'sec', [(0, 1), (1, 0)])  8.93 us
    ppermute x2, starting transfers between devices, body(): u0, u1 = (lax.ppermute(first, both, stay), lax.ppermute(second, both, turn))  8.31 us
    ppermute x1, waiting for transfers between devices, body(): after = lax.ppermute(hidden, ('sec', 'ep'), second_only(experts, 1))  6.25 us
  transfers between devices with their start and end apart: 7, of which 3 were waited for; matrix products, arithmetic and copies ran while one was open for 0% of the time, Pallas kernels for 4%

profile of v6, /device:TPU:1, one launch (start us, length us, event | category | flops | bytes accessed | tf_op | source)
XLA Modules:
  0.0 146.8 jit_solution(16822289625694450821)
XLA Ops:
  0.0 3.1 %shard_map.121 = (bf16[1536,512]{1,0:T(8,128)(2,1)}, bf16[1536,512]{1,0:T(8,128)(2,1)}) custom-call(s32[1]{0:T(128)} %bitcast.6.parity, bf16[1,2048,256]{2,1,0:T(8,128)(2,1)} %gate.1, bf16[1,2048,256]{2,1,0:T(8,128)(2,1)} %up.1, bf16[1,256,2048]{2,1,0:T(8,128)(2,1)} %down.1), custom_call_target="tpu_custom_call" | custom-call | bytes 6000000 | tf_op jit(solution)/shard_map/pallas_call | solution.py:289
  3.1 5.8 %collective-permute-start.2 = (bf16[1536,512]{1,0:T(8,128)(2,1)}, bf16[1536,512]{1,0:T(8,128)(2,1)}, u32[]{:S(2)}, u32[]{:S(2)}) collective-permute-start(bf16[1536,512]{1,0:T(8,128)(2,1)} %get-tuple-element.17), channel_id=1, source_target_pairs={{0,1},{1,256},{2,257},{3,0},{256,3},{257,258},{258,259},{259,2},{4... | collective-permute-start | bytes 4718600 | tf_op jit(solution)/shard_map/ppermute | solution.py:327
  8.9 2.5 %collective-permute-start.1 = (bf16[1536,512]{1,0:T(8,128)(2,1)}, bf16[1536,512]{1,0:T(8,128)(2,1)}, u32[]{:S(2)}, u32[]{:S(2)}) collective-permute-start(bf16[1536,512]{1,0:T(8,128)(2,1)} %get-tuple-element.16.first), channel_id=1, source_target_pairs={{0,256},{1,257},{2,0},{3,1},{256,258},{257,259},{258,2},{259,3},{4... | collective-permute-start | bytes 4718600 | tf_op jit(solution)/shard_map/ppermute | solution.py:327
  11.4 5.0 %shard_map.118 = (bf16[128,1024]{1,0:T(8,128)(2,1)}, bf16[512,1024]{1,0:T(8,128)(2,1)}) custom-call(s32[2,128]{1,0:T(2,128)} %bitcast.15, bf16[128,1024]{1,0:T(8,128)(2,1)} %refs_1_.1, bf16[128,1024]{1,0:T(8,128)(2,1)} %refs_2_.1, bf16[128,1024]{1,0:T(8,128)(2,1)} %refs_3_.1, bf16[128,1024]{1,0:T(8,128)(2,1)} %refs_4_.1), custom_call_target="tpu_custom_call" | custom-call | flops 300000000 | bytes 3000000 | tf_op jit(solution)/shard_map/pallas_call | solution.py:298
  16.5 3.2 %collective-permute-start = (bf16[128,1024]{1,0:T(8,128)(2,1)}, bf16[128,1024]{1,0:T(8,128)(2,1)S(1)}, u32[]{:S(2)}, u32[]{:S(2)}) collective-permute-start(bf16[128,1024]{1,0:T(8,128)(2,1)} %get-tuple-element.15.hidden), channel_id=1, source_target_pairs={{256,260},{260,264},{264,268},{268,272},{272,276},{276,280},{280,2... | collective-permute-start | bytes 786440 | tf_op jit(solution)/shard_map/ppermute | solution.py:335
  19.7 6.2 %collective-permute-done.after = bf16[128,1024]{1,0:T(8,128)(2,1)S(1)} collective-permute-done((bf16[128,1024]{1,0:T(8,128)(2,1)}, bf16[128,1024]{1,0:T(8,128)(2,1)S(1)}, u32[]{:S(2)}, u32[]{:S(2)}) %collective-permute-start) | collective-permute-done | bytes 262176 | tf_op jit(solution)/shard_map/ppermute | solution.py:335
  25.9 0.0 copy-start.5
  25.9 0.7 copy-done.5
  26.6 0.0 copy-start.1
  26.6 0.0 copy-start.2
  26.6 0.0 copy-start.3
  26.6 15.9 %all-to-all-start = ((bf16[64,8,1024]{2,1,0:T(8,128)(2,1)}), bf16[64,8,1024]{2,1,0:T(8,128)(2,1)S(1)}, u32[]{:S(2)}, u32[]{:S(2)}) async-start(bf16[64,8,1024]{2,1,0:T(8,128)(2,1)} %bitcast.17), calls=%async_computation | async-start | bytes 2097152 | tf_op jit(solution)/shard_map/all_to_all | solution.py:339
  42.6 0.0 copy-done.1
  42.6 0.0 copy-done.2
  42.6 0.0 copy-done.3
  42.6 1.0 shard_map.120.after.sums
  43.6 0.0 copy-start.6
  43.6 0.0 copy-start.7
  43.6 0.0 copy-start
  43.6 0.0 collective-permute-done.2.message
  43.6 8.9 %collective-permute-start.4 = (bf16[1536,512]{1,0:T(8,128)(2,1)}, bf16[1536,512]{1,0:T(8,128)(2,1)}, u32[]{:S(2)}, u32[]{:S(2)}) collective-permute-start(bf16[1536,512]{1,0:T(8,128)(2,1)} %shard_map.122.u1), channel_id=1, source_target_pairs={{0,256},{256,0},{1,257},{257,1},{2,258},{258,2},{3,259},{259,3},{4... | collective-permute-start | bytes 4718600 | tf_op jit(solution)/shard_map/ppermute | solution.py:329
  52.6 0.0 collective-permute-done.1.u0
  52.6 1.3 collective-permute-start.3
  53.9 0.0 copy-done.6
  53.9 0.0 copy-done.7
  53.9 0.1 pad_add_fusion.place
  54.0 10.9 %all-to-all-done = bf16[64,8,1024]{2,1,0:T(8,128)(2,1)S(1)} async-done(((bf16[64,8,1024]{2,1,0:T(8,128)(2,1)}), bf16[64,8,1024]{2,1,0:T(8,128)(2,1)S(1)}, u32[]{:S(2)}, u32[]{:S(2)}) %all-to-all-start) | async-done | bytes 1048608 | tf_op jit(solution)/shard_map/all_to_all | solution.py:339
  64.9 0.0 collective-permute-done.4.v1
  64.9 0.0 collective-permute-done.3.v0
  64.9 0.0 copy-done
  64.9 4.7 %shard_map.123 = (bf16[4,544,512]{2,1,0:T(8,128)(2,1)S(1)}, bf16[1024,1024]{1,0:T(8,128)(2,1)S(1)}, bf16[128,1024]{1,0:T(8,128)(2,1)S(1)}) custom-call(s32[5]{0:T(128)S(1)} %pad_add_fusion.place, bf16[512,1024]{1,0:T(8,128)(2,1)S(1)} %bitcast.11, f32[1,1024]{1,0:T(1,128)S(1)} %bitcast.14, f32[72,128]{1,0:T(8,128)S(1)} %shard_map.120.after.sums, ...), custom_call_target="tpu_custom_call" | custom-call | flops 2200000000 | bytes 9000000 | tf_op jit(solution)/shard_map/pallas_call | solution.py:344
  69.6 3.4 %collective-permute-start.5 = (bf16[128,1024]{1,0:T(8,128)(2,1)S(1)}, bf16[128,1024]{1,0:T(8,128)(2,1)S(1)}, u32[]{:S(2)}, u32[]{:S(2)}) collective-permute-start(bf16[128,1024]{1,0:T(8,128)(2,1)S(1)} %get-tuple-element.19), channel_id=1, source_target_pairs={{256,260},{260,264},{264,268},{268,272},{272,276},{276,280},{280,2... | collective-permute-start | bytes 786440 | tf_op jit(solution)/shard_map/ppermute | solution.py:357
  73.0 5.2 %collective-permute-done.5.after = bf16[128,1024]{1,0:T(8,128)(2,1)S(1)} collective-permute-done((bf16[128,1024]{1,0:T(8,128)(2,1)S(1)}, bf16[128,1024]{1,0:T(8,128)(2,1)S(1)}, u32[]{:S(2)}, u32[]{:S(2)}) %collective-permute-start.5) | collective-permute-done | bytes 262176 | tf_op jit(solution)/shard_map/ppermute | solution.py:357
  78.2 24.0 %all_to_all.20.got = bf16[4,544,512]{2,1,0:T(8,128)(2,1)S(1)} all-to-all(bf16[4,544,512]{2,1,0:T(8,128)(2,1)S(1)} %shard_map.124), channel_id=1, replica_groups=mesh['sec'=2,'ep'=64,'tp'=4] {'tp'}, dimensions={0} | all-to-all | bytes 4456448 | tf_op jit(solution)/shard_map/all_to_all | solution.py:359
  102.2 0.4 shard_map.125
  102.6 12.2 %all_to_all.21.inners = bf16[4,512,256]{2,1,0:T(8,128)(2,1)S(1)} all-to-all(bf16[4,512,256]{2,1,0:T(8,128)(2,1)S(1)} %get-tuple-element.21), channel_id=1, replica_groups=mesh['sec'=2,'ep'=64,'tp'=4] {'tp'}, dimensions={0} | all-to-all | bytes 2097152 | tf_op jit(solution)/shard_map/all_to_all | solution.py:368
  114.8 1.8 %shard_map.126 = bf16[512,1024]{1,0:T(8,128)(2,1)S(1)} custom-call(s32[5]{0:T(128)S(1)} %pad_add_fusion.place, bf16[4,512,256]{2,1,0:T(8,128)(2,1)S(1)} %all_to_all.21.inners, bf16[1024,1024]{1,0:T(8,128)(2,1)S(1)} %get-tuple-element.22.columns), custom_call_target="tpu_custom_call" | custom-call | flops 1100000000 | bytes 4000000 | tf_op jit(solution)/shard_map/pallas_call | solution.py:369
  116.6 0.0 copy-start.4
  116.6 28.9 %all_to_all.22 = bf16[64,8,1024]{2,1,0:T(8,128)(2,1)S(1)} all-to-all(bf16[64,8,1024]{2,1,0:T(8,128)(2,1)S(1)} %bitcast.9), channel_id=1, replica_groups=mesh['sec'=2,'ep'=64,'tp'=4] {'ep'}, dimensions={0} | all-to-all | bytes 2097152 | tf_op jit(solution)/shard_map/all_to_all | solution.py:377
  145.5 0.0 copy-done.4
  145.5 1.3 shard_map.127
  (4 shorter events, 0.0 us)
Async XLA Ops:
  3.1 40.5 %collective-permute-start.2 = (bf16[1536,512]{1,0:T(8,128)(2,1)}, bf16[1536,512]{1,0:T(8,128)(2,1)}, u32[]{:S(2)}, u32[]{:S(2)}) collective-permute-start(bf16[1536,512]{1,0:T(8,128)(2,1)} %get-tuple-element.17), channel_id=1, source_target_pairs={{0,1},{1,256},{2,257},{3,0},{256,3},{257,258},{258,259},{259,2},{4... | collective-permute-start | bytes 4718600 | tf_op jit(solution)/shard_map/ppermute | solution.py:327
  8.9 43.7 %collective-permute-start.1 = (bf16[1536,512]{1,0:T(8,128)(2,1)}, bf16[1536,512]{1,0:T(8,128)(2,1)}, u32[]{:S(2)}, u32[]{:S(2)}) collective-permute-start(bf16[1536,512]{1,0:T(8,128)(2,1)} %get-tuple-element.16.first), channel_id=1, source_target_pairs={{0,256},{1,257},{2,0},{3,1},{256,258},{257,259},{258,2},{259,3},{4... | collective-permute-start | bytes 4718600 | tf_op jit(solution)/shard_map/ppermute | solution.py:327
  16.5 9.5 %collective-permute-start = (bf16[128,1024]{1,0:T(8,128)(2,1)}, bf16[128,1024]{1,0:T(8,128)(2,1)S(1)}, u32[]{:S(2)}, u32[]{:S(2)}) collective-permute-start(bf16[128,1024]{1,0:T(8,128)(2,1)} %get-tuple-element.15.hidden), channel_id=1, source_target_pairs={{256,260},{260,264},{264,268},{268,272},{272,276},{276,280},{280,2... | collective-permute-start | bytes 786440 | tf_op jit(solution)/shard_map/ppermute | solution.py:335
  25.9 0.7 copy-start.5
  26.6 15.9 %copy-start.1 = (bf16[128,1024]{1,0:T(8,128)(2,1)S(1)}, bf16[128,1024]{1,0:T(8,128)(2,1)}, u32[]{:S(2)}) copy-start(bf16[128,1024]{1,0:T(8,128)(2,1)} %get-tuple-element.15.hidden) | copy-start | bytes 786436
  26.6 15.9 %copy-start.2 = (f32[1024,64]{0,1:T(8,128)S(1)}, f32[1024,64]{0,1:T(8,128)}, u32[]{:S(2)}) copy-start(f32[1024,64]{0,1:T(8,128)} %param.17) | copy-start | bytes 786436
  26.6 15.9 %copy-start.3 = (f32[1024]{0:T(1024)S(1)}, f32[1024]{0:T(1024)}, u32[]{:S(2)}) copy-start(f32[1024]{0:T(1024)} %param.16) | copy-start | bytes 12292
  26.6 38.2 %all-to-all-start = ((bf16[64,8,1024]{2,1,0:T(8,128)(2,1)}), bf16[64,8,1024]{2,1,0:T(8,128)(2,1)S(1)}, u32[]{:S(2)}, u32[]{:S(2)}) async-start(bf16[64,8,1024]{2,1,0:T(8,128)(2,1)} %bitcast.17), calls=%async_computation | async-start | bytes 2097152 | tf_op jit(solution)/shard_map/all_to_all | solution.py:339
  43.6 10.3 %copy-start.6 = (s32[4]{0:T(128)S(1)}, s32[4]{0:T(128)}, u32[]{:S(2)}) copy-start(s32[4]{0:T(128)} %constant.53.clone) | copy-start | bytes 52
  43.6 10.3 %copy-start.7 = (s32[4]{0:T(128)S(1)}, s32[4]{0:T(128)}, u32[]{:S(2)}) copy-start(s32[4]{0:T(128)} %constant.52.clone) | copy-start | bytes 52
  43.6 21.3 %copy-start = (bf16[1536,512]{1,0:T(8,128)(2,1)S(1)}, bf16[1536,512]{1,0:T(8,128)(2,1)}, u32[]{:S(2)}) copy-start(bf16[1536,512]{1,0:T(8,128)(2,1)} %get-tuple-element.16.first) | copy-start | bytes 4718596
  43.6 21.2 %collective-permute-start.4 = (bf16[1536,512]{1,0:T(8,128)(2,1)}, bf16[1536,512]{1,0:T(8,128)(2,1)}, u32[]{:S(2)}, u32[]{:S(2)}) collective-permute-start(bf16[1536,512]{1,0:T(8,128)(2,1)} %shard_map.122.u1), channel_id=1, source_target_pairs={{0,256},{256,0},{1,257},{257,1},{2,258},{258,2},{3,259},{259,3},{4... | collective-permute-start | bytes 4718600 | tf_op jit(solution)/shard_map/ppermute | solution.py:329
  52.6 12.3 %collective-permute-start.3 = (bf16[1536,512]{1,0:T(8,128)(2,1)}, bf16[1536,512]{1,0:T(8,128)(2,1)}, u32[]{:S(2)}, u32[]{:S(2)}) collective-permute-start(bf16[1536,512]{1,0:T(8,128)(2,1)} %collective-permute-done.1.u0), channel_id=1, source_target_pairs={{0,256},{1,257},{258,2},{259,3},{4,260},{5,261},{262,6},{263,7},{8... | collective-permute-start | bytes 4718600 | tf_op jit(solution)/shard_map/ppermute | solution.py:329
  69.6 8.6 %collective-permute-start.5 = (bf16[128,1024]{1,0:T(8,128)(2,1)S(1)}, bf16[128,1024]{1,0:T(8,128)(2,1)S(1)}, u32[]{:S(2)}, u32[]{:S(2)}) collective-permute-start(bf16[128,1024]{1,0:T(8,128)(2,1)S(1)} %get-tuple-element.19), channel_id=1, source_target_pairs={{256,260},{260,264},{264,268},{268,272},{272,276},{276,280},{280,2... | collective-permute-start | bytes 786440 | tf_op jit(solution)/shard_map/ppermute | solution.py:357
  116.6 28.9 %copy-start.4 = (s32[128,2]{0,1:T(2,128)S(1)}, s32[128,2]{0,1:T(2,128)}, u32[]{:S(2)}) copy-start(s32[128,2]{0,1:T(2,128)} %param.18) | copy-start | bytes 3076

commit v7 on v6

--- a/solution.py
+++ b/solution.py
@@ -121,7 +121,7 @@
         scores = nt(q[:, cols], k[:, cols]) * scale
         top = jnp.max(scores, axis=1, keepdims=True)
         e = jnp.exp(scores - top)
-        weights = (e / jnp.sum(e, axis=1, keepdims=True)).astype(BF)
+        weights = (e * (1.0 / jnp.sum(e, axis=1, keepdims=True))).astype(BF)
         attended = jnp.dot(weights, v[:, cols], preferred_element_type=F32)
         h = (resid[:, cols].astype(F32) + attended).astype(BF)
         hidden[:, cols] = h
@@ -263,10 +263,11 @@
     wide = spread(slot, share)
     high = wide.astype(BF)
     low = (wide - high.astype(F32)).astype(BF)
-    rows = returned[...]
+    both = jnp.concatenate([high, low], axis=1)
     dims = (((0,), (0,)), ((), ()))
-    mixed = lax.dot_general(high, rows, dims, preferred_element_type=F32)
-    mixed += lax.dot_general(low, rows, dims, preferred_element_type=F32)
+    mixed = lax.dot_general(both, returned[...], dims, preferred_element_type=F32)
+    tokens = hidden.shape[0]
+    mixed = mixed[0:tokens, :] + mixed[tokens:, :]
     out[...] = (hidden[...].astype(F32) + mixed).astype(BF)
 
 

time: 147 us -> 147 us (level)
  no operation moved by 1% of the time
where the time goes in v7:
time: 147 us
  blocking collectives  65 us (44%)
  starting transfers between devices  41.1 us (28%)
  waiting for transfers between devices  22.3 us (15%)
  Pallas kernels  17.4 us (12%)
    all_to_all x1, blocking collectives, body(): lax.all_to_all(expert_out.reshape(experts, CAP, width), 'ep', split_axis=...  28.9 us
    all_to_all x1, blocking collectives, body(): got = lax.all_to_all(partial, 'tp', split_axis=0, concat_axis=0, tiled=True)  24 us
    all_to_all x1, starting transfers between devices, body(): lax.all_to_all(outgoing.reshape(experts, CAP, width), 'ep', split_axis=0,...  15.9 us
    all_to_all x1, blocking collectives, body(): lax.all_to_all(inner, 'tp', split_axis=0, concat_axis=0, tiled=True)  12.2 us
    all_to_all x1, waiting for transfers between devices, body(): lax.all_to_all(outgoing.reshape(experts, CAP, width), 'ep', split_axis=0,...  10.9 us
    ppermute x1, starting transfers between devices, body(): lax.ppermute(u1, 'sec', [(0, 1), (1, 0)])  8.93 us
    ppermute x2, starting transfers between devices, body(): u0, u1 = (lax.ppermute(first, both, stay), lax.ppermute(second, both, turn))  8.31 us
    ppermute x1, waiting for transfers between devices, body(): after = lax.ppermute(hidden, ('sec', 'ep'), second_only(experts, 1))  6.25 us
  transfers between devices with their start and end apart: 7, of which 3 were waited for; matrix products, arithmetic and copies ran while one was open for 0% of the time, Pallas kernels for 4%

profile of v7, /device:TPU:1, one launch (start us, length us, event | category | flops | bytes accessed | tf_op | source)
XLA Modules:
  0.0 146.8 jit_solution(8955948521085965284)
XLA Ops:
  0.0 3.1 %shard_map.121 = (bf16[1536,512]{1,0:T(8,128)(2,1)}, bf16[1536,512]{1,0:T(8,128)(2,1)}) custom-call(s32[1]{0:T(128)} %bitcast.6.parity, bf16[1,2048,256]{2,1,0:T(8,128)(2,1)} %gate.1, bf16[1,2048,256]{2,1,0:T(8,128)(2,1)} %up.1, bf16[1,256,2048]{2,1,0:T(8,128)(2,1)} %down.1), custom_call_target="tpu_custom_call" | custom-call | bytes 6000000 | tf_op jit(solution)/shard_map/pallas_call | solution.py:290
  3.1 5.8 %collective-permute-start.2 = (bf16[1536,512]{1,0:T(8,128)(2,1)}, bf16[1536,512]{1,0:T(8,128)(2,1)}, u32[]{:S(2)}, u32[]{:S(2)}) collective-permute-start(bf16[1536,512]{1,0:T(8,128)(2,1)} %get-tuple-element.17), channel_id=1, source_target_pairs={{0,1},{1,256},{2,257},{3,0},{256,3},{257,258},{258,259},{259,2},{4... | collective-permute-start | bytes 4718600 | tf_op jit(solution)/shard_map/ppermute | solution.py:328
  8.9 2.5 %collective-permute-start.1 = (bf16[1536,512]{1,0:T(8,128)(2,1)}, bf16[1536,512]{1,0:T(8,128)(2,1)}, u32[]{:S(2)}, u32[]{:S(2)}) collective-permute-start(bf16[1536,512]{1,0:T(8,128)(2,1)} %get-tuple-element.16.first), channel_id=1, source_target_pairs={{0,256},{1,257},{2,0},{3,1},{256,258},{257,259},{258,2},{259,3},{4... | collective-permute-start | bytes 4718600 | tf_op jit(solution)/shard_map/ppermute | solution.py:328
  11.4 5.0 %shard_map.118 = (bf16[128,1024]{1,0:T(8,128)(2,1)}, bf16[512,1024]{1,0:T(8,128)(2,1)}) custom-call(s32[2,128]{1,0:T(2,128)} %bitcast.15, bf16[128,1024]{1,0:T(8,128)(2,1)} %refs_1_.1, bf16[128,1024]{1,0:T(8,128)(2,1)} %refs_2_.1, bf16[128,1024]{1,0:T(8,128)(2,1)} %refs_3_.1, bf16[128,1024]{1,0:T(8,128)(2,1)} %refs_4_.1), custom_call_target="tpu_custom_call" | custom-call | flops 300000000 | bytes 3000000 | tf_op jit(solution)/shard_map/pallas_call | solution.py:299
  16.5 3.2 %collective-permute-start = (bf16[128,1024]{1,0:T(8,128)(2,1)}, bf16[128,1024]{1,0:T(8,128)(2,1)S(1)}, u32[]{:S(2)}, u32[]{:S(2)}) collective-permute-start(bf16[128,1024]{1,0:T(8,128)(2,1)} %get-tuple-element.15.hidden), channel_id=1, source_target_pairs={{256,260},{260,264},{264,268},{268,272},{272,276},{276,280},{280,2... | collective-permute-start | bytes 786440 | tf_op jit(solution)/shard_map/ppermute | solution.py:336
  19.7 6.2 %collective-permute-done.after = bf16[128,1024]{1,0:T(8,128)(2,1)S(1)} collective-permute-done((bf16[128,1024]{1,0:T(8,128)(2,1)}, bf16[128,1024]{1,0:T(8,128)(2,1)S(1)}, u32[]{:S(2)}, u32[]{:S(2)}) %collective-permute-start) | collective-permute-done | bytes 262176 | tf_op jit(solution)/shard_map/ppermute | solution.py:336
  25.9 0.0 copy-start.5
  25.9 0.7 copy-done.5
  26.6 0.0 copy-start.1
  26.6 0.0 copy-start.2
  26.6 0.0 copy-start.3
  26.6 15.9 %all-to-all-start = ((bf16[64,8,1024]{2,1,0:T(8,128)(2,1)}), bf16[64,8,1024]{2,1,0:T(8,128)(2,1)S(1)}, u32[]{:S(2)}, u32[]{:S(2)}) async-start(bf16[64,8,1024]{2,1,0:T(8,128)(2,1)} %bitcast.17), calls=%async_computation | async-start | bytes 2097152 | tf_op jit(solution)/shard_map/all_to_all | solution.py:340
  42.6 0.0 copy-done.1
  42.6 0.0 copy-done.2
  42.6 0.0 copy-done.3
  42.6 1.0 shard_map.120.after.sums
  43.6 0.0 copy-start.6
  43.6 0.0 copy-start.7
  43.6 0.0 copy-start
  43.6 0.0 collective-permute-done.2.message
  43.6 8.9 %collective-permute-start.4 = (bf16[1536,512]{1,0:T(8,128)(2,1)}, bf16[1536,512]{1,0:T(8,128)(2,1)}, u32[]{:S(2)}, u32[]{:S(2)}) collective-permute-start(bf16[1536,512]{1,0:T(8,128)(2,1)} %shard_map.122.u1), channel_id=1, source_target_pairs={{0,256},{256,0},{1,257},{257,1},{2,258},{258,2},{3,259},{259,3},{4... | collective-permute-start | bytes 4718600 | tf_op jit(solution)/shard_map/ppermute | solution.py:330
  52.6 0.0 collective-permute-done.1.u0
  52.6 1.3 collective-permute-start.3
  53.9 0.0 copy-done.6
  53.9 0.0 copy-done.7
  53.9 0.1 pad_add_fusion.place
  54.0 10.9 %all-to-all-done = bf16[64,8,1024]{2,1,0:T(8,128)(2,1)S(1)} async-done(((bf16[64,8,1024]{2,1,0:T(8,128)(2,1)}), bf16[64,8,1024]{2,1,0:T(8,128)(2,1)S(1)}, u32[]{:S(2)}, u32[]{:S(2)}) %all-to-all-start) | async-done | bytes 1048608 | tf_op jit(solution)/shard_map/all_to_all | solution.py:340
  64.9 0.0 collective-permute-done.4.v1
  64.9 0.0 collective-permute-done.3.v0
  64.9 0.0 copy-done
  64.9 4.7 %shard_map.123 = (bf16[4,544,512]{2,1,0:T(8,128)(2,1)S(1)}, bf16[1024,1024]{1,0:T(8,128)(2,1)S(1)}, bf16[128,1024]{1,0:T(8,128)(2,1)S(1)}) custom-call(s32[5]{0:T(128)S(1)} %pad_add_fusion.place, bf16[512,1024]{1,0:T(8,128)(2,1)S(1)} %bitcast.11, f32[1,1024]{1,0:T(1,128)S(1)} %bitcast.14, f32[72,128]{1,0:T(8,128)S(1)} %shard_map.120.after.sums, ...), custom_call_target="tpu_custom_call" | custom-call | flops 2200000000 | bytes 9000000 | tf_op jit(solution)/shard_map/pallas_call | solution.py:345
  69.6 3.4 %collective-permute-start.5 = (bf16[128,1024]{1,0:T(8,128)(2,1)S(1)}, bf16[128,1024]{1,0:T(8,128)(2,1)S(1)}, u32[]{:S(2)}, u32[]{:S(2)}) collective-permute-start(bf16[128,1024]{1,0:T(8,128)(2,1)S(1)} %get-tuple-element.19), channel_id=1, source_target_pairs={{256,260},{260,264},{264,268},{268,272},{272,276},{276,280},{280,2... | collective-permute-start | bytes 786440 | tf_op jit(solution)/shard_map/ppermute | solution.py:358
  73.0 5.2 %collective-permute-done.5.after = bf16[128,1024]{1,0:T(8,128)(2,1)S(1)} collective-permute-done((bf16[128,1024]{1,0:T(8,128)(2,1)S(1)}, bf16[128,1024]{1,0:T(8,128)(2,1)S(1)}, u32[]{:S(2)}, u32[]{:S(2)}) %collective-permute-start.5) | collective-permute-done | bytes 262176 | tf_op jit(solution)/shard_map/ppermute | solution.py:358
  78.2 24.0 %all_to_all.20.got = bf16[4,544,512]{2,1,0:T(8,128)(2,1)S(1)} all-to-all(bf16[4,544,512]{2,1,0:T(8,128)(2,1)S(1)} %shard_map.124), channel_id=1, replica_groups=mesh['sec'=2,'ep'=64,'tp'=4] {'tp'}, dimensions={0} | all-to-all | bytes 4456448 | tf_op jit(solution)/shard_map/all_to_all | solution.py:360
  102.2 0.4 shard_map.125
  102.6 12.2 %all_to_all.21.inners = bf16[4,512,256]{2,1,0:T(8,128)(2,1)S(1)} all-to-all(bf16[4,512,256]{2,1,0:T(8,128)(2,1)S(1)} %get-tuple-element.21), channel_id=1, replica_groups=mesh['sec'=2,'ep'=64,'tp'=4] {'tp'}, dimensions={0} | all-to-all | bytes 2097152 | tf_op jit(solution)/shard_map/all_to_all | solution.py:369
  114.8 1.8 %shard_map.126 = bf16[512,1024]{1,0:T(8,128)(2,1)S(1)} custom-call(s32[5]{0:T(128)S(1)} %pad_add_fusion.place, bf16[4,512,256]{2,1,0:T(8,128)(2,1)S(1)} %all_to_all.21.inners, bf16[1024,1024]{1,0:T(8,128)(2,1)S(1)} %get-tuple-element.22.columns), custom_call_target="tpu_custom_call" | custom-call | flops 1100000000 | bytes 4000000 | tf_op jit(solution)/shard_map/pallas_call | solution.py:370
  116.6 0.0 copy-start.4
  116.6 28.9 %all_to_all.22 = bf16[64,8,1024]{2,1,0:T(8,128)(2,1)S(1)} all-to-all(bf16[64,8,1024]{2,1,0:T(8,128)(2,1)S(1)} %bitcast.9), channel_id=1, replica_groups=mesh['sec'=2,'ep'=64,'tp'=4] {'ep'}, dimensions={0} | all-to-all | bytes 2097152 | tf_op jit(solution)/shard_map/all_to_all | solution.py:378
  145.5 0.0 copy-done.4
  145.5 1.3 shard_map.127
  (4 shorter events, 0.0 us)
Async XLA Ops:
  3.1 40.5 %collective-permute-start.2 = (bf16[1536,512]{1,0:T(8,128)(2,1)}, bf16[1536,512]{1,0:T(8,128)(2,1)}, u32[]{:S(2)}, u32[]{:S(2)}) collective-permute-start(bf16[1536,512]{1,0:T(8,128)(2,1)} %get-tuple-element.17), channel_id=1, source_target_pairs={{0,1},{1,256},{2,257},{3,0},{256,3},{257,258},{258,259},{259,2},{4... | collective-permute-start | bytes 4718600 | tf_op jit(solution)/shard_map/ppermute | solution.py:328
  8.9 43.7 %collective-permute-start.1 = (bf16[1536,512]{1,0:T(8,128)(2,1)}, bf16[1536,512]{1,0:T(8,128)(2,1)}, u32[]{:S(2)}, u32[]{:S(2)}) collective-permute-start(bf16[1536,512]{1,0:T(8,128)(2,1)} %get-tuple-element.16.first), channel_id=1, source_target_pairs={{0,256},{1,257},{2,0},{3,1},{256,258},{257,259},{258,2},{259,3},{4... | collective-permute-start | bytes 4718600 | tf_op jit(solution)/shard_map/ppermute | solution.py:328
  16.5 9.5 %collective-permute-start = (bf16[128,1024]{1,0:T(8,128)(2,1)}, bf16[128,1024]{1,0:T(8,128)(2,1)S(1)}, u32[]{:S(2)}, u32[]{:S(2)}) collective-permute-start(bf16[128,1024]{1,0:T(8,128)(2,1)} %get-tuple-element.15.hidden), channel_id=1, source_target_pairs={{256,260},{260,264},{264,268},{268,272},{272,276},{276,280},{280,2... | collective-permute-start | bytes 786440 | tf_op jit(solution)/shard_map/ppermute | solution.py:336
  25.9 0.7 copy-start.5
  26.6 15.9 %copy-start.1 = (bf16[128,1024]{1,0:T(8,128)(2,1)S(1)}, bf16[128,1024]{1,0:T(8,128)(2,1)}, u32[]{:S(2)}) copy-start(bf16[128,1024]{1,0:T(8,128)(2,1)} %get-tuple-element.15.hidden) | copy-start | bytes 786436
  26.6 15.9 %copy-start.2 = (f32[1024,64]{0,1:T(8,128)S(1)}, f32[1024,64]{0,1:T(8,128)}, u32[]{:S(2)}) copy-start(f32[1024,64]{0,1:T(8,128)} %param.17) | copy-start | bytes 786436
  26.6 15.9 %copy-start.3 = (f32[1024]{0:T(1024)S(1)}, f32[1024]{0:T(1024)}, u32[]{:S(2)}) copy-start(f32[1024]{0:T(1024)} %param.16) | copy-start | bytes 12292
  26.6 38.2 %all-to-all-start = ((bf16[64,8,1024]{2,1,0:T(8,128)(2,1)}), bf16[64,8,1024]{2,1,0:T(8,128)(2,1)S(1)}, u32[]{:S(2)}, u32[]{:S(2)}) async-start(bf16[64,8,1024]{2,1,0:T(8,128)(2,1)} %bitcast.17), calls=%async_computation | async-start | bytes 2097152 | tf_op jit(solution)/shard_map/all_to_all | solution.py:340
  43.6 10.3 %copy-start.6 = (s32[4]{0:T(128)S(1)}, s32[4]{0:T(128)}, u32[]{:S(2)}) copy-start(s32[4]{0:T(128)} %constant.53.clone) | copy-start | bytes 52
  43.6 10.3 %copy-start.7 = (s32[4]{0:T(128)S(1)}, s32[4]{0:T(128)}, u32[]{:S(2)}) copy-start(s32[4]{0:T(128)} %constant.52.clone) | copy-start | bytes 52
  43.6 21.3 %copy-start = (bf16[1536,512]{1,0:T(8,128)(2,1)S(1)}, bf16[1536,512]{1,0:T(8,128)(2,1)}, u32[]{:S(2)}) copy-start(bf16[1536,512]{1,0:T(8,128)(2,1)} %get-tuple-element.16.first) | copy-start | bytes 4718596
  43.6 21.2 %collective-permute-start.4 = (bf16[1536,512]{1,0:T(8,128)(2,1)}, bf16[1536,512]{1,0:T(8,128)(2,1)}, u32[]{:S(2)}, u32[]{:S(2)}) collective-permute-start(bf16[1536,512]{1,0:T(8,128)(2,1)} %shard_map.122.u1), channel_id=1, source_target_pairs={{0,256},{256,0},{1,257},{257,1},{2,258},{258,2},{3,259},{259,3},{4... | collective-permute-start | bytes 4718600 | tf_op jit(solution)/shard_map/ppermute | solution.py:330
  52.6 12.3 %collective-permute-start.3 = (bf16[1536,512]{1,0:T(8,128)(2,1)}, bf16[1536,512]{1,0:T(8,128)(2,1)}, u32[]{:S(2)}, u32[]{:S(2)}) collective-permute-start(bf16[1536,512]{1,0:T(8,128)(2,1)} %collective-permute-done.1.u0), channel_id=1, source_target_pairs={{0,256},{1,257},{258,2},{259,3},{4,260},{5,261},{262,6},{263,7},{8... | collective-permute-start | bytes 4718600 | tf_op jit(solution)/shard_map/ppermute | solution.py:330
  69.6 8.6 %collective-permute-start.5 = (bf16[128,1024]{1,0:T(8,128)(2,1)S(1)}, bf16[128,1024]{1,0:T(8,128)(2,1)S(1)}, u32[]{:S(2)}, u32[]{:S(2)}) collective-permute-start(bf16[128,1024]{1,0:T(8,128)(2,1)S(1)} %get-tuple-element.19), channel_id=1, source_target_pairs={{256,260},{260,264},{264,268},{268,272},{272,276},{276,280},{280,2... | collective-permute-start | bytes 786440 | tf_op jit(solution)/shard_map/ppermute | solution.py:358
  116.6 28.9 %copy-start.4 = (s32[128,2]{0,1:T(2,128)S(1)}, s32[128,2]{0,1:T(2,128)}, u32[]{:S(2)}) copy-start(s32[128,2]{0,1:T(2,128)} %param.18) | copy-start | bytes 3076
